TPU v7x, 512 devices: a whole 4x4x16 slice. The times are simulated.
512 devices in a mesh: gx: 64 (over y, z), gy: 4 (over x), ga: 2 (over core).
Axes of the slice: x: 4, y: 4, z: 16, core: 2. Of those that a mesh axis runs over, the one named last changes fastest.
Arguments:
- right_side: float32 [3, 512, 32, 256], P(None, 'gx', 'gy', 'ga'), may hold values from -24 to 24
- fine_stiff: float32 [3, 512, 32, 256], P(None, 'gx', 'gy', 'ga'), may hold values from 4 to 16
- fine_couple: bfloat16 [7, 3, 3, 512, 32, 256], P(None, None, None, 'gx', 'gy', 'ga'), may hold values from -1 to 1
- fine_prolong: float32 [3, 3, 512, 32, 256], P(None, None, 'gx', 'gy', 'ga'), may hold values from -3.5 to 3.5
- middle_stiff: float32 [3, 256, 16, 128], P(None, 'gx', 'gy', 'ga'), may hold values from 12 to 48
- middle_couple: bfloat16 [7, 3, 3, 256, 16, 128], P(None, None, None, 'gx', 'gy', 'ga'), may hold values from -3 to 3
- middle_prolong: float32 [3, 3, 256, 16, 128], P(None, None, 'gx', 'gy', 'ga'), may hold values from -3.5 to 3.5
- coarse_stiff: float32 [3, 128, 16, 64], P(None, 'gx', 'gy', 'ga'), may hold values from 36 to 144
- coarse_couple: bfloat16 [7, 3, 3, 128, 16, 64], P(None, None, None, 'gx', 'gy', 'ga'), may hold values from -9 to 9
- coarse_prolong: float32 [3, 3, 128, 16, 64], P(None, None, 'gx', 'gy', 'ga'), may hold values from -3.5 to 3.5
- bottom_stiff: float32 [3, 16384], replicated, may hold values from 48 to 192
- bottom_couple: bfloat16 [7, 3, 3, 16384], replicated, may hold values from -27 to 27
Outputs:
- solution: float32 [3, 512, 32, 256], P(None, 'gx', 'gy', 'ga')
- residual: float32 [3, 512, 32, 256], P(None, 'gx', 'gy', 'ga')
All inputs are finite; a program needn't handle non-finite values.
Results may differ from a plain program's by a relative error of at most 0.0003.
Values sent between devices are 32-bit elements; how exact they have to be, the bound alone decides.
No kernel may reach another device: no remote copies, remote signals or barrier semaphores. Data moves between devices by JAX's collectives and lax.ppermute only.
A program may use at most 128 MiB of HBM per device.

v0:
```python
import jax
import jax.numpy as jnp
from jax import lax
from jax.sharding import PartitionSpec as P

SWEEPS = 8


center_value = 1.0
half_width = 0.7
damping = 0.7
ratio_first = half_width / center_value
ratio_second = 1.0 / (2.0 * center_value / half_width - ratio_first)
carry_coef = ratio_second * ratio_first
fresh_coef = 2.0 * ratio_second / half_width
inverse_center = 1.0 / center_value
level_factors = ((2, 2, 2), (2, 1, 2), (2, 1, 4))


def extended(cells, sides, width):
    for axis, dim in sides:
        count = lax.axis_size(axis)
        ends = count - 1
        head = lax.slice_in_dim(cells, 0, width, axis=dim)
        tail = lax.slice_in_dim(cells, cells.shape[dim] - width, cells.shape[dim], axis=dim)
        cells = jnp.concatenate(
            [
                lax.ppermute(tail, axis, [(i, (i + 1) % count) for i in range(ends)]),
                cells,
                lax.ppermute(head, axis, [((i + 1) % count, i) for i in range(ends)]),
            ],
            axis=dim,
        )
    return cells


def fine_spread(field):
    return extended(field, (("gx", 1), ("gy", 2), ("ga", 3)), 1)


def middle_spread(field):
    return extended(field, (("gx", 1), ("gy", 2), ("ga", 3)), 1)


def coarse_spread(field):
    return extended(field, (("gx", 1), ("gy", 2), ("ga", 3)), 1)


def bottom_spread(field):
    return extended(field, (("gx", 1), ("gy", 2), ("ga", 3)), 1)


def apply_operator(padded, stiff, couple):
    inner = padded[:, 1:-1, 1:-1, 1:-1]
    views = (
        inner,
        padded[:, :-2, 1:-1, 1:-1],
        padded[:, 2:, 1:-1, 1:-1],
        padded[:, 1:-1, :-2, 1:-1],
        padded[:, 1:-1, 2:, 1:-1],
        padded[:, 1:-1, 1:-1, :-2],
        padded[:, 1:-1, 1:-1, 2:],
    )
    rows_out = []
    for comp in range(3):
        total = stiff[comp] * inner[comp]
        for direction in range(7):
            for source in range(3):
                total = (
                    total
                    + couple[direction, comp, source].astype(jnp.float32) * views[direction][source]
                )
        rows_out.append(total)
    return jnp.stack(rows_out)


def smooth(solution, residual, stiff, couple, spread, keep_residual):
    first = residual / stiff * inverse_center
    solution = solution + first
    residual = residual - apply_operator(spread(first), stiff, couple)
    second = carry_coef * first + fresh_coef * (residual / stiff)
    solution = solution + second
    if keep_residual:
        residual = residual - apply_operator(spread(second), stiff, couple)
    return (solution, residual)


def restrict(prolong, residual, factors):
    term = jnp.sum(prolong * residual[:, None], axis=0)
    shape = term.shape
    term = term.reshape(
        3,
        shape[1] // factors[0],
        factors[0],
        shape[2] // factors[1],
        factors[1],
        shape[3] // factors[2],
        factors[2],
    )
    return jnp.sum(term, axis=(2, 4, 6))


def prolongate(prolong, coarse, factors):
    shape = coarse.shape
    upward = jnp.broadcast_to(
        coarse[:, :, None, :, None, :, None],
        (3, shape[1], factors[0], shape[2], factors[1], shape[3], factors[2]),
    )
    upward = upward.reshape(3, shape[1] * factors[0], shape[2] * factors[1], shape[3] * factors[2])
    return jnp.sum(prolong * upward[None], axis=1)


def jacobi(load, stiff, couple, spread):
    solution = damping * load / stiff
    for sweep in range(SWEEPS - 1):
        solution = (
            solution + damping * (load - apply_operator(spread(solution), stiff, couple)) / stiff
        )
    return solution


def local(
    right_side,
    fine_stiff,
    fine_couple,
    fine_prolong,
    middle_stiff,
    middle_couple,
    middle_prolong,
    coarse_stiff,
    coarse_couple,
    coarse_prolong,
    bottom_stiff,
    bottom_couple,
):
    levels = (
        (fine_stiff, fine_couple, fine_prolong),
        (middle_stiff, middle_couple, middle_prolong),
        (coarse_stiff, coarse_couple, coarse_prolong),
    )
    spreads = (fine_spread, middle_spread, coarse_spread)
    loads = [right_side]
    before = []
    for level in range(3):
        stiff, couple, prolong = levels[level]
        load = loads[level]
        smoothed, remain = smooth(jnp.zeros_like(load), load, stiff, couple, spreads[level], True)
        before.append(smoothed)
        loads.append(restrict(prolong, remain, level_factors[level]))
    bottom_load = loads[3]
    block_x, block_y, block_z = (bottom_load.shape[1], bottom_load.shape[2], bottom_load.shape[3])
    devices_x = lax.axis_size("gx")
    devices_y = lax.axis_size("gy")
    devices_z = lax.axis_size("ga")
    grid_shape = (devices_x * block_x, devices_y * block_y, devices_z * block_z)
    grid_stiff = bottom_stiff.reshape((3,) + grid_shape)
    grid_couple = bottom_couple.reshape((7, 3, 3) + grid_shape)
    first_row = lax.axis_index("gx") * block_x
    first_col = lax.axis_index("gy") * block_y
    first_deep = lax.axis_index("ga") * block_z
    own_stiff = lax.dynamic_slice(
        grid_stiff, (0, first_row, first_col, first_deep), (3, block_x, block_y, block_z)
    )
    own_couple = lax.dynamic_slice(
        grid_couple,
        (0, 0, 0, first_row, first_col, first_deep),
        (7, 3, 3, block_x, block_y, block_z),
    )
    correction = jacobi(bottom_load, own_stiff, own_couple, bottom_spread)
    remain = loads[0]
    for level in (2, 1, 0):
        stiff, couple, prolong = levels[level]
        guess = before[level] + prolongate(prolong, correction, level_factors[level])
        remain = loads[level] - apply_operator(spreads[level](guess), stiff, couple)
        correction, remain = smooth(guess, remain, stiff, couple, spreads[level], level == 0)
    return (correction, remain)


def solution(mesh):
    placed = (
        P(None, "gx", "gy", "ga"),
        P(None, "gx", "gy", "ga"),
        P(None, None, None, "gx", "gy", "ga"),
        P(None, None, "gx", "gy", "ga"),
        P(None, "gx", "gy", "ga"),
        P(None, None, None, "gx", "gy", "ga"),
        P(None, None, "gx", "gy", "ga"),
        P(None, "gx", "gy", "ga"),
        P(None, None, None, "gx", "gy", "ga"),
        P(None, None, "gx", "gy", "ga"),
        P(),
        P(),
    )
    return jax.shard_map(
        local,
        mesh=mesh,
        in_specs=placed,
        out_specs=(P(None, "gx", "gy", "ga"), P(None, "gx", "gy", "ga")),
        check_vma=False,
    )
```

profile of v0, /device:TPU:25, one launch (start us, length us, event | category | flops | bytes accessed | tf_op | source)
XLA Modules:
  0.0 594.1 jit_solution(10012544663690681022)
XLA Ops:
  5.3 9.7 %collective-permute-start.1 = (f32[3,1,8,128]{3,2,1,0:T(8,128)S(1)}, f32[3,1,8,128]{3,2,1,0:T(8,128)S(1)}, u32[]{:S(2)}, u32[]{:S(2)}) collective-permute-start(f32[3,1,8,128]{3,2,1,0:T(8,128)S(1)} %get-tuple-element.493), channel_id=1, source_target_pairs={{8,0},{16,8},{24,16},{32,24},{40,32},{48,40},{56,48},{64,56},{72,6... | collective-permute-start | bytes 36872 | tf_op jit(solution)/shard_map/ppermute | solution.py:30
  24.9 4.9 collective-permute-start.5
  37.1 6.0 %collective-permute-start.7 = (f32[3,1,8,128]{3,2,1,0:T(8,128)S(1)}, f32[3,1,8,128]{3,2,1,0:T(8,128)S(1)}, u32[]{:S(2)}, u32[]{:S(2)}) collective-permute-start(f32[3,1,8,128]{3,2,1,0:T(8,128)S(1)} %get-tuple-element.491), channel_id=1, source_target_pairs={{8,0},{16,8},{24,16},{32,24},{40,32},{48,40},{56,48},{64,56},{72,6... | collective-permute-start | bytes 36872 | tf_op jit(solution)/shard_map/ppermute | solution.py:30
  53.1 4.6 collective-permute-start.11
  59.4 7.7 %reshape.6937 = f32[3,4,2,4,2,64,2]{6,5,4,3,2,1,0:T(8,128)} reshape(f32[3,8,8,128]{3,2,1,0:T(8,128)S(1)} %multiply_reduce_fusion.1) | data formatting | bytes 196608 | tf_op jit(solution)/shard_map/reshape | solution.py:91
  70.5 6.0 %collective-permute-start.13 = (f32[3,1,4,64]{3,2,1,0:T(4,128)S(1)}, f32[3,1,4,64]{3,2,1,0:T(4,128)S(1)}, u32[]{:S(2)}, u32[]{:S(2)}) collective-permute-start(f32[3,1,4,64]{3,2,1,0:T(4,128)S(1)} %get-tuple-element.562), channel_id=1, source_target_pairs={{8,0},{16,8},{24,16},{32,24},{40,32},{48,40},{56,48},{64,56},{72,6... | collective-permute-start | bytes 9224 | tf_op jit(solution)/shard_map/ppermute | solution.py:30
  78.4 4.5 collective-permute-done.12
  90.5 4.8 collective-permute-start.17
  106.3 4.5 collective-permute-start.20
  123.1 5.5 collective-permute-start.25
  188.5 5.5 collective-permute-start.31
  208.0 4.9 collective-permute-start.35
  222.3 6.2 %collective-permute-start.37 = (f32[3,1,4,8]{3,2,0,1:T(4,128)S(1)}, f32[3,1,4,8]{3,2,0,1:T(4,128)S(1)}, u32[]{:S(2)}, u32[]{:S(2)}) collective-permute-start(f32[3,1,4,8]{3,2,0,1:T(4,128)S(1)} %get-tuple-element.281), channel_id=1, source_target_pairs={{8,0},{16,8},{24,16},{32,24},{40,32},{48,40},{56,48},{64,56},{72,6... | collective-permute-start | bytes 1160 | tf_op jit(solution)/shard_map/ppermute | solution.py:30
  230.5 4.5 collective-permute-done.36
  242.5 4.9 collective-permute-start.41
  247.5 15.1 %reshape.6940 = bf16[7,3,3,64,16,16]{5,4,3,0,2,1:T(8,128)(2,1)} reshape(bf16[7,3,3,16384]{3,0,2,1:T(8,128)(2,1)} %param.23) | data formatting | bytes 4128768 | tf_op jit(solution)/shard_map/reshape | solution.py:157
  275.4 4.5 collective-permute-start.44
  296.1 4.5 collective-permute-start.50
  317.8 4.5 collective-permute-start.56
  339.6 4.5 collective-permute-start.62
  361.3 4.5 collective-permute-start.68
  397.4 5.5 collective-permute-start.79
  430.1 5.9 collective-permute-start.85
  462.2 5.8 collective-permute-start.91
  470.0 4.5 collective-permute-done.90
  497.6 4.5 collective-permute-start.98
  513.4 5.6 mul.7536
  521.0 5.5 collective-permute-start.103
  537.4 4.6 collective-permute-start.107
  545.6 6.0 %collective-permute-start.109 = (f32[3,1,8,128]{3,2,1,0:T(8,128)S(1)}, f32[3,1,8,128]{3,2,1,0:T(8,128)S(1)}, u32[]{:S(2)}, u32[]{:S(2)}) collective-permute-start(f32[3,1,8,128]{3,2,1,0:T(8,128)S(1)} %get-tuple-element.479), channel_id=1, source_target_pairs={{8,0},{16,8},{24,16},{32,24},{40,32},{48,40},{56,48},{64,56},{72,6... | collective-permute-start | bytes 36872 | tf_op jit(solution)/shard_map/ppermute | solution.py:30
  570.8 6.0 %collective-permute-start.115 = (f32[3,1,8,128]{3,2,1,0:T(8,128)S(1)}, f32[3,1,8,128]{3,2,1,0:T(8,128)S(1)}, u32[]{:S(2)}, u32[]{:S(2)}) collective-permute-start(f32[3,1,8,128]{3,2,1,0:T(8,128)S(1)} %get-tuple-element.477), channel_id=1, source_target_pairs={{8,0},{16,8},{24,16},{32,24},{40,32},{48,40},{56,48},{64,56},{72,6... | collective-permute-start | bytes 36872 | tf_op jit(solution)/shard_map/ppermute | solution.py:30
  587.3 4.6 collective-permute-start.119
  (619 shorter events, 410.0 us)
Async XLA Ops:
  1.8 13.2 %collective-permute-start = (f32[3,1,8,128]{3,2,1,0:T(8,128)S(1)}, f32[3,1,8,128]{3,2,1,0:T(8,128)S(1)}, u32[]{:S(2)}, u32[]{:S(2)}) collective-permute-start(f32[3,1,8,128]{3,2,1,0:T(8,128)S(1)} %get-tuple-element.492), channel_id=1, source_target_pairs={{0,8},{8,16},{16,24},{24,32},{32,40},{40,48},{48,56},{56,64},{64,7... | collective-permute-start | bytes 36872 | tf_op jit(solution)/shard_map/ppermute | solution.py:28
  5.3 10.5 %collective-permute-start.1 = (f32[3,1,8,128]{3,2,1,0:T(8,128)S(1)}, f32[3,1,8,128]{3,2,1,0:T(8,128)S(1)}, u32[]{:S(2)}, u32[]{:S(2)}) collective-permute-start(f32[3,1,8,128]{3,2,1,0:T(8,128)S(1)} %get-tuple-element.493), channel_id=1, source_target_pairs={{8,0},{16,8},{24,16},{32,24},{40,32},{48,40},{56,48},{64,56},{72,6... | collective-permute-start | bytes 36872 | tf_op jit(solution)/shard_map/ppermute | solution.py:30
  35.2 8.0 %collective-permute-start.6 = (f32[3,1,8,128]{3,2,1,0:T(8,128)S(1)}, f32[3,1,8,128]{3,2,1,0:T(8,128)S(1)}, u32[]{:S(2)}, u32[]{:S(2)}) collective-permute-start(f32[3,1,8,128]{3,2,1,0:T(8,128)S(1)} %get-tuple-element.490), channel_id=1, source_target_pairs={{0,8},{8,16},{16,24},{24,32},{32,40},{40,48},{48,56},{56,64},{64,7... | collective-permute-start | bytes 36872 | tf_op jit(solution)/shard_map/ppermute | solution.py:28
  37.1 6.8 %collective-permute-start.7 = (f32[3,1,8,128]{3,2,1,0:T(8,128)S(1)}, f32[3,1,8,128]{3,2,1,0:T(8,128)S(1)}, u32[]{:S(2)}, u32[]{:S(2)}) collective-permute-start(f32[3,1,8,128]{3,2,1,0:T(8,128)S(1)} %get-tuple-element.491), channel_id=1, source_target_pairs={{8,0},{16,8},{24,16},{32,24},{40,32},{48,40},{56,48},{64,56},{72,6... | collective-permute-start | bytes 36872 | tf_op jit(solution)/shard_map/ppermute | solution.py:30
  70.5 8.0 %collective-permute-start.13 = (f32[3,1,4,64]{3,2,1,0:T(4,128)S(1)}, f32[3,1,4,64]{3,2,1,0:T(4,128)S(1)}, u32[]{:S(2)}, u32[]{:S(2)}) collective-permute-start(f32[3,1,4,64]{3,2,1,0:T(4,128)S(1)} %get-tuple-element.562), channel_id=1, source_target_pairs={{8,0},{16,8},{24,16},{32,24},{40,32},{48,40},{56,48},{64,56},{72,6... | collective-permute-start | bytes 9224 | tf_op jit(solution)/shard_map/ppermute | solution.py:30
  89.2 6.8 %collective-permute-start.16 = (f32[3,6,6,1]{3,2,1,0:T(8,128)S(1)}, f32[3,6,6,1]{3,2,1,0:T(8,128)S(1)}, u32[]{:S(2)}, u32[]{:S(2)}) collective-permute-start(f32[3,6,6,1]{3,2,1,0:T(8,128)S(1)} %get-tuple-element.524), channel_id=1, source_target_pairs={{0,1},{2,3},{4,5},{6,7},{8,9},{10,11},{12,13},{14,15},{16,17},{18,... | collective-permute-start | bytes 1304 | tf_op jit(solution)/shard_map/ppermute | solution.py:28
  105.0 9.2 %collective-permute-start.21 = (f32[3,6,1,64]{3,2,1,0:T(1,128)S(1)}, f32[3,6,1,64]{3,2,1,0:T(1,128)S(1)}, u32[]{:S(2)}, u32[]{:S(2)}) collective-permute-start(f32[3,6,1,64]{3,2,1,0:T(1,128)S(1)} %get-tuple-element.552), channel_id=1, source_target_pairs={{2,0},{4,2},{6,4},{3,1},{5,3},{7,5},{10,8},{12,10},{14,12},{11,9},... | collective-permute-start | bytes 13832 | tf_op jit(solution)/shard_map/ppermute | solution.py:30
  106.3 7.9 %collective-permute-start.20 = (f32[3,6,1,64]{3,2,1,0:T(1,128)S(1)}, f32[3,6,1,64]{3,2,1,0:T(1,128)S(1)}, u32[]{:S(2)}, u32[]{:S(2)}) collective-permute-start(f32[3,6,1,64]{3,2,1,0:T(1,128)S(1)} %get-tuple-element.553), channel_id=1, source_target_pairs={{0,2},{2,4},{4,6},{1,3},{3,5},{5,7},{8,10},{10,12},{12,14},{9,11},... | collective-permute-start | bytes 13832 | tf_op jit(solution)/shard_map/ppermute | solution.py:28
  121.2 26.0 %collective-permute-start.24 = (f32[3,1,4,32]{2,3,1,0:T(8,128)S(1)}, f32[3,1,4,32]{2,3,1,0:T(8,128)S(1)}, u32[]{:S(2)}, u32[]{:S(2)}) collective-permute-start(f32[3,1,4,32]{2,3,1,0:T(8,128)S(1)} %get-tuple-element.488), channel_id=1, source_target_pairs={{0,8},{8,16},{16,24},{24,32},{32,40},{40,48},{48,56},{56,64},{64,7... | collective-permute-start | bytes 4616 | tf_op jit(solution)/shard_map/ppermute | solution.py:28
  123.1 24.1 %collective-permute-start.25 = (f32[3,1,4,32]{2,3,1,0:T(8,128)S(1)}, f32[3,1,4,32]{2,3,1,0:T(8,128)S(1)}, u32[]{:S(2)}, u32[]{:S(2)}) collective-permute-start(f32[3,1,4,32]{2,3,1,0:T(8,128)S(1)} %get-tuple-element.489), channel_id=1, source_target_pairs={{8,0},{16,8},{24,16},{32,24},{40,32},{48,40},{56,48},{64,56},{72,6... | collective-permute-start | bytes 4616 | tf_op jit(solution)/shard_map/ppermute | solution.py:30
  148.1 24.8 %collective-permute-start.26 = (f32[3,4,1,32]{2,3,1,0:T(8,128)}, f32[3,4,1,32]{2,3,1,0:T(8,128)S(1)}, u32[]{:S(2)}, u32[]{:S(2)}) collective-permute-start(f32[3,4,1,32]{2,3,1,0:T(8,128)} %get-tuple-element.401), channel_id=1, source_target_pairs={{0,2},{2,4},{4,6},{1,3},{3,5},{5,7},{8,10},{10,12},{12,14},{9,11},... | collective-permute-start | bytes 4616 | tf_op jit(solution)/shard_map/ppermute | solution.py:28
  151.7 21.3 %collective-permute-start.27 = (f32[3,4,1,32]{2,3,1,0:T(8,128)}, f32[3,4,1,32]{2,3,1,0:T(8,128)S(1)}, u32[]{:S(2)}, u32[]{:S(2)}) collective-permute-start(f32[3,4,1,32]{2,3,1,0:T(8,128)} %get-tuple-element.402), channel_id=1, source_target_pairs={{2,0},{4,2},{6,4},{3,1},{5,3},{7,5},{10,8},{12,10},{14,12},{11,9},... | collective-permute-start | bytes 4616 | tf_op jit(solution)/shard_map/ppermute | solution.py:30
  174.0 7.1 %collective-permute-start.29 = (f32[3,4,6,1]{3,1,2,0:T(4,128)S(1)}, f32[3,4,6,1]{3,1,2,0:T(4,128)S(1)}, u32[]{:S(2)}, u32[]{:S(2)}) collective-permute-start(f32[3,4,6,1]{3,1,2,0:T(4,128)S(1)} %get-tuple-element.550), channel_id=1, source_target_pairs={{1,0},{3,2},{5,4},{7,6},{9,8},{11,10},{13,12},{15,14},{17,16},{19,... | collective-permute-start | bytes 872 | tf_op jit(solution)/shard_map/ppermute | solution.py:30
  186.6 7.4 %collective-permute-start.30 = (f32[3,1,4,32]{2,3,1,0:T(8,128)S(1)}, f32[3,1,4,32]{2,3,1,0:T(8,128)S(1)}, u32[]{:S(2)}, u32[]{:S(2)}) collective-permute-start(f32[3,1,4,32]{2,3,1,0:T(8,128)S(1)} %get-tuple-element.486), channel_id=1, source_target_pairs={{0,8},{8,16},{16,24},{24,32},{32,40},{40,48},{48,56},{56,64},{64,7... | collective-permute-start | bytes 4616 | tf_op jit(solution)/shard_map/ppermute | solution.py:28
  188.5 6.6 %collective-permute-start.31 = (f32[3,1,4,32]{2,3,1,0:T(8,128)S(1)}, f32[3,1,4,32]{2,3,1,0:T(8,128)S(1)}, u32[]{:S(2)}, u32[]{:S(2)}) collective-permute-start(f32[3,1,4,32]{2,3,1,0:T(8,128)S(1)} %get-tuple-element.487), channel_id=1, source_target_pairs={{8,0},{16,8},{24,16},{32,24},{40,32},{48,40},{56,48},{64,56},{72,6... | collective-permute-start | bytes 4616 | tf_op jit(solution)/shard_map/ppermute | solution.py:30
  196.0 9.1 %collective-permute-start.32 = (f32[3,4,1,32]{2,3,1,0:T(8,128)}, f32[3,4,1,32]{2,3,1,0:T(8,128)S(1)}, u32[]{:S(2)}, u32[]{:S(2)}) collective-permute-start(f32[3,4,1,32]{2,3,1,0:T(8,128)} %get-tuple-element.399), channel_id=1, source_target_pairs={{0,2},{2,4},{4,6},{1,3},{3,5},{5,7},{8,10},{10,12},{12,14},{9,11},... | collective-permute-start | bytes 4616 | tf_op jit(solution)/shard_map/ppermute | solution.py:28
  222.3 8.2 %collective-permute-start.37 = (f32[3,1,4,8]{3,2,0,1:T(4,128)S(1)}, f32[3,1,4,8]{3,2,0,1:T(4,128)S(1)}, u32[]{:S(2)}, u32[]{:S(2)}) collective-permute-start(f32[3,1,4,8]{3,2,0,1:T(4,128)S(1)} %get-tuple-element.281), channel_id=1, source_target_pairs={{8,0},{16,8},{24,16},{32,24},{40,32},{48,40},{56,48},{64,56},{72,6... | collective-permute-start | bytes 1160 | tf_op jit(solution)/shard_map/ppermute | solution.py:30
  241.2 21.4 %collective-permute-start.40 = (f32[3,3,6,1]{3,2,0,1:T(8,128)S(1)}, f32[3,3,6,1]{3,2,0,1:T(8,128)S(1)}, u32[]{:S(2)}, u32[]{:S(2)}) collective-permute-start(f32[3,3,6,1]{3,2,0,1:T(8,128)S(1)} %get-tuple-element.546), channel_id=1, source_target_pairs={{0,1},{2,3},{4,5},{6,7},{8,9},{10,11},{12,13},{14,15},{16,17},{18,... | collective-permute-start | bytes 656 | tf_op jit(solution)/shard_map/ppermute | solution.py:28
  242.5 20.1 %collective-permute-start.41 = (f32[3,3,6,1]{3,2,0,1:T(8,128)S(1)}, f32[3,3,6,1]{3,2,0,1:T(8,128)S(1)}, u32[]{:S(2)}, u32[]{:S(2)}) collective-permute-start(f32[3,3,6,1]{3,2,0,1:T(8,128)S(1)} %get-tuple-element.547), channel_id=1, source_target_pairs={{1,0},{3,2},{5,4},{7,6},{9,8},{11,10},{13,12},{15,14},{17,16},{19,... | collective-permute-start | bytes 656 | tf_op jit(solution)/shard_map/ppermute | solution.py:30
  395.4 7.4 %collective-permute-start.78 = (f32[3,1,4,32]{2,3,1,0:T(8,128)S(1)}, f32[3,1,4,32]{2,3,1,0:T(8,128)S(1)}, u32[]{:S(2)}, u32[]{:S(2)}) collective-permute-start(f32[3,1,4,32]{2,3,1,0:T(8,128)S(1)} %get-tuple-element.484), channel_id=1, source_target_pairs={{0,8},{8,16},{16,24},{24,32},{32,40},{40,48},{48,56},{56,64},{64,7... | collective-permute-start | bytes 4616 | tf_op jit(solution)/shard_map/ppermute | solution.py:28
  404.8 6.8 %collective-permute-start.80 = (f32[3,4,1,32]{2,3,1,0:T(8,128)}, f32[3,4,1,32]{2,3,1,0:T(8,128)S(1)}, u32[]{:S(2)}, u32[]{:S(2)}) collective-permute-start(f32[3,4,1,32]{2,3,1,0:T(8,128)} %get-tuple-element.397), channel_id=1, source_target_pairs={{0,2},{2,4},{4,6},{1,3},{3,5},{5,7},{8,10},{10,12},{12,14},{9,11},... | collective-permute-start | bytes 4616 | tf_op jit(solution)/shard_map/ppermute | solution.py:28
  408.7 7.3 %collective-permute-start.81 = (f32[3,4,1,32]{2,3,1,0:T(8,128)}, f32[3,4,1,32]{2,3,1,0:T(8,128)S(1)}, u32[]{:S(2)}, u32[]{:S(2)}) collective-permute-start(f32[3,4,1,32]{2,3,1,0:T(8,128)} %get-tuple-element.398), channel_id=1, source_target_pairs={{2,0},{4,2},{6,4},{3,1},{5,3},{7,5},{10,8},{12,10},{14,12},{11,9},... | collective-permute-start | bytes 4616 | tf_op jit(solution)/shard_map/ppermute | solution.py:30
  428.1 7.9 %collective-permute-start.84 = (f32[3,1,4,32]{2,3,1,0:T(8,128)S(1)}, f32[3,1,4,32]{2,3,1,0:T(8,128)S(1)}, u32[]{:S(2)}, u32[]{:S(2)}) collective-permute-start(f32[3,1,4,32]{2,3,1,0:T(8,128)S(1)} %get-tuple-element.482), channel_id=1, source_target_pairs={{0,8},{8,16},{16,24},{24,32},{32,40},{40,48},{48,56},{56,64},{64,7... | collective-permute-start | bytes 4616 | tf_op jit(solution)/shard_map/ppermute | solution.py:28
  430.1 7.1 %collective-permute-start.85 = (f32[3,1,4,32]{2,3,1,0:T(8,128)S(1)}, f32[3,1,4,32]{2,3,1,0:T(8,128)S(1)}, u32[]{:S(2)}, u32[]{:S(2)}) collective-permute-start(f32[3,1,4,32]{2,3,1,0:T(8,128)S(1)} %get-tuple-element.483), channel_id=1, source_target_pairs={{8,0},{16,8},{24,16},{32,24},{40,32},{48,40},{56,48},{64,56},{72,6... | collective-permute-start | bytes 4616 | tf_op jit(solution)/shard_map/ppermute | solution.py:30
  438.0 6.8 %collective-permute-start.86 = (f32[3,4,1,32]{2,3,1,0:T(8,128)}, f32[3,4,1,32]{2,3,1,0:T(8,128)S(1)}, u32[]{:S(2)}, u32[]{:S(2)}) collective-permute-start(f32[3,4,1,32]{2,3,1,0:T(8,128)} %get-tuple-element.395), channel_id=1, source_target_pairs={{0,2},{2,4},{4,6},{1,3},{3,5},{5,7},{8,10},{10,12},{12,14},{9,11},... | collective-permute-start | bytes 4616 | tf_op jit(solution)/shard_map/ppermute | solution.py:28
  441.6 7.5 %collective-permute-start.87 = (f32[3,4,1,32]{2,3,1,0:T(8,128)}, f32[3,4,1,32]{2,3,1,0:T(8,128)S(1)}, u32[]{:S(2)}, u32[]{:S(2)}) collective-permute-start(f32[3,4,1,32]{2,3,1,0:T(8,128)} %get-tuple-element.396), channel_id=1, source_target_pairs={{2,0},{4,2},{6,4},{3,1},{5,3},{7,5},{10,8},{12,10},{14,12},{11,9},... | collective-permute-start | bytes 4616 | tf_op jit(solution)/shard_map/ppermute | solution.py:30
  462.2 7.7 %collective-permute-start.91 = (f32[3,1,4,64]{3,2,1,0:T(4,128)S(1)}, f32[3,1,4,64]{3,2,1,0:T(4,128)S(1)}, u32[]{:S(2)}, u32[]{:S(2)}) collective-permute-start(f32[3,1,4,64]{3,2,1,0:T(4,128)S(1)} %get-tuple-element.558), channel_id=1, source_target_pairs={{8,0},{16,8},{24,16},{32,24},{40,32},{48,40},{56,48},{64,56},{72,6... | collective-permute-start | bytes 9224 | tf_op jit(solution)/shard_map/ppermute | solution.py:30
  519.1 7.4 %collective-permute-start.102 = (f32[3,1,8,128]{3,2,1,0:T(8,128)S(1)}, f32[3,1,8,128]{3,2,1,0:T(8,128)S(1)}, u32[]{:S(2)}, u32[]{:S(2)}) collective-permute-start(f32[3,1,8,128]{3,2,1,0:T(8,128)S(1)} %get-tuple-element.480), channel_id=1, source_target_pairs={{0,8},{8,16},{16,24},{24,32},{32,40},{40,48},{48,56},{56,64},{64,7... | collective-permute-start | bytes 36872 | tf_op jit(solution)/shard_map/ppermute | solution.py:28
  543.6 8.0 %collective-permute-start.108 = (f32[3,1,8,128]{3,2,1,0:T(8,128)S(1)}, f32[3,1,8,128]{3,2,1,0:T(8,128)S(1)}, u32[]{:S(2)}, u32[]{:S(2)}) collective-permute-start(f32[3,1,8,128]{3,2,1,0:T(8,128)S(1)} %get-tuple-element.478), channel_id=1, source_target_pairs={{0,8},{8,16},{16,24},{24,32},{32,40},{40,48},{48,56},{56,64},{64,7... | collective-permute-start | bytes 36872 | tf_op jit(solution)/shard_map/ppermute | solution.py:28
  545.6 6.8 %collective-permute-start.109 = (f32[3,1,8,128]{3,2,1,0:T(8,128)S(1)}, f32[3,1,8,128]{3,2,1,0:T(8,128)S(1)}, u32[]{:S(2)}, u32[]{:S(2)}) collective-permute-start(f32[3,1,8,128]{3,2,1,0:T(8,128)S(1)} %get-tuple-element.479), channel_id=1, source_target_pairs={{8,0},{16,8},{24,16},{32,24},{40,32},{48,40},{56,48},{64,56},{72,6... | collective-permute-start | bytes 36872 | tf_op jit(solution)/shard_map/ppermute | solution.py:30
  568.9 8.0 %collective-permute-start.114 = (f32[3,1,8,128]{3,2,1,0:T(8,128)S(1)}, f32[3,1,8,128]{3,2,1,0:T(8,128)S(1)}, u32[]{:S(2)}, u32[]{:S(2)}) collective-permute-start(f32[3,1,8,128]{3,2,1,0:T(8,128)S(1)} %get-tuple-element.476), channel_id=1, source_target_pairs={{0,8},{8,16},{16,24},{24,32},{32,40},{40,48},{48,56},{56,64},{64,7... | collective-permute-start | bytes 36872 | tf_op jit(solution)/shard_map/ppermute | solution.py:28
  570.8 6.8 %collective-permute-start.115 = (f32[3,1,8,128]{3,2,1,0:T(8,128)S(1)}, f32[3,1,8,128]{3,2,1,0:T(8,128)S(1)}, u32[]{:S(2)}, u32[]{:S(2)}) collective-permute-start(f32[3,1,8,128]{3,2,1,0:T(8,128)S(1)} %get-tuple-element.477), channel_id=1, source_target_pairs={{8,0},{16,8},{24,16},{32,24},{40,32},{48,40},{56,48},{64,56},{72,6... | collective-permute-start | bytes 36872 | tf_op jit(solution)/shard_map/ppermute | solution.py:30
  (144 other events, 4338.7 us)
where the time goes:
time: 600 us; the launch traced here: 594 us
  starting transfers between devices  360 us (60%)
  waiting for transfers between devices  98.1 us (16%)
  local copies, waits for them, and re-layouts  92 us (15%)
  other arithmetic  40.9 us (7%)
    ppermute x60, starting transfers between devices, extended(): lax.ppermute(head, axis, [((i + 1) % count, i) for i in range(ends)])  201 us
    ppermute x60, starting transfers between devices, extended(): lax.ppermute(tail, axis, [(i, (i + 1) % count) for i in range(ends)])  159 us
    ppermute x60, waiting for transfers between devices, extended(): lax.ppermute(tail, axis, [(i, (i + 1) % count) for i in range(ends)])  51.5 us
    ppermute x60, waiting for transfers between devices, extended(): lax.ppermute(head, axis, [((i + 1) % count, i) for i in range(ends)])  46.7 us
    slice x67, local copies, waits for them, and re-layouts, apply_operator(): couple[direction, comp, source].astype(jnp.float32)  45.3 us
    add x60, other arithmetic, apply_operator(): total + couple[direction, comp, source].astype(jnp.float32) * views[direc...  20 us
    reshape x1, local copies, waits for them, and re-layouts, local(): grid_couple = bottom_couple.reshape((7, 3, 3) + grid_shape)  15.1 us
  transfers between devices with their start and end apart: 120, of which 58 were waited for; matrix products, arithmetic and copies ran while one was open for 12% of the time, Pallas kernels for 0%

commit v1 on v0

v1 whole, which is shorter than its diff:
```python
import jax
import jax.numpy as jnp
from jax import lax
from jax.experimental import pallas as pl
from jax.experimental.pallas import tpu as pltpu
from jax.sharding import PartitionSpec as P

SWEEPS = 8
center_value = 1.0
half_width = 0.7
damping = 0.7
ratio_first = half_width / center_value
ratio_second = 1.0 / (2.0 * center_value / half_width - ratio_first)
carry_coef = ratio_second * ratio_first
fresh_coef = 2.0 * ratio_second / half_width

F32 = jnp.float32
REACH = 8
WINDOW = 2 * REACH + 1
ROWS = 40


def iota(shape, dim):
    return lax.broadcasted_iota(jnp.int32, shape, dim)


def dot(a, b):
    return jnp.dot(a, b, precision=lax.Precision.HIGHEST, preferred_element_type=F32)


def combine(stiff, coef, views):
    outs = []
    for a in range(3):
        total = stiff[a] * views[0][a]
        for k in range(7):
            for b in range(3):
                total = total + coef(k * 9 + a * 3 + b) * views[k][b]
        outs.append(total)
    return outs


class Fine:
    def __init__(self, ids):
        self.core = ids[0]
        self.spot = (ids[0], 1 - ids[0])
        right = ids[0].astype(F32)
        self.right = (right, 1.0 - right)
        self.row = iota((8, 128), 0)
        self.lane = iota((8, 128), 1)

    def apply(self, get, halo, stiff, coefs, use, halves=(0, 1)):
        for x in range(8):
            mids = [[get(h, b, x) for b in range(3)] for h in range(2)]
            for h in halves:
                views = [mids[h]]
                spot = self.spot[h]
                lows, highs = [], []
                for b in range(3):
                    lows.append(halo[0, 0, spot, 8 * b : 8 * b + 8, :] if x == 0 else get(h, b, x - 1))
                    highs.append(halo[1, 0, spot, 8 * b : 8 * b + 8, :] if x == 7 else get(h, b, x + 1))
                views += [lows, highs]
                lows, highs = [], []
                for b in range(3):
                    at = 8 * b + x
                    v = mids[h][b]
                    edge = jnp.broadcast_to(halo[0, 1, spot, at : at + 1, :], (8, 128))
                    lows.append(jnp.where(self.row == 0, edge, pltpu.roll(v, 1, 0)))
                    edge = jnp.broadcast_to(halo[1, 1, spot, at : at + 1, :], (8, 128))
                    highs.append(jnp.where(self.row == 7, edge, pltpu.roll(v, 7, 0)))
                views += [lows, highs]
                lows, highs = [], []
                for b in range(3):
                    v, o = mids[h][b], mids[1 - h][b]
                    lows.append(
                        jnp.where(self.lane == 0, pltpu.roll(o, 1, 1) * self.right[h], pltpu.roll(v, 1, 1))
                    )
                    highs.append(
                        jnp.where(
                            self.lane == 127,
                            pltpu.roll(o, 127, 1) * self.right[1 - h],
                            pltpu.roll(v, 127, 1),
                        )
                    )
                views += [lows, highs]
                coef = coefs[h]
                out = combine([stiff(h, a, x) for a in range(3)], lambda i: coef[i * 8 + x], views)
                use(h, x, out)

    def send(self, get, xs, ys):
        up = self.core == 0
        for h in range(2):
            spot = self.spot[h]
            for b in range(3):
                xs[spot, 8 * b : 8 * b + 8, :] = jnp.where(up, get(h, b, 7), get(h, b, 0))
                for x in range(8):
                    v = get(h, b, x)
                    ys[spot, 8 * b + x : 8 * b + x + 1, :] = jnp.where(up, v[7:8], v[0:1])


def at(ref):
    return lambda h, b, x: ref[h, 8 * b + x]


def given(fine, ref, which):
    return lambda h, b, x: ref[fine.spot[h], which, 8 * b + x]


def fine_first(ids, ls, first, xs, ys):
    fine = Fine(ids)
    load, stiff = given(fine, ls, 0), given(fine, ls, 1)
    for h in range(2):
        for i in range(24):
            first[h, i] = load(h, i // 8, i % 8) / stiff(h, i // 8, i % 8)
    fine.send(at(first), xs, ys)


def fine_second(ids, ls, first, halo, own, other, rest, second, xs, ys):
    fine = Fine(ids)
    load, stiff = given(fine, ls, 0), given(fine, ls, 1)

    def use(h, x, out):
        for a in range(3):
            r = load(h, a, x) - out[a]
            rest[h, 8 * a + x] = r
            second[h, 8 * a + x] = carry_coef * first[h, 8 * a + x] + fresh_coef * (r / stiff(h, a, x))

    fine.apply(at(first), halo, stiff, (own, other), use)
    fine.send(at(second), xs, ys)


def fine_down(ids, ls, first, second, rest, halo, own, other, pre, keep, send):
    fine = Fine(ids)
    stiff = given(fine, ls, 1)
    terms = [[[[] for _ in range(4)] for _ in range(3)] for _ in range(2)]
    coefs = (own, other)

    def use(h, x, out):
        r = [rest[h, 8 * a + x] - out[a] for a in range(3)]
        for b in range(3):
            t = sum(coefs[h][(63 + 3 * a + b) * 8 + x] * r[a] for a in range(3))
            terms[h][b][x // 2].append(t)
            pre[h, 8 * b + x] = first[h, 8 * b + x] + second[h, 8 * b + x]

    fine.apply(at(second), halo, stiff, coefs, use)
    pairs = (iota((24, 48), 1) // 2 == iota((24, 48), 0)).astype(F32)
    source, to = iota((128, 128), 0), iota((128, 128), 1)
    tiles = []
    for h in range(2):
        total = None
        for p in range(2):
            stacked = jnp.concatenate([sum(terms[h][b][2 * i + p]) for b in range(3) for i in range(2)], axis=0)
            part = dot(stacked, (to == 64 * p + source // 2).astype(F32))
            total = part if total is None else total + part
        tiles.append(dot(pairs, total))
    keep[...] = tiles[0]
    up = fine.core == 0
    for b in range(3):
        mine = pltpu.roll(tiles[0][8 * b : 8 * b + 8], 4, 0)
        its = tiles[1][8 * b : 8 * b + 8]
        first_rows = fine.row < 4
        send[8 * b : 8 * b + 8, :] = jnp.where(
            up, jnp.where(first_rows, mine, its), jnp.where(first_rows, its, mine)
        )


def fine_up_first(ids, ls, guess, halo, own, other, rest, first, xs, ys):
    fine = Fine(ids)
    load, stiff = given(fine, ls, 0), given(fine, ls, 1)

    def use(h, x, out):
        for a in range(3):
            r = load(h, a, x) - out[a]
            rest[h, 8 * a + x] = r
            first[h, 8 * a + x] = r / stiff(h, a, x)

    fine.apply(at(guess), halo, stiff, (own, other), use)
    fine.send(at(first), xs, ys)


def fine_up_second(ids, ls, guess, first, rest, halo, own, other, result, remain, second, xs, ys):
    fine = Fine(ids)
    stiff = given(fine, ls, 1)

    def use(h, x, out):
        for a in range(3):
            r = rest[h, 8 * a + x] - out[a]
            f = first[h, 8 * a + x]
            s = carry_coef * f + fresh_coef * (r / stiff(h, a, x))
            second[h, 8 * a + x] = s
            if h == 0:
                remain[8 * a + x] = r
                result[8 * a + x] = guess[h, 8 * a + x] + f + s

    fine.apply(at(first), halo, stiff, (own, other), use)
    fine.send(at(second), xs, ys)


def fine_last(ids, ls, second, remain, halo, own, residual):
    fine = Fine(ids)
    stiff = given(fine, ls, 1)

    def use(h, x, out):
        for a in range(3):
            residual[8 * a + x] = remain[8 * a + x] - out[a]

    fine.apply(at(second), halo, stiff, (own, None), use, halves=(0,))


def rows8():
    return iota((8, 128), 0)


def lanes8():
    return iota((8, 128), 1)


def side_views(tiles, g, width):
    row, lane = rows8(), lanes8()
    y, z = g // 2, g % 2
    views = [[], [], [], []]
    for b in range(3):
        v = tiles[g][b]
        edge = pltpu.roll(tiles[g - 2][b], 5, 0) if y > 0 else jnp.zeros_like(v)
        views[0].append(jnp.where(row % 4 == 0, edge, pltpu.roll(v, 1, 0)))
        edge = pltpu.roll(tiles[g + 2][b], 3, 0) if y < 3 else jnp.zeros_like(v)
        views[1].append(jnp.where(row % 4 == 3, edge, pltpu.roll(v, 7, 0)))
        edge = pltpu.roll(tiles[g - 1][b], 129 - width, 1) if z == 1 else jnp.zeros_like(v)
        views[2].append(jnp.where(lane % width == 0, edge, pltpu.roll(v, 1, 1)))
        edge = pltpu.roll(tiles[g + 1][b], width - 1, 1) if z == 0 else jnp.zeros_like(v)
        views[3].append(jnp.where(lane % width == width - 1, edge, pltpu.roll(v, 127, 1)))
    return views


def loaded(ref):
    return [[ref[3 * g + b] for b in range(3)] for g in range(8)]


def filled(stiff):
    return jnp.where(stiff == 0.0, 1.0, stiff)


class Middle:
    def __init__(self, packed):
        self.packed = packed

    def stiff(self, g, a):
        return self.packed[g, 63 + a]

    def stiff_edge(self, g, a):
        return filled(self.packed[g, 107 + a])

    def prolong(self, g, i):
        return self.packed[g, 66 + i]

    def coef(self, g):
        return lambda i: self.packed[g, i]

    def coef_edge(self, g):
        def get(i):
            tile = self.packed[g, 75 + i // 2]
            return pltpu.roll(tile, 64, 1) if i % 2 else tile

        return get

    def apply(self, own_ref, edge_ref, use, use_edge=None):
        row, lane = rows8(), lanes8()
        own, edge = loaded(own_ref), loaded(edge_ref)
        for g in range(8):
            swap = [pltpu.roll(v, 64, 1) for v in own[g]]
            swap_edge = [pltpu.roll(v, 64, 1) for v in edge[g]]
            turned = [pltpu.roll(v, 4, 0) for v in swap]
            low, high, low_edge, high_edge = [], [], [], []
            for b in range(3):
                low.append(jnp.where(lane >= 64, swap[b], jnp.where(row < 4, swap_edge[b], turned[b])))
                high.append(jnp.where(lane < 64, swap[b], jnp.where(row < 4, turned[b], swap_edge[b])))
                low_edge.append(jnp.where(lane >= 64, swap_edge[b], swap[b]))
                high_edge.append(jnp.where(lane >= 64, swap[b], swap_edge[b]))
            views = [own[g], low, high] + side_views(own, g, 64)
            use(g, combine([self.stiff(g, a) for a in range(3)], self.coef(g), views))
            if use_edge is not None:
                views = [edge[g], low_edge, high_edge] + side_views(edge, g, 64)
                use_edge(g, combine([self.stiff_edge(g, a) for a in range(3)], self.coef_edge(g), views))


class Coarse:
    def __init__(self, packed):
        self.packed = packed

    def stiff(self, g, a):
        return filled(self.packed[g, 63 + a])

    def prolong(self, g, i):
        return self.packed[g, 66 + i]

    def apply(self, ref, use):
        lane = lanes8()
        tiles = loaded(ref)
        for g in range(8):
            low, high = [], []
            for v in tiles[g]:
                t = pltpu.roll(v, 32, 1)
                low.append(jnp.where(lane < 32, pltpu.roll(t, 4, 0), t))
                t = pltpu.roll(v, 96, 1)
                high.append(jnp.where(lane >= 96, pltpu.roll(t, 4, 0), t))
            views = [tiles[g], low, high] + side_views(tiles, g, 32)
            use(g, combine([self.stiff(g, a) for a in range(3)], lambda i: self.packed[g, i], views))


def middle_down(ids, got, packed, load, load_edge, pre, down, first, first_edge, rest, second, second_edge):
    level = Middle(packed)
    row, lane = rows8(), lanes8()
    for g in range(8):
        y, z = g // 2, g % 2
        for b in range(3):
            n = 3 * g + b
            load[n] = got[g, 8 * b : 8 * b + 8, :]
            low = got[2 * y, 24 + 8 * b : 32 + 8 * b, :]
            high = got[2 * y + 1, 24 + 8 * b : 32 + 8 * b, :]
            if z == 0:
                high = pltpu.roll(high, 4, 0)
            else:
                low = pltpu.roll(low, 4, 0)
            load_edge[n] = jnp.where(row < 4, low, high)
            first[n] = load[n] / level.stiff(g, b)
            first_edge[n] = load_edge[n] / level.stiff_edge(g, b)

    def use(g, out):
        for a in range(3):
            n = 3 * g + a
            r = load[n] - out[a]
            rest[n] = r
            second[n] = carry_coef * first[n] + fresh_coef * (r / level.stiff(g, a))

    def use_edge(g, out):
        for a in range(3):
            n = 3 * g + a
            r = load_edge[n] - out[a]
            second_edge[n] = carry_coef * first_edge[n] + fresh_coef * (r / level.stiff_edge(g, a))

    level.apply(first, first_edge, use, use_edge)
    terms = [[], [], []]

    def use_last(g, out):
        r = [rest[3 * g + a] - out[a] for a in range(3)]
        for b in range(3):
            n = 3 * g + b
            pre[n] = first[n] + second[n]
            terms[b].append(sum(level.prolong(g, 3 * a + b) * r[a] for a in range(3)))

    level.apply(second, second_edge, use_last)
    source, to = iota((128, 128), 0), iota((128, 128), 1)
    total = None
    for b in range(3):
        pick = to == 32 * b + (source % 64) // 2
        part = dot(jnp.concatenate(terms[b], axis=0), pick.astype(F32))
        total = part if total is None else total + part
    for g in range(8):
        down[g] = total[8 * g : 8 * g + 8]


def own_lanes(y, z):
    return lanes8() // 8 == (4 * (y % 2) + rows8() % 4) * 2 + z


def coarse_down(ids, low, mid, high, packed, load, pre, send, down, first, rest, second):
    level = Coarse(packed)
    row, lane = rows8(), lanes8()
    place = lane // 32
    for g in range(8):
        under, here, over = low[g], mid[g], high[g]
        turned = [pltpu.roll(v, 4, 0) for v in (under, here, over)]

        def moved(v, b, to):
            shift = (32 * (to - b)) % 128
            return pltpu.roll(v, shift, 1) if shift else v

        for b in range(3):
            n = 3 * g + b
            top = jnp.where(place == 0, moved(under, b, 0), moved(turned[0], b, 1))
            own = jnp.where(place == 2, moved(here, b, 2), moved(turned[1], b, 3))
            bottom = jnp.where(place == 0, moved(turned[2], b, 0), moved(over, b, 1))
            tile = jnp.where(row < 4, jnp.where(place < 2, top, own), jnp.where(place < 2, bottom, 0.0))
            load[n] = tile
            first[n] = tile / level.stiff(g, b)

    def use(g, out):
        for a in range(3):
            n = 3 * g + a
            r = load[n] - out[a]
            rest[n] = r
            second[n] = carry_coef * first[n] + fresh_coef * (r / level.stiff(g, a))

    level.apply(first, use)
    terms = []

    def use_last(g, out):
        r = [rest[3 * g + a] - out[a] for a in range(3)]
        for b in range(3):
            n = 3 * g + b
            pre[n] = first[n] + second[n]
            terms.append(sum(level.prolong(g, 3 * a + b) * r[a] for a in range(3)))

    level.apply(second, use_last)
    for m in range(6):
        t = [pre[4 * m + i] for i in range(4)]
        right = jnp.where(row < 4, t[0], pltpu.roll(t[1], 4, 0))
        left = pltpu.roll(jnp.where(row < 4, t[2], pltpu.roll(t[3], 4, 0)), 64, 1)
        send[m] = jnp.where(lane >= 64, right, left)
    source, to = iota((128, 128), 0), iota((128, 128), 1)
    pick = (source >= 64) & (to % 8 == (source % 32) // 4)
    out = dot(jnp.concatenate(terms, axis=0), pick.astype(F32))
    down[...] = jnp.zeros((8, 128), F32)
    for b in range(3):
        for half in range(2):
            total = jnp.zeros((8, 128), F32)
            for g in range(4 * half, 4 * half + 4):
                n = 8 * (3 * g + b)
                total = total + jnp.where((row < 4) & own_lanes(g // 2, g % 2), out[n : n + 8], 0.0)
            down[2 * b + half : 2 * b + half + 1, :] = jnp.sum(total, axis=0, keepdims=True)


SHIFTS = ((-4, -3, -2, -1, 1, 2, 3, 4), (-8, -7, -6, -5, 5, 6, 7, 8))


def bottom_window(ids, stiff, couple, stiff_out, coefs_out):
    tiles = stiff.shape[1] // 128
    for j in range(2 * WINDOW):
        t = jnp.clip(2 * (ids[2] - REACH) + j, 0, tiles - 1)
        span = pl.ds(pl.multiple_of(t * 128, 128), 128)
        v = stiff[:, span]
        for a in range(3):
            stiff_out[a, j : j + 1, :] = v[a : a + 1]
        for k in range(7):
            for a in range(3):
                v = couple[k, a, :, span].astype(F32)
                for b in range(3):
                    coefs_out[k * 9 + a * 3 + b, j : j + 1, :] = v[b : b + 1]
    pad = ROWS - 2 * WINDOW
    for a in range(3):
        stiff_out[a, 2 * WINDOW :, :] = jnp.ones((pad, 128), F32)
    for i in range(63):
        coefs_out[i, 2 * WINDOW :, :] = jnp.zeros((pad, 128), F32)


def bottom_and_up(
    ids, got, mine, bottom_stiff, bottom_coefs, load2, low, mid, high, packed2, pre1, packed1,
    guess1, lower, upper, load, now, guess, first, rest,
):
    load[...] = jnp.zeros((3, ROWS, 128), F32)
    for b in range(3):
        load[b, 2 * REACH : 2 * REACH + 2, :] = mine[2 * b : 2 * b + 2, :]
        for s in range(2):
            for g in range(8):
                p = REACH - SHIFTS[s][g]
                load[b, 2 * p : 2 * p + 2, :] = got[g, 8 * s + 2 * b : 8 * s + 2 * b + 2, :]
    lane = iota((ROWS, 128), 1)
    row = iota((ROWS, 128), 0)
    plane = ids[2] - REACH + row // 2
    inside = (plane >= 0) & (plane < ids[3]) & (row < 2 * WINDOW)
    j, k = (row % 2) * 8 + lane // 16, lane % 16
    weights = [jnp.where(inside, damping / bottom_stiff[a], 0.0) for a in range(3)]
    for a in range(3):
        now[a] = weights[a] * load[a]

    def sweep(_, carry):
        v = [now[b] for b in range(3)]
        views = [v]
        views.append([pltpu.roll(e, 2, 0) for e in v])
        views.append([pltpu.roll(e, ROWS - 2, 0) for e in v])
        low_y, high_y = [], []
        for e in v:
            t = pltpu.roll(e, 16, 1)
            t = jnp.where(lane < 16, pltpu.roll(t, 1, 0), t)
            low_y.append(jnp.where(j == 0, 0.0, t))
            t = pltpu.roll(e, 112, 1)
            t = jnp.where(lane >= 112, pltpu.roll(t, ROWS - 1, 0), t)
            high_y.append(jnp.where(j == 15, 0.0, t))
        views += [low_y, high_y]
        views.append([jnp.where(k == 0, 0.0, pltpu.roll(e, 1, 1)) for e in v])
        views.append([jnp.where(k == 15, 0.0, pltpu.roll(e, 127, 1)) for e in v])
        out = combine([bottom_stiff[a] for a in range(3)], lambda i: bottom_coefs[i], views)
        for a in range(3):
            now[a] = v[a] + weights[a] * (load[a] - out[a])
        return carry

    lax.fori_loop(0, SWEEPS - 1, sweep, 0)

    level = Coarse(packed2)
    row, lane = rows8(), lanes8()

    def spread(b, q, half):
        r = 2 * (REACH + q) + half
        return jnp.broadcast_to(now[b, r : r + 1, :], (8, 128))

    outer, inner = [], []
    for g in range(8):
        here = own_lanes(g // 2, g % 2)
        for b in range(3):
            e = jnp.where(row < 4, spread(b, -1, g // 4), spread(b, 1, g // 4))
            outer.append(jnp.where(here, e, 0.0))
            inner.append(jnp.where(here, spread(b, 0, g // 4), 0.0))
    source, to = iota((128, 128), 0), iota((128, 128), 1)
    pick = (source % 8 == (to % 32) // 4).astype(F32)
    ups = dot(jnp.concatenate(outer + inner, axis=0), pick)
    for g in range(8):
        up = []
        for b in range(3):
            n = 8 * (3 * g + b)
            up.append(jnp.where((row < 4) & (lane >= 64), ups[192 + n : 200 + n], ups[n : n + 8]))
        for a in range(3):
            n = 3 * g + a
            m, u = n // 4, n % 4
            under, over = low[m], high[m]
            if u % 2 == 1:
                under = pltpu.roll(under, 4, 0)
            else:
                over = pltpu.roll(over, 4, 0)
            sides = jnp.where(row < 4, under, over)
            if u < 2:
                sides = pltpu.roll(sides, 64, 1)
            total = jnp.where(lane < 64, sides, jnp.where(row < 4, mid[n], 0.0))
            for b in range(3):
                total = total + level.prolong(g, 3 * a + b) * up[b]
            guess[n] = total

    def use(g, out):
        for a in range(3):
            n = 3 * g + a
            r = load2[n] - out[a]
            rest[n] = r
            first[n] = r / level.stiff(g, a)

    level.apply(guess, use)
    final = []

    def use_last(g, out):
        for a in range(3):
            n = 3 * g + a
            f = first[n]
            e = guess[n] + f + (carry_coef * f + fresh_coef * ((rest[n] - out[a]) / level.stiff(g, a)))
            under = jnp.where((lane >= 64) & (lane < 96), e, 0.0)
            over = jnp.where(lane >= 96, pltpu.roll(e, 4, 0), 0.0)
            final.append(jnp.where(row < 4, under, over))

    level.apply(first, use_last)

    pick = (source >= 64) & (source % 32 == (to % 64) // 2)
    ups = dot(jnp.concatenate(final, axis=0), pick.astype(F32))
    middle = Middle(packed1)
    for g in range(8):
        for a in range(3):
            total = pre1[3 * g + a]
            for b in range(3):
                n = 8 * (3 * g + b)
                total = total + middle.prolong(g, 3 * a + b) * ups[n : n + 8]
            guess1[3 * g + a] = total
    for m in range(12):
        s, t = guess1[2 * m], guess1[2 * m + 1]
        upper[m] = jnp.where(row < 4, pltpu.roll(s, 4, 0), t)
        lower[m] = jnp.where(row < 4, s, pltpu.roll(t, 4, 0))


def middle_up(
    ids, low, mid, high, load, load_edge, packed, pre, own, other, result, xs, ys, guess_edge, first, first_edge, rest, final
):
    fine = Fine(ids)
    level = Middle(packed)
    row = rows8()
    for n in range(24):
        under, over = low[n // 2], high[n // 2]
        if n % 2 == 1:
            under = pltpu.roll(under, 4, 0)
        else:
            over = pltpu.roll(over, 4, 0)
        guess_edge[n] = jnp.where(row < 4, under, over)

    def use(g, out):
        for a in range(3):
            n = 3 * g + a
            r = load[n] - out[a]
            rest[n] = r
            first[n] = r / level.stiff(g, a)

    def use_edge(g, out):
        for a in range(3):
            n = 3 * g + a
            first_edge[n] = (load_edge[n] - out[a]) / level.stiff_edge(g, a)

    level.apply(mid, guess_edge, use, use_edge)

    def use_last(g, out):
        for a in range(3):
            n = 3 * g + a
            f = first[n]
            e = mid[n] + f + (carry_coef * f + fresh_coef * ((rest[n] - out[a]) / level.stiff(g, a)))
            final[g, 8 * a : 8 * a + 8, :] = e

    level.apply(first, first_edge, use_last)
    rows = (iota((48, 24), 0) // 2 == iota((48, 24), 1)).astype(F32)
    source, to = iota((128, 128), 0), iota((128, 128), 1)
    for h in range(2):
        tall = dot(rows, final[2 * ids[1] + fine.spot[h]])
        ups = [dot(tall, (source == 64 * p + to // 2).astype(F32)) for p in range(2)]
        coefs0 = (own, other)[h]
        for a in range(3):
            for x in range(8):
                total = pre[h, 8 * a + x]
                for b in range(3):
                    n = 16 * b + 8 * (x // 4)
                    total = total + coefs0[(63 + 3 * a + b) * 8 + x] * ups[(x // 2) % 2][n : n + 8]
                result[h, 8 * a + x] = total
    fine.send(at(result), xs, ys)


def side_by_side(left, right):
    return jnp.concatenate([left, right], axis=1)


def pack_edges(ids, mc, ms, mp, cc, cs, cp, up, down, coarse):
    def mid(i, x):
        if i < 63:
            return mc[i // 9, i // 3 % 3, i % 3, x].astype(F32)
        return jnp.zeros((4, 64), F32)

    for t in range(32):
        up[t] = side_by_side(mid(2 * t + 1, 3), mid(2 * t, 3))
        down[t] = side_by_side(mid(2 * t, 0), mid(2 * t + 1, 0))
    for a in range(3):
        up[32 + a] = side_by_side(ms[a, 2], ms[a, 3])
        down[32 + a] = side_by_side(ms[a, 0], ms[a, 1])

    def low(i):
        if i < 63:
            got = cc[i // 9, i // 3 % 3, i % 3]
        elif i < 66:
            got = cs[i - 63]
        elif i < 75:
            got = cp[(i - 66) // 3, (i - 66) % 3]
        else:
            return [jnp.zeros((4, 32), F32)] * 2
        return [got[0].astype(F32), got[1].astype(F32)]

    for t in range(38):
        both = jnp.concatenate(low(2 * t) + low(2 * t + 1), axis=1)
        up[35 + t] = both
        down[35 + t] = both
        coarse[t] = both


def pack_levels(ids, mc, ms, mp, low, high, coarse, one, two):
    for i in range(75):
        if i < 63:
            v = [mc[i // 9, i // 3 % 3, i % 3, x].astype(F32) for x in range(4)]
        elif i < 66:
            v = [ms[i - 63, x] for x in range(4)]
        else:
            v = [mp[(i - 66) // 3, (i - 66) % 3, x] for x in range(4)]
        one[i, 0:4, :] = side_by_side(v[0], v[1])
        one[i, 4:8, :] = side_by_side(v[2], v[3])
    for t in range(35):
        one[75 + t, 0:4, :] = low[t]
        one[75 + t, 4:8, :] = high[t]
    lane = iota((4, 128), 1)
    for t in range(38):
        under, here, over = low[35 + t], coarse[t], high[35 + t]
        two[2 * t, 0:4, :] = jnp.where(lane < 64, under, pltpu.roll(here, 64, 1))
        two[2 * t, 4:8, :] = jnp.where(lane < 64, over, 0.0)
        two[2 * t + 1, 0:4, :] = jnp.where(lane < 64, pltpu.roll(under, 64, 1), here)
        two[2 * t + 1, 4:8, :] = jnp.where(lane < 64, pltpu.roll(over, 64, 1), 0.0)


VMEM = pl.BlockSpec(memory_space=pltpu.VMEM)
SMEM = pl.BlockSpec(memory_space=pltpu.SMEM)


def run(kernel, ids, ins, outs, scratch=()):
    return pl.pallas_call(
        kernel,
        out_shape=[jax.ShapeDtypeStruct(s, F32) for s in outs],
        in_specs=[SMEM] + [VMEM] * len(ins),
        out_specs=[VMEM] * len(outs),
        scratch_shapes=[pltpu.VMEM(s, F32) for s in scratch],
        compiler_params=pltpu.CompilerParams(vmem_limit_bytes=24 * 1024 * 1024),
    )(ids, *ins)


def shifted(value, axis, count, shift):
    return lax.ppermute(value, axis, [(i, i + shift) for i in range(count) if 0 <= i + shift < count])


def split_shift(value, axis, count):
    pairs = [(2 * i, 2 * i + 2) for i in range(count - 1)] + [(2 * i + 3, 2 * i + 1) for i in range(count - 1)]
    return lax.ppermute(value, (axis, "ga"), pairs)


def skewed(value, count, shifts):
    pairs = [
        (8 * i + g, 8 * (i + s) + g) for g, s in enumerate(shifts) for i in range(count) if 0 <= i + s < count
    ]
    return lax.ppermute(value, ("gx", "gy", "ga"), pairs)


def group_gather(value):
    return lax.all_to_all(jnp.broadcast_to(value[None], (8,) + value.shape), ("gy", "ga"), 0, 0)


def local(
    right_side,
    fine_stiff,
    fine_couple,
    fine_prolong,
    middle_stiff,
    middle_couple,
    middle_prolong,
    coarse_stiff,
    coarse_couple,
    coarse_prolong,
    bottom_stiff,
    bottom_couple,
):
    count = lax.axis_size("gx")
    gx, gy, ga = lax.axis_index("gx"), lax.axis_index("gy"), lax.axis_index("ga")
    ids = jnp.stack([ga, gy, gx, jnp.int32(count)]).astype(jnp.int32)

    def exchange(xs, ys):
        both = jnp.stack([split_shift(xs, "gx", count), split_shift(ys, "gy", 4)])
        return lax.all_gather(both, "ga")

    half = (2, 24, 8, 128)
    edge = (2, 24, 128)
    block = (24, 8, 128)

    raw = [middle_couple, middle_stiff, middle_prolong]
    up, down, packed = run(
        pack_edges,
        ids,
        raw + [coarse_couple, coarse_stiff, coarse_prolong],
        [(73, 4, 128), (73, 4, 128), (38, 4, 128)],
    )
    below, above = shifted(up, "gx", count, 1), shifted(down, "gx", count, -1)
    one, two = run(pack_levels, ids, raw + [below, above, packed], [(110, 8, 128), (76, 8, 128)])
    packed1 = lax.all_gather(one, ("gy", "ga"))
    packed2 = lax.all_gather(two, ("gy", "ga"))

    ls = lax.all_gather(jnp.stack([right_side.reshape(block), fine_stiff.reshape(block)]), "ga")
    own = jnp.concatenate([fine_couple.astype(F32).reshape(504, 8, 128), fine_prolong.reshape(72, 8, 128)])
    other = lax.ppermute(own, "ga", [(0, 1), (1, 0)])
    first, xs, ys = run(fine_first, ids, [ls], [half, edge, edge])
    halo = exchange(xs, ys)
    rest, second, xs, ys = run(fine_second, ids, [ls, first, halo, own, other], [half, half, edge, edge])

    bottom_s, bottom_c = run(bottom_window, ids, [bottom_stiff, bottom_couple], [(3, ROWS, 128), (63, ROWS, 128)])

    halo = exchange(xs, ys)
    pre0, keep, send = run(
        fine_down, ids, [ls, first, second, rest, halo, own, other], [half, (24, 128), (24, 128)]
    )
    got = group_gather(jnp.concatenate([keep, split_shift(send, "gx", count)]))

    tiles = (24, 8, 128)
    load1, edge1, pre1, load2 = run(
        middle_down, ids, [got, packed1], [tiles, tiles, tiles, (8, 8, 128)], [tiles] * 5
    )
    low, high = shifted(load2, "gx", count, 1), shifted(load2, "gx", count, -1)

    load2, pre2, send, mine = run(
        coarse_down, ids, [low, load2, high, packed2], [tiles, tiles, (6, 8, 128), (8, 128)], [tiles] * 3
    )
    got = group_gather(jnp.concatenate([skewed(mine, count, s) for s in SHIFTS]))
    low, high = shifted(send, "gx", count, 1), shifted(send, "gx", count, -1)

    guess1, lower, upper = run(
        bottom_and_up,
        ids,
        [got, mine, bottom_s, bottom_c, load2, low, pre2, high, packed2, pre1, packed1],
        [tiles, (12, 8, 128), (12, 8, 128)],
        [(3, ROWS, 128), (3, ROWS, 128), tiles, tiles, tiles],
    )
    low, high = shifted(upper, "gx", count, 1), shifted(lower, "gx", count, -1)

    guess, xs, ys = run(
        middle_up,
        ids,
        [low, guess1, high, load1, edge1, packed1, pre0, own, other],
        [half, edge, edge],
        [tiles] * 4 + [(8, 24, 128)],
    )

    halo = exchange(xs, ys)
    rest, first, xs, ys = run(fine_up_first, ids, [ls, guess, halo, own, other], [half, half, edge, edge])
    halo = exchange(xs, ys)
    result, remain, second, xs, ys = run(
        fine_up_second,
        ids,
        [ls, guess, first, rest, halo, own, other],
        [block, block, half, edge, edge],
    )
    halo = exchange(xs, ys)
    (residual,) = run(fine_last, ids, [ls, second, remain, halo, own], [block])
    whole = (3, 8, 8, 128)
    return result.reshape(whole), residual.reshape(whole)


def solution(mesh):
    placed = (
        P(None, "gx", "gy", "ga"),
        P(None, "gx", "gy", "ga"),
        P(None, None, None, "gx", "gy", "ga"),
        P(None, None, "gx", "gy", "ga"),
        P(None, "gx", "gy", "ga"),
        P(None, None, None, "gx", "gy", "ga"),
        P(None, None, "gx", "gy", "ga"),
        P(None, "gx", "gy", "ga"),
        P(None, None, None, "gx", "gy", "ga"),
        P(None, None, "gx", "gy", "ga"),
        P(),
        P(),
    )
    return jax.shard_map(
        local,
        mesh=mesh,
        in_specs=placed,
        out_specs=(P(None, "gx", "gy", "ga"), P(None, "gx", "gy", "ga")),
        check_vma=False,
    )
```

time: 600 us -> 224 us (0.37)
  starting transfers between devices: 360 us -> 91.4 us
  waiting for transfers between devices: 98.1 us -> 22.6 us
  local copies, waits for them, and re-layouts: 92 us -> 23.9 us
  blocking collectives: 0 us -> 49.7 us
  other arithmetic: 40.9 us -> 0.48 us
  Pallas kernels: 0 us -> 19.6 us
  between operations: 3.45 us -> 14.5 us
    ppermute x120 -> x22, starting transfers between devices: 360 us -> 83.5 us  [the longest x8 35.6 us: shifted(): lax.ppermute(value, axis, [(i, i + shift) for i in range(count) if 0 <= i...]
    ppermute x120 -> x22, waiting for transfers between devices: 98.1 us -> 16.3 us  [the longest x11 9.25 us: split_shift(): return lax.ppermute(value, (axis, 'ga'), pairs)]
    slice x107 -> x0, local copies, waits for them, and re-layouts: 50.5 us -> none  [the longest x67 45.3 us: apply_operator(): couple[direction, comp, source].astype(jnp.float32)]
    all_gather x0 -> x6, blocking collectives: none -> 37.8 us  [the longest x5 33.4 us: exchange(): return lax.all_gather(both, 'ga')]
    reshape x3 -> x0, local copies, waits for them, and re-layouts: 25.4 us -> none  [the longest x1 15.1 us: local(): grid_couple = bottom_couple.reshape((7, 3, 3) + grid_shape)]
    add x75 -> x0, other arithmetic: 22.8 us -> none  [the longest x60 20 us: apply_operator(): total + couple[direction, comp, source].astype(jnp.float32) * views[direc...]
    unnamed x135 -> x53, local copies, waits for them, and re-layouts: 2.59 us -> 23.3 us
    pallas_call x0 -> x13, Pallas kernels: none -> 19.6 us  [run(): pl.pallas_call(kernel, out_shape=[jax.ShapeDtypeStruct(s, F32) for s in o...]
  transfers between devices with their start and end apart: 120 -> 25, of which waited for: 58 -> 13; matrix products, arithmetic and copies ran while one was open for 12% -> 2% of each run, Pallas kernels for 0% -> 3%
where the time goes in v1:
time: 224 us; the launch traced here: 222 us
  starting transfers between devices  91.4 us (41%)
  blocking collectives  49.7 us (22%)
  local copies, waits for them, and re-layouts  23.9 us (11%)
  waiting for transfers between devices  22.6 us (10%)
  Pallas kernels  19.6 us (9%)
  between operations  14.5 us (6%)
    ppermute x8, starting transfers between devices, shifted(): lax.ppermute(value, axis, [(i, i + shift) for i in range(count) if 0 <= i...  35.6 us
    all_gather x5, blocking collectives, exchange(): return lax.all_gather(both, 'ga')  33.4 us
    ppermute x11, starting transfers between devices, split_shift(): return lax.ppermute(value, (axis, 'ga'), pairs)  29.6 us
    unnamed x53, local copies, waits for them, and re-layouts  23.3 us
    pallas_call x13, Pallas kernels, run(): pl.pallas_call(kernel, out_shape=[jax.ShapeDtypeStruct(s, F32) for s in o...  19.6 us
    ppermute x2, starting transfers between devices, skewed(): return lax.ppermute(value, ('gx', 'gy', 'ga'), pairs)  14.8 us
    all_to_all x1, blocking collectives, group_gather(): lax.all_to_all(jnp.broadcast_to(value[None], (8,) + value.shape), ('gy',...  11.9 us
    ppermute x11, waiting for transfers between devices, split_shift(): return lax.ppermute(value, (axis, 'ga'), pairs)  9.25 us
  transfers between devices with their start and end apart: 25, of which 13 were waited for; matrix products, arithmetic and copies ran while one was open for 2% of the time, Pallas kernels for 3%

profile of v1, /device:TPU:25, one launch (start us, length us, event | category | flops | bytes accessed | tf_op | source)
XLA Modules:
  0.0 222.1 jit_solution(4386966304130311597)
XLA Ops:
  13.0 3.7 %collective-permute-start.6 = (f32[73,4,128]{2,1,0:T(4,128)S(1)}, f32[73,4,128]{2,1,0:T(4,128)S(1)}, u32[]{:S(2)}, u32[]{:S(2)}) collective-permute-start(f32[73,4,128]{2,1,0:T(4,128)S(1)} %get-tuple-element.51), channel_id=1, source_target_pairs={{0,8},{8,16},{16,24},{24,32},{32,40},{40,48},{48,56},{56,64},{64,7... | collective-permute-start | bytes 448520 | tf_op jit(solution)/shard_map/ppermute | solution.py:688
  16.7 9.7 %collective-permute-start.7 = (f32[73,4,128]{2,1,0:T(4,128)S(1)}, f32[73,4,128]{2,1,0:T(4,128)S(1)}, u32[]{:S(2)}, u32[]{:S(2)}) collective-permute-start(f32[73,4,128]{2,1,0:T(4,128)S(1)} %get-tuple-element.52), channel_id=1, source_target_pairs={{8,0},{16,8},{24,16},{32,24},{40,32},{48,40},{56,48},{64,56},{72,6... | collective-permute-start | bytes 448520 | tf_op jit(solution)/shard_map/ppermute | solution.py:688
  31.7 3.5 %collective-permute-start.2 = (f32[576,8,128]{2,1,0:T(8,128)S(1)}, f32[576,8,128]{2,1,0:T(8,128)S(1)}, u32[]{:S(2)}, u32[]{:S(2)}) collective-permute-start(f32[576,8,128]{2,1,0:T(8,128)S(1)} %pad_maximum_fusion.own), channel_id=1, source_target_pairs={{0,1},{1,0},{2,3},{3,2},{4,5},{5,4},{6,7},{7,6},{8,9},{9,8},{10,11... | collective-permute-start | bytes 7077896 | tf_op jit(solution)/shard_map/ppermute | solution.py:747
  35.3 4.4 %all-gather = f32[4,24,8,128]{3,2,1,0:T(8,128)S(1)} all-gather(f32[2,24,8,128]{3,2,1,0:T(8,128)S(1)} %pad_maximum_fusion.1), channel_id=2, replica_groups=mesh['gx'=64,'gy'=4,'ga'=2] {'ga'}, dimensions={0}, use_global_device_ids=true | all-gather | bytes 589824 | tf_op jit(solution)/shard_map/all_gather | solution.py:745
  41.5 6.2 %collective-permute-start = (f32[2,24,128]{2,1,0:T(8,128)S(1)}, f32[2,24,128]{2,1,0:T(8,128)S(1)}, u32[]{:S(2)}, u32[]{:S(2)}) collective-permute-start(f32[2,24,128]{2,1,0:T(8,128)S(1)} %get-tuple-element.43), channel_id=1, source_target_pairs={{0,8},{8,16},{16,24},{24,32},{32,40},{40,48},{48,56},{56,64},{64,7... | collective-permute-start | bytes 73736 | tf_op jit(solution)/shard_map/ppermute | solution.py:693
  48.7 5.2 %all-gather.1 = f32[4,2,24,128]{3,2,1,0:T(8,128)S(1)} all-gather(f32[2,2,24,128]{3,2,1,0:T(8,128)S(1)} %pad_maximum_fusion.2), channel_id=3, replica_groups=mesh['gx'=64,'gy'=4,'ga'=2] {'ga'}, dimensions={0}, use_global_device_ids=true | all-gather | bytes 147456 | tf_op jit(solution)/shard_map/all_gather | solution.py:727
  56.3 3.6 %collective-permute-start.3 = (f32[2,24,128]{2,1,0:T(8,128)S(1)}, f32[2,24,128]{2,1,0:T(8,128)S(1)}, u32[]{:S(2)}, u32[]{:S(2)}) collective-permute-start(f32[2,24,128]{2,1,0:T(8,128)S(1)} %get-tuple-element.47), channel_id=1, source_target_pairs={{0,8},{8,16},{16,24},{24,32},{32,40},{40,48},{48,56},{56,64},{64,7... | collective-permute-start | bytes 73736 | tf_op jit(solution)/shard_map/ppermute | solution.py:693
  61.3 6.8 %all-gather.2 = f32[4,2,24,128]{3,2,1,0:T(8,128)S(1)} all-gather(f32[2,2,24,128]{3,2,1,0:T(8,128)S(1)} %pad_maximum_fusion.3), channel_id=4, replica_groups=mesh['gx'=64,'gy'=4,'ga'=2] {'ga'}, dimensions={0}, use_global_device_ids=true | all-gather | bytes 147456 | tf_op jit(solution)/shard_map/all_gather | solution.py:727
  69.9 1.9 collective-permute-start.5
  71.8 2.5 %collective-permute-done.5 = f32[24,128]{1,0:T(8,128)S(1)} collective-permute-done((f32[24,128]{1,0:T(8,128)S(1)}, f32[24,128]{1,0:T(8,128)S(1)}, u32[]{:S(2)}, u32[]{:S(2)}) %collective-permute-start.5) | collective-permute-done | bytes 12320 | tf_op jit(solution)/shard_map/ppermute | solution.py:693
  74.4 11.9 %all_to_all.10.got = f32[8,48,128]{2,1,0:T(8,128)S(1)} all-to-all(f32[8,48,128]{2,1,0:T(8,128)S(1)} %broadcast_in_dim.4), channel_id=1, replica_groups=mesh['gx'=64,'gy'=4,'ga'=2] {'gy','ga'}, dimensions={0} | all-to-all | bytes 393216 | tf_op jit(solution)/shard_map/all_to_all | solution.py:704
  86.3 2.2 copy-done.2
  90.1 1.9 collective-permute-start.8
  92.1 5.5 %collective-permute-start.9 = (f32[8,8,128]{2,1,0:T(8,128)S(1)}, f32[8,8,128]{2,1,0:T(8,128)S(1)}, u32[]{:S(2)}, u32[]{:S(2)}) collective-permute-start(f32[8,8,128]{2,1,0:T(8,128)S(1)} %get-tuple-element.55.mid), channel_id=1, source_target_pairs={{8,0},{16,8},{24,16},{32,24},{40,32},{48,40},{56,48},{64,56},{72,6... | collective-permute-start | bytes 98312 | tf_op jit(solution)/shard_map/ppermute | solution.py:688
  98.2 5.6 %all-gather.13.cloned.1.call-done = f32[608,8,128]{2,1,0:T(8,128)} async-done(((f32[76,8,128]{2,1,0:T(8,128)}), f32[608,8,128]{2,1,0:T(8,128)}) %all-gather.13.cloned.1.call-update) | async-done | bytes 2490384 | tf_op jit(solution)/shard_map/all_gather | solution.py:743
  108.2 12.0 %collective-permute-start.11 = (f32[8,128]{1,0:T(8,128)S(1)}, f32[8,128]{1,0:T(8,128)S(1)}, u32[]{:S(2)}, u32[]{:S(2)}) collective-permute-start(f32[8,128]{1,0:T(8,128)S(1)} %get-tuple-element.57.mine), channel_id=1, source_target_pairs={{64,0},{72,8},{80,16},{88,24},{96,32},{104,40},{112,48},{120,56},{... | collective-permute-start | bytes 12296 | tf_op jit(solution)/shard_map/ppermute | solution.py:700
  120.2 2.8 %collective-permute-start.10 = (f32[8,128]{1,0:T(8,128)S(1)}, f32[8,128]{1,0:T(8,128)S(1)}, u32[]{:S(2)}, u32[]{:S(2)}) collective-permute-start(f32[8,128]{1,0:T(8,128)S(1)} %get-tuple-element.57.mine), channel_id=1, source_target_pairs={{32,0},{40,8},{48,16},{56,24},{64,32},{72,40},{80,48},{88,56},{96,... | collective-permute-start | bytes 12296 | tf_op jit(solution)/shard_map/ppermute | solution.py:700
  123.0 3.3 %collective-permute-done.10 = f32[8,128]{1,0:T(8,128)S(1)} collective-permute-done((f32[8,128]{1,0:T(8,128)S(1)}, f32[8,128]{1,0:T(8,128)S(1)}, u32[]{:S(2)}, u32[]{:S(2)}) %collective-permute-start.10) | collective-permute-done | bytes 4128 | tf_op jit(solution)/shard_map/ppermute | solution.py:700
  126.9 7.9 %all-to-all-start.1 = ((f32[8,16,128]{2,1,0:T(8,128)}), f32[8,16,128]{2,1,0:T(8,128)S(1)}, u32[]{:S(2)}, u32[]{:S(2)}) async-start(f32[8,16,128]{2,1,0:T(8,128)} %broadcast_in_dim.5), calls=%async_computation.1 | async-start | bytes 131072 | tf_op jit(solution)/shard_map/all_to_all | solution.py:704
  134.8 2.4 %collective-permute-start.12 = (f32[6,8,128]{2,1,0:T(8,128)}, f32[6,8,128]{2,1,0:T(8,128)S(1)}, u32[]{:S(2)}, u32[]{:S(2)}) collective-permute-start(f32[6,8,128]{2,1,0:T(8,128)} %copy-done.21), channel_id=1, source_target_pairs={{0,8},{8,16},{16,24},{24,32},{32,40},{40,48},{48,56},{56,64},{64,7... | collective-permute-start | bytes 73736 | tf_op jit(solution)/shard_map/ppermute | solution.py:688
  137.2 5.1 %collective-permute-start.13 = (f32[6,8,128]{2,1,0:T(8,128)}, f32[6,8,128]{2,1,0:T(8,128)S(1)}, u32[]{:S(2)}, u32[]{:S(2)}) collective-permute-start(f32[6,8,128]{2,1,0:T(8,128)} %copy-done.21), channel_id=1, source_target_pairs={{8,0},{16,8},{24,16},{32,24},{40,32},{48,40},{56,48},{64,56},{72,6... | collective-permute-start | bytes 73736 | tf_op jit(solution)/shard_map/ppermute | solution.py:688
  142.3 3.6 %copy.15.couple = bf16[7,3,3,16384]{3,2,1,0:T(4,128)(2,1)S(1)} copy(bf16[7,3,3,16384]{3,0,2,1:T(8,128)(2,1)} %param.23) | data formatting | bytes 4128768 | tf_op args[11]
  149.4 2.0 copy-done.3
  156.0 2.9 %shard_map.139 = (f32[24,8,128]{2,1,0:T(8,128)S(1)}, f32[12,8,128]{2,1,0:T(8,128)S(1)}, f32[12,8,128]{2,1,0:T(8,128)S(1)}) custom-call(s32[4]{0:T(128)S(1)} %pad_add_fusion.ids, f32[8,16,128]{2,1,0:T(8,128)S(1)} %all-to-all-done.1.got, f32[8,128]{1,0:T(8,128)S(1)} %get-tuple-element.57.mine, f32[3,40,128]{2,1,0:T(8,128)S(1)} %copy-done.14, ...), custom_call_target="tpu_custom_call" | custom-call | tf_op jit(solution)/shard_map/pallas_call | solution.py:677
  158.9 1.9 collective-permute-start.14
  160.9 5.5 %collective-permute-start.15 = (f32[12,8,128]{2,1,0:T(8,128)S(1)}, f32[12,8,128]{2,1,0:T(8,128)S(1)}, u32[]{:S(2)}, u32[]{:S(2)}) collective-permute-start(f32[12,8,128]{2,1,0:T(8,128)S(1)} %get-tuple-element.66), channel_id=1, source_target_pairs={{8,0},{16,8},{24,16},{32,24},{40,32},{48,40},{56,48},{64,56},{72,6... | collective-permute-start | bytes 147464 | tf_op jit(solution)/shard_map/ppermute | solution.py:688
  167.5 2.1 shard_map.140
  171.0 5.8 %collective-permute-start.16 = (f32[2,24,128]{2,1,0:T(8,128)S(1)}, f32[2,24,128]{2,1,0:T(8,128)S(1)}, u32[]{:S(2)}, u32[]{:S(2)}) collective-permute-start(f32[2,24,128]{2,1,0:T(8,128)S(1)} %get-tuple-element.71), channel_id=1, source_target_pairs={{0,8},{8,16},{16,24},{24,32},{32,40},{40,48},{48,56},{56,64},{64,7... | collective-permute-start | bytes 73736 | tf_op jit(solution)/shard_map/ppermute | solution.py:693
  177.7 7.3 %all-gather.5 = f32[4,2,24,128]{3,2,1,0:T(8,128)S(1)} all-gather(f32[2,2,24,128]{3,2,1,0:T(8,128)S(1)} %pad_maximum_fusion.4), channel_id=7, replica_groups=mesh['gx'=64,'gy'=4,'ga'=2] {'ga'}, dimensions={0}, use_global_device_ids=true | all-gather | bytes 147456 | tf_op jit(solution)/shard_map/all_gather | solution.py:727
  187.4 3.6 %collective-permute-start.18 = (f32[2,24,128]{2,1,0:T(8,128)S(1)}, f32[2,24,128]{2,1,0:T(8,128)S(1)}, u32[]{:S(2)}, u32[]{:S(2)}) collective-permute-start(f32[2,24,128]{2,1,0:T(8,128)S(1)} %get-tuple-element.75), channel_id=1, source_target_pairs={{0,8},{8,16},{16,24},{24,32},{32,40},{40,48},{48,56},{56,64},{64,7... | collective-permute-start | bytes 73736 | tf_op jit(solution)/shard_map/ppermute | solution.py:693
  192.0 7.2 %all-gather.6 = f32[4,2,24,128]{3,2,1,0:T(8,128)S(1)} all-gather(f32[2,2,24,128]{3,2,1,0:T(8,128)S(1)} %pad_maximum_fusion.5), channel_id=8, replica_groups=mesh['gx'=64,'gy'=4,'ga'=2] {'ga'}, dimensions={0}, use_global_device_ids=true | all-gather | bytes 147456 | tf_op jit(solution)/shard_map/all_gather | solution.py:727
  206.9 6.9 %all-gather.7 = f32[4,2,24,128]{3,2,1,0:T(8,128)S(1)} all-gather(f32[2,2,24,128]{3,2,1,0:T(8,128)S(1)} %pad_maximum_fusion.6), channel_id=9, replica_groups=mesh['gx'=64,'gy'=4,'ga'=2] {'ga'}, dimensions={0}, use_global_device_ids=true | all-gather | bytes 147456 | tf_op jit(solution)/shard_map/all_gather | solution.py:727
  (106 shorter events, 50.8 us)
Async XLA Ops:
  7.2 79.1 %all-gather.11.cloned.1.call-start = ((), (), s32[]{:S(2)}) async-start(), calls=%async_computation.2 | async-start | bytes 4055040 | tf_op jit(solution)/shard_map/all_gather | solution.py:742
  12.2 19.1 %copy-start.22 = (bf16[7,3,3,8,8,128]{5,4,3,2,1,0:T(8,128)(2,1)S(1)}, bf16[7,3,3,8,8,128]{5,4,3,2,1,0:T(8,128)(2,1)}, u32[]{:S(2)}) copy-start(bf16[7,3,3,8,8,128]{5,4,3,2,1,0:T(8,128)(2,1)} %param.14) | copy-start | bytes 3096580
  13.0 18.6 %copy-start.23 = (f32[3,3,8,8,128]{4,3,2,1,0:T(8,128)S(1)}, f32[3,3,8,8,128]{4,3,2,1,0:T(8,128)}, u32[]{:S(2)}) copy-start(f32[3,3,8,8,128]{4,3,2,1,0:T(8,128)} %param.15) | copy-start | bytes 884740
  13.0 15.0 %collective-permute-start.6 = (f32[73,4,128]{2,1,0:T(4,128)S(1)}, f32[73,4,128]{2,1,0:T(4,128)S(1)}, u32[]{:S(2)}, u32[]{:S(2)}) collective-permute-start(f32[73,4,128]{2,1,0:T(4,128)S(1)} %get-tuple-element.51), channel_id=1, source_target_pairs={{0,8},{8,16},{16,24},{24,32},{32,40},{40,48},{48,56},{56,64},{64,7... | collective-permute-start | bytes 448520 | tf_op jit(solution)/shard_map/ppermute | solution.py:688
  16.7 12.2 %collective-permute-start.7 = (f32[73,4,128]{2,1,0:T(4,128)S(1)}, f32[73,4,128]{2,1,0:T(4,128)S(1)}, u32[]{:S(2)}, u32[]{:S(2)}) collective-permute-start(f32[73,4,128]{2,1,0:T(4,128)S(1)} %get-tuple-element.52), channel_id=1, source_target_pairs={{8,0},{16,8},{24,16},{32,24},{40,32},{48,40},{56,48},{64,56},{72,6... | collective-permute-start | bytes 448520 | tf_op jit(solution)/shard_map/ppermute | solution.py:688
  30.6 73.2 %all-gather.13.cloned.1.call-start = ((), (), s32[]{:S(2)}) async-start(), calls=%async_computation.3 | async-start | bytes 2801664 | tf_op jit(solution)/shard_map/all_gather | solution.py:743
  31.6 3.7 %copy-start.24 = (f32[3,8,8,128]{3,2,1,0:T(8,128)S(1)}, f32[3,8,8,128]{3,2,1,0:T(8,128)}, u32[]{:S(2)}) copy-start(f32[3,8,8,128]{3,2,1,0:T(8,128)} %param.13) | copy-start | bytes 294916
  31.6 3.6 %copy-start.25 = (f32[3,8,8,128]{3,2,1,0:T(8,128)S(1)}, f32[3,8,8,128]{3,2,1,0:T(8,128)}, u32[]{:S(2)}) copy-start(f32[3,8,8,128]{3,2,1,0:T(8,128)} %param.12) | copy-start | bytes 294916
  31.7 22.1 %collective-permute-start.2 = (f32[576,8,128]{2,1,0:T(8,128)S(1)}, f32[576,8,128]{2,1,0:T(8,128)S(1)}, u32[]{:S(2)}, u32[]{:S(2)}) collective-permute-start(f32[576,8,128]{2,1,0:T(8,128)S(1)} %pad_maximum_fusion.own), channel_id=1, source_target_pairs={{0,1},{1,0},{2,3},{3,2},{4,5},{5,4},{6,7},{7,6},{8,9},{9,8},{10,11... | collective-permute-start | bytes 7077896 | tf_op jit(solution)/shard_map/ppermute | solution.py:747
  40.2 7.5 %collective-permute-start.1 = (f32[2,24,128]{2,1,0:T(8,128)S(1)}, f32[2,24,128]{2,1,0:T(8,128)S(1)}, u32[]{:S(2)}, u32[]{:S(2)}) collective-permute-start(f32[2,24,128]{2,1,0:T(8,128)S(1)} %get-tuple-element.44), channel_id=1, source_target_pairs={{0,2},{2,4},{4,6},{3,1},{5,3},{7,5},{8,10},{10,12},{12,14},{11,9},... | collective-permute-start | bytes 73736 | tf_op jit(solution)/shard_map/ppermute | solution.py:693
  41.5 7.2 %collective-permute-start = (f32[2,24,128]{2,1,0:T(8,128)S(1)}, f32[2,24,128]{2,1,0:T(8,128)S(1)}, u32[]{:S(2)}, u32[]{:S(2)}) collective-permute-start(f32[2,24,128]{2,1,0:T(8,128)S(1)} %get-tuple-element.43), channel_id=1, source_target_pairs={{0,8},{8,16},{16,24},{24,32},{32,40},{40,48},{48,56},{56,64},{64,7... | collective-permute-start | bytes 73736 | tf_op jit(solution)/shard_map/ppermute | solution.py:693
  53.8 14.3 %copy-start = (f32[576,8,128]{2,1,0:T(8,128)}, f32[576,8,128]{2,1,0:T(8,128)S(1)}, u32[]{:S(2)}) copy-start(f32[576,8,128]{2,1,0:T(8,128)S(1)} %collective-permute-done.2.other) | copy-start | bytes 7077892
  55.0 5.5 %collective-permute-start.4 = (f32[2,24,128]{2,1,0:T(8,128)S(1)}, f32[2,24,128]{2,1,0:T(8,128)S(1)}, u32[]{:S(2)}, u32[]{:S(2)}) collective-permute-start(f32[2,24,128]{2,1,0:T(8,128)S(1)} %get-tuple-element.48), channel_id=1, source_target_pairs={{0,2},{2,4},{4,6},{3,1},{5,3},{7,5},{8,10},{10,12},{12,14},{11,9},... | collective-permute-start | bytes 73736 | tf_op jit(solution)/shard_map/ppermute | solution.py:693
  56.3 5.0 %collective-permute-start.3 = (f32[2,24,128]{2,1,0:T(8,128)S(1)}, f32[2,24,128]{2,1,0:T(8,128)S(1)}, u32[]{:S(2)}, u32[]{:S(2)}) collective-permute-start(f32[2,24,128]{2,1,0:T(8,128)S(1)} %get-tuple-element.47), channel_id=1, source_target_pairs={{0,8},{8,16},{16,24},{24,32},{32,40},{40,48},{48,56},{56,64},{64,7... | collective-permute-start | bytes 73736 | tf_op jit(solution)/shard_map/ppermute | solution.py:693
  69.9 4.4 %collective-permute-start.5 = (f32[24,128]{1,0:T(8,128)S(1)}, f32[24,128]{1,0:T(8,128)S(1)}, u32[]{:S(2)}, u32[]{:S(2)}) collective-permute-start(f32[24,128]{1,0:T(8,128)S(1)} %get-tuple-element.50), channel_id=1, source_target_pairs={{0,8},{8,16},{16,24},{24,32},{32,40},{40,48},{48,56},{56,64},{64,7... | collective-permute-start | bytes 36872 | tf_op jit(solution)/shard_map/ppermute | solution.py:693
  90.1 13.6 %collective-permute-start.8 = (f32[8,8,128]{2,1,0:T(8,128)S(1)}, f32[8,8,128]{2,1,0:T(8,128)S(1)}, u32[]{:S(2)}, u32[]{:S(2)}) collective-permute-start(f32[8,8,128]{2,1,0:T(8,128)S(1)} %get-tuple-element.55.mid), channel_id=1, source_target_pairs={{0,8},{8,16},{16,24},{24,32},{32,40},{40,48},{48,56},{56,64},{64,7... | collective-permute-start | bytes 98312 | tf_op jit(solution)/shard_map/ppermute | solution.py:688
  92.1 11.7 %collective-permute-start.9 = (f32[8,8,128]{2,1,0:T(8,128)S(1)}, f32[8,8,128]{2,1,0:T(8,128)S(1)}, u32[]{:S(2)}, u32[]{:S(2)}) collective-permute-start(f32[8,8,128]{2,1,0:T(8,128)S(1)} %get-tuple-element.55.mid), channel_id=1, source_target_pairs={{8,0},{16,8},{24,16},{32,24},{40,32},{48,40},{56,48},{64,56},{72,6... | collective-permute-start | bytes 98312 | tf_op jit(solution)/shard_map/ppermute | solution.py:688
  108.2 14.8 %collective-permute-start.11 = (f32[8,128]{1,0:T(8,128)S(1)}, f32[8,128]{1,0:T(8,128)S(1)}, u32[]{:S(2)}, u32[]{:S(2)}) collective-permute-start(f32[8,128]{1,0:T(8,128)S(1)} %get-tuple-element.57.mine), channel_id=1, source_target_pairs={{64,0},{72,8},{80,16},{88,24},{96,32},{104,40},{112,48},{120,56},{... | collective-permute-start | bytes 12296 | tf_op jit(solution)/shard_map/ppermute | solution.py:700
  120.2 6.1 %collective-permute-start.10 = (f32[8,128]{1,0:T(8,128)S(1)}, f32[8,128]{1,0:T(8,128)S(1)}, u32[]{:S(2)}, u32[]{:S(2)}) collective-permute-start(f32[8,128]{1,0:T(8,128)S(1)} %get-tuple-element.57.mine), channel_id=1, source_target_pairs={{32,0},{40,8},{48,16},{56,24},{64,32},{72,40},{80,48},{88,56},{96,... | collective-permute-start | bytes 12296 | tf_op jit(solution)/shard_map/ppermute | solution.py:700
  126.9 22.5 %all-to-all-start.1 = ((f32[8,16,128]{2,1,0:T(8,128)}), f32[8,16,128]{2,1,0:T(8,128)S(1)}, u32[]{:S(2)}, u32[]{:S(2)}) async-start(f32[8,16,128]{2,1,0:T(8,128)} %broadcast_in_dim.5), calls=%async_computation.1 | async-start | bytes 131072 | tf_op jit(solution)/shard_map/all_to_all | solution.py:704
  134.8 11.1 %copy-start.10 = (f32[3,16384]{1,0:T(4,128)S(1)}, f32[3,16384]{1,0:T(4,128)}, u32[]{:S(2)}) copy-start(f32[3,16384]{1,0:T(4,128)} %stiff.1) | copy-start | bytes 589828
  134.8 14.0 %collective-permute-start.12 = (f32[6,8,128]{2,1,0:T(8,128)}, f32[6,8,128]{2,1,0:T(8,128)S(1)}, u32[]{:S(2)}, u32[]{:S(2)}) collective-permute-start(f32[6,8,128]{2,1,0:T(8,128)} %copy-done.21), channel_id=1, source_target_pairs={{0,8},{8,16},{16,24},{24,32},{32,40},{40,48},{48,56},{56,64},{64,7... | collective-permute-start | bytes 73736 | tf_op jit(solution)/shard_map/ppermute | solution.py:688
  137.2 11.6 %collective-permute-start.13 = (f32[6,8,128]{2,1,0:T(8,128)}, f32[6,8,128]{2,1,0:T(8,128)S(1)}, u32[]{:S(2)}, u32[]{:S(2)}) collective-permute-start(f32[6,8,128]{2,1,0:T(8,128)} %copy-done.21), channel_id=1, source_target_pairs={{8,0},{16,8},{24,16},{32,24},{40,32},{48,40},{56,48},{64,56},{72,6... | collective-permute-start | bytes 73736 | tf_op jit(solution)/shard_map/ppermute | solution.py:688
  156.0 11.5 %copy-start.1 = (f32[576,8,128]{2,1,0:T(8,128)S(1)}, f32[576,8,128]{2,1,0:T(8,128)}, u32[]{:S(2)}) copy-start(f32[576,8,128]{2,1,0:T(8,128)} %copy-done) | copy-start | bytes 7077892
  158.9 7.4 %collective-permute-start.14 = (f32[12,8,128]{2,1,0:T(8,128)S(1)}, f32[12,8,128]{2,1,0:T(8,128)S(1)}, u32[]{:S(2)}, u32[]{:S(2)}) collective-permute-start(f32[12,8,128]{2,1,0:T(8,128)S(1)} %get-tuple-element.64), channel_id=1, source_target_pairs={{0,8},{8,16},{16,24},{24,32},{32,40},{40,48},{48,56},{56,64},{64,7... | collective-permute-start | bytes 147464 | tf_op jit(solution)/shard_map/ppermute | solution.py:688
  160.9 6.6 %collective-permute-start.15 = (f32[12,8,128]{2,1,0:T(8,128)S(1)}, f32[12,8,128]{2,1,0:T(8,128)S(1)}, u32[]{:S(2)}, u32[]{:S(2)}) collective-permute-start(f32[12,8,128]{2,1,0:T(8,128)S(1)} %get-tuple-element.66), channel_id=1, source_target_pairs={{8,0},{16,8},{24,16},{32,24},{40,32},{48,40},{56,48},{64,56},{72,6... | collective-permute-start | bytes 147464 | tf_op jit(solution)/shard_map/ppermute | solution.py:688
  169.7 7.1 %collective-permute-start.17 = (f32[2,24,128]{2,1,0:T(8,128)S(1)}, f32[2,24,128]{2,1,0:T(8,128)S(1)}, u32[]{:S(2)}, u32[]{:S(2)}) collective-permute-start(f32[2,24,128]{2,1,0:T(8,128)S(1)} %get-tuple-element.72), channel_id=1, source_target_pairs={{0,2},{2,4},{4,6},{3,1},{5,3},{7,5},{8,10},{10,12},{12,14},{11,9},... | collective-permute-start | bytes 73736 | tf_op jit(solution)/shard_map/ppermute | solution.py:693
  171.0 6.7 %collective-permute-start.16 = (f32[2,24,128]{2,1,0:T(8,128)S(1)}, f32[2,24,128]{2,1,0:T(8,128)S(1)}, u32[]{:S(2)}, u32[]{:S(2)}) collective-permute-start(f32[2,24,128]{2,1,0:T(8,128)S(1)} %get-tuple-element.71), channel_id=1, source_target_pairs={{0,8},{8,16},{16,24},{24,32},{32,40},{40,48},{48,56},{56,64},{64,7... | collective-permute-start | bytes 73736 | tf_op jit(solution)/shard_map/ppermute | solution.py:693
  186.1 5.0 %collective-permute-start.19 = (f32[2,24,128]{2,1,0:T(8,128)S(1)}, f32[2,24,128]{2,1,0:T(8,128)S(1)}, u32[]{:S(2)}, u32[]{:S(2)}) collective-permute-start(f32[2,24,128]{2,1,0:T(8,128)S(1)} %get-tuple-element.76), channel_id=1, source_target_pairs={{0,2},{2,4},{4,6},{3,1},{5,3},{7,5},{8,10},{10,12},{12,14},{11,9},... | collective-permute-start | bytes 73736 | tf_op jit(solution)/shard_map/ppermute | solution.py:693
  187.4 4.6 %collective-permute-start.18 = (f32[2,24,128]{2,1,0:T(8,128)S(1)}, f32[2,24,128]{2,1,0:T(8,128)S(1)}, u32[]{:S(2)}, u32[]{:S(2)}) collective-permute-start(f32[2,24,128]{2,1,0:T(8,128)S(1)} %get-tuple-element.75), channel_id=1, source_target_pairs={{0,8},{8,16},{16,24},{24,32},{32,40},{40,48},{48,56},{56,64},{64,7... | collective-permute-start | bytes 73736 | tf_op jit(solution)/shard_map/ppermute | solution.py:693
  201.0 4.6 %collective-permute-start.21 = (f32[2,24,128]{2,1,0:T(8,128)S(1)}, f32[2,24,128]{2,1,0:T(8,128)S(1)}, u32[]{:S(2)}, u32[]{:S(2)}) collective-permute-start(f32[2,24,128]{2,1,0:T(8,128)S(1)} %get-tuple-element.81), channel_id=1, source_target_pairs={{0,2},{2,4},{4,6},{3,1},{5,3},{7,5},{8,10},{10,12},{12,14},{11,9},... | collective-permute-start | bytes 73736 | tf_op jit(solution)/shard_map/ppermute | solution.py:693
  202.3 4.6 %collective-permute-start.20 = (f32[2,24,128]{2,1,0:T(8,128)S(1)}, f32[2,24,128]{2,1,0:T(8,128)S(1)}, u32[]{:S(2)}, u32[]{:S(2)}) collective-permute-start(f32[2,24,128]{2,1,0:T(8,128)S(1)} %get-tuple-element.80), channel_id=1, source_target_pairs={{0,8},{8,16},{16,24},{24,32},{32,40},{40,48},{48,56},{56,64},{64,7... | collective-permute-start | bytes 73736 | tf_op jit(solution)/shard_map/ppermute | solution.py:693
  (19 other events, 19.7 us)
Sparse Core Ops, SparseCore 0:
  30.7 37.0 all-gather.10
  69.9 33.7 all-gather.12

commit v2 on v1

--- a/solution.py
+++ b/solution.py
@@ -214,21 +214,31 @@
     return iota((8, 128), 1)
 
 
-def side_views(tiles, g, width):
-    row, lane = rows8(), lanes8()
-    y, z = g // 2, g % 2
-    views = [[], [], [], []]
-    for b in range(3):
-        v = tiles[g][b]
-        edge = pltpu.roll(tiles[g - 2][b], 5, 0) if y > 0 else jnp.zeros_like(v)
-        views[0].append(jnp.where(row % 4 == 0, edge, pltpu.roll(v, 1, 0)))
-        edge = pltpu.roll(tiles[g + 2][b], 3, 0) if y < 3 else jnp.zeros_like(v)
-        views[1].append(jnp.where(row % 4 == 3, edge, pltpu.roll(v, 7, 0)))
-        edge = pltpu.roll(tiles[g - 1][b], 129 - width, 1) if z == 1 else jnp.zeros_like(v)
-        views[2].append(jnp.where(lane % width == 0, edge, pltpu.roll(v, 1, 1)))
-        edge = pltpu.roll(tiles[g + 1][b], width - 1, 1) if z == 0 else jnp.zeros_like(v)
-        views[3].append(jnp.where(lane % width == width - 1, edge, pltpu.roll(v, 127, 1)))
-    return views
+class Group:
+    def __init__(self, ids, own, other):
+        self.packed = (own, other)
+        self.spot = (ids[0], 1 - ids[0])
+        right = ids[0].astype(F32)
+        self.right = (right, 1.0 - right)
+
+    def field(self, g, i):
+        return self.packed[g % 2][g // 2, i]
+
+    def sides(self, tiles, g, width):
+        row, lane = rows8(), lanes8()
+        y, h = g // 2, g % 2
+        views = [[], [], [], []]
+        for b in range(3):
+            v, o = tiles[g][b], tiles[g ^ 1][b]
+            edge = pltpu.roll(tiles[g - 2][b], 5, 0) if y > 0 else jnp.zeros_like(v)
+            views[0].append(jnp.where(row % 4 == 0, edge, pltpu.roll(v, 1, 0)))
+            edge = pltpu.roll(tiles[g + 2][b], 3, 0) if y < 3 else jnp.zeros_like(v)
+            views[1].append(jnp.where(row % 4 == 3, edge, pltpu.roll(v, 7, 0)))
+            edge = pltpu.roll(o, 129 - width, 1) * self.right[h]
+            views[2].append(jnp.where(lane % width == 0, edge, pltpu.roll(v, 1, 1)))
+            edge = pltpu.roll(o, width - 1, 1) * self.right[1 - h]
+            views[3].append(jnp.where(lane % width == width - 1, edge, pltpu.roll(v, 127, 1)))
+        return views
 
 
 def loaded(ref):
@@ -239,25 +249,22 @@
     return jnp.where(stiff == 0.0, 1.0, stiff)
 
 
-class Middle:
-    def __init__(self, packed):
-        self.packed = packed
-
+class Middle(Group):
     def stiff(self, g, a):
-        return self.packed[g, 63 + a]
+        return self.field(g, 63 + a)
 
     def stiff_edge(self, g, a):
-        return filled(self.packed[g, 107 + a])
+        return filled(self.field(g, 107 + a))
 
     def prolong(self, g, i):
-        return self.packed[g, 66 + i]
+        return self.field(g, 66 + i)
 
     def coef(self, g):
-        return lambda i: self.packed[g, i]
+        return lambda i: self.field(g, i)
 
     def coef_edge(self, g):
         def get(i):
-            tile = self.packed[g, 75 + i // 2]
+            tile = self.field(g, 75 + i // 2)
             return pltpu.roll(tile, 64, 1) if i % 2 else tile
 
         return get
@@ -275,22 +282,19 @@
                 high.append(jnp.where(lane < 64, swap[b], jnp.where(row < 4, turned[b], swap_edge[b])))
                 low_edge.append(jnp.where(lane >= 64, swap_edge[b], swap[b]))
                 high_edge.append(jnp.where(lane >= 64, swap[b], swap_edge[b]))
-            views = [own[g], low, high] + side_views(own, g, 64)
+            views = [own[g], low, high] + self.sides(own, g, 64)
             use(g, combine([self.stiff(g, a) for a in range(3)], self.coef(g), views))
             if use_edge is not None:
-                views = [edge[g], low_edge, high_edge] + side_views(edge, g, 64)
+                views = [edge[g], low_edge, high_edge] + self.sides(edge, g, 64)
                 use_edge(g, combine([self.stiff_edge(g, a) for a in range(3)], self.coef_edge(g), views))
 
 
-class Coarse:
-    def __init__(self, packed):
-        self.packed = packed
-
+class Coarse(Group):
     def stiff(self, g, a):
-        return filled(self.packed[g, 63 + a])
+        return filled(self.field(g, 63 + a))
 
     def prolong(self, g, i):
-        return self.packed[g, 66 + i]
+        return self.field(g, 66 + i)
 
     def apply(self, ref, use):
         lane = lanes8()
@@ -302,24 +306,22 @@
                 low.append(jnp.where(lane < 32, pltpu.roll(t, 4, 0), t))
                 t = pltpu.roll(v, 96, 1)
                 high.append(jnp.where(lane >= 96, pltpu.roll(t, 4, 0), t))
-            views = [tiles[g], low, high] + side_views(tiles, g, 32)
-            use(g, combine([self.stiff(g, a) for a in range(3)], lambda i: self.packed[g, i], views))
-
-
-def middle_down(ids, got, packed, load, load_edge, pre, down, first, first_edge, rest, second, second_edge):
-    level = Middle(packed)
+            views = [tiles[g], low, high] + self.sides(tiles, g, 32)
+            use(g, combine([self.stiff(g, a) for a in range(3)], lambda i: self.field(g, i), views))
+
+
+def middle_down(ids, got, packed, other, load, load_edge, pre, down, first, first_edge, rest, second, second_edge):
+    level = Middle(ids, packed, other)
     row, lane = rows8(), lanes8()
     for g in range(8):
-        y, z = g // 2, g % 2
+        y, z = g // 2, level.spot[g % 2]
         for b in range(3):
             n = 3 * g + b
-            load[n] = got[g, 8 * b : 8 * b + 8, :]
-            low = got[2 * y, 24 + 8 * b : 32 + 8 * b, :]
-            high = got[2 * y + 1, 24 + 8 * b : 32 + 8 * b, :]
-            if z == 0:
-                high = pltpu.roll(high, 4, 0)
-            else:
-                low = pltpu.roll(low, 4, 0)
+            load[n] = got[z, y, 8 * b : 8 * b + 8, :]
+            low = got[0, y, 24 + 8 * b : 32 + 8 * b, :]
+            high = got[1, y, 24 + 8 * b : 32 + 8 * b, :]
+            low = jnp.where(z == 1, pltpu.roll(low, 4, 0), low)
+            high = jnp.where(z == 0, pltpu.roll(high, 4, 0), high)
             load_edge[n] = jnp.where(row < 4, low, high)
             first[n] = load[n] / level.stiff(g, b)
             first_edge[n] = load_edge[n] / level.stiff_edge(g, b)
@@ -362,8 +364,8 @@
     return lanes8() // 8 == (4 * (y % 2) + rows8() % 4) * 2 + z
 
 
-def coarse_down(ids, low, mid, high, packed, load, pre, send, down, first, rest, second):
-    level = Coarse(packed)
+def coarse_down(ids, low, mid, high, packed, other, load, pre, send, down, first, rest, second):
+    level = Coarse(ids, packed, other)
     row, lane = rows8(), lanes8()
     place = lane // 32
     for g in range(8):
@@ -415,7 +417,7 @@
             total = jnp.zeros((8, 128), F32)
             for g in range(4 * half, 4 * half + 4):
                 n = 8 * (3 * g + b)
-                total = total + jnp.where((row < 4) & own_lanes(g // 2, g % 2), out[n : n + 8], 0.0)
+                total = total + jnp.where((row < 4) & own_lanes(g // 2, level.spot[g % 2]), out[n : n + 8], 0.0)
             down[2 * b + half : 2 * b + half + 1, :] = jnp.sum(total, axis=0, keepdims=True)
 
 
@@ -423,9 +425,9 @@
 
 
 def bottom_window(ids, stiff, couple, stiff_out, coefs_out):
-    tiles = stiff.shape[1] // 128
+    tiles = ids[3] * 2
     for j in range(2 * WINDOW):
-        t = jnp.clip(2 * (ids[2] - REACH) + j, 0, tiles - 1)
+        t = jnp.clip(2 * (ids[2] - REACH) + j, 0, tiles - 1) - ids[4]
         span = pl.ds(pl.multiple_of(t * 128, 128), 128)
         v = stiff[:, span]
         for a in range(3):
@@ -443,7 +445,7 @@
 
 
 def bottom_and_up(
-    ids, got, mine, bottom_stiff, bottom_coefs, load2, low, mid, high, packed2, pre1, packed1,
+    ids, got, mine, bottom_stiff, bottom_coefs, load2, low, mid, high, packed2, other2, pre1, packed1, other1,
     guess1, lower, upper, load, now, guess, first, rest,
 ):
     load[...] = jnp.zeros((3, ROWS, 128), F32)
@@ -452,7 +454,7 @@
         for s in range(2):
             for g in range(8):
                 p = REACH - SHIFTS[s][g]
-                load[b, 2 * p : 2 * p + 2, :] = got[g, 8 * s + 2 * b : 8 * s + 2 * b + 2, :]
+                load[b, 2 * p : 2 * p + 2, :] = got[g % 2, g // 2, 8 * s + 2 * b : 8 * s + 2 * b + 2, :]
     lane = iota((ROWS, 128), 1)
     row = iota((ROWS, 128), 0)
     plane = ids[2] - REACH + row // 2
@@ -485,7 +487,7 @@
 
     lax.fori_loop(0, SWEEPS - 1, sweep, 0)
 
-    level = Coarse(packed2)
+    level = Coarse(ids, packed2, other2)
     row, lane = rows8(), lanes8()
 
     def spread(b, q, half):
@@ -494,7 +496,7 @@
 
     outer, inner = [], []
     for g in range(8):
-        here = own_lanes(g // 2, g % 2)
+        here = own_lanes(g // 2, level.spot[g % 2])
         for b in range(3):
             e = jnp.where(row < 4, spread(b, -1, g // 4), spread(b, 1, g // 4))
             outer.append(jnp.where(here, e, 0.0))
@@ -546,7 +548,7 @@
 
     pick = (source >= 64) & (source % 32 == (to % 64) // 2)
     ups = dot(jnp.concatenate(final, axis=0), pick.astype(F32))
-    middle = Middle(packed1)
+    middle = Middle(ids, packed1, other1)
     for g in range(8):
         for a in range(3):
             total = pre1[3 * g + a]
@@ -561,10 +563,10 @@
 
 
 def middle_up(
-    ids, low, mid, high, load, load_edge, packed, pre, own, other, result, xs, ys, guess_edge, first, first_edge, rest, final
+    ids, low, mid, high, load, load_edge, packed, packed_other, pre, own, other, result, xs, ys, guess_edge, first, first_edge, rest, final
 ):
     fine = Fine(ids)
-    level = Middle(packed)
+    level = Middle(ids, packed, packed_other)
     row = rows8()
     for n in range(24):
         under, over = low[n // 2], high[n // 2]
@@ -599,7 +601,7 @@
     rows = (iota((48, 24), 0) // 2 == iota((48, 24), 1)).astype(F32)
     source, to = iota((128, 128), 0), iota((128, 128), 1)
     for h in range(2):
-        tall = dot(rows, final[2 * ids[1] + fine.spot[h]])
+        tall = dot(rows, final[2 * ids[1] + h])
         ups = [dot(tall, (source == 64 * p + to // 2).astype(F32)) for p in range(2)]
         coefs0 = (own, other)[h]
         for a in range(3):
@@ -680,7 +682,7 @@
         in_specs=[SMEM] + [VMEM] * len(ins),
         out_specs=[VMEM] * len(outs),
         scratch_shapes=[pltpu.VMEM(s, F32) for s in scratch],
-        compiler_params=pltpu.CompilerParams(vmem_limit_bytes=24 * 1024 * 1024),
+        compiler_params=pltpu.CompilerParams(vmem_limit_bytes=8 * 1024 * 1024),
     )(ids, *ins)
 
 
@@ -701,7 +703,9 @@
 
 
 def group_gather(value):
-    return lax.all_to_all(jnp.broadcast_to(value[None], (8,) + value.shape), ("gy", "ga"), 0, 0)
+    pair = lax.all_gather(value, "gy", axis_index_groups=[[0, 1], [2, 3]])
+    four = lax.all_gather(pair, "gy", axis_index_groups=[[0, 2], [1, 3]])
+    return lax.all_gather(four.reshape((4,) + value.shape), "ga")
 
 
 def local(
@@ -720,7 +724,9 @@
 ):
     count = lax.axis_size("gx")
     gx, gy, ga = lax.axis_index("gx"), lax.axis_index("gy"), lax.axis_index("ga")
-    ids = jnp.stack([ga, gy, gx, jnp.int32(count)]).astype(jnp.int32)
+    span = min(WINDOW, count)
+    start = 2 * jnp.clip(gx - REACH, 0, count - span)
+    ids = jnp.stack([ga, gy, gx, jnp.int32(count), start]).astype(jnp.int32)
 
     def exchange(xs, ys):
         both = jnp.stack([split_shift(xs, "gx", count), split_shift(ys, "gy", 4)])
@@ -738,18 +744,24 @@
         [(73, 4, 128), (73, 4, 128), (38, 4, 128)],
     )
     below, above = shifted(up, "gx", count, 1), shifted(down, "gx", count, -1)
-    one, two = run(pack_levels, ids, raw + [below, above, packed], [(110, 8, 128), (76, 8, 128)])
-    packed1 = lax.all_gather(one, ("gy", "ga"))
-    packed2 = lax.all_gather(two, ("gy", "ga"))
 
     ls = lax.all_gather(jnp.stack([right_side.reshape(block), fine_stiff.reshape(block)]), "ga")
     own = jnp.concatenate([fine_couple.astype(F32).reshape(504, 8, 128), fine_prolong.reshape(72, 8, 128)])
     other = lax.ppermute(own, "ga", [(0, 1), (1, 0)])
     first, xs, ys = run(fine_first, ids, [ls], [half, edge, edge])
+    below, above, _ = lax.optimization_barrier((below, above, xs))
+    one, two = run(pack_levels, ids, raw + [below, above, packed], [(110, 8, 128), (76, 8, 128)])
+    swap = [(0, 1), (1, 0)]
+    packed1 = lax.all_gather(one, "gy")
+    packed2 = lax.all_gather(two, "gy")
+    other1 = lax.ppermute(packed1, "ga", swap)
+    other2 = lax.ppermute(packed2, "ga", swap)
     halo = exchange(xs, ys)
     rest, second, xs, ys = run(fine_second, ids, [ls, first, halo, own, other], [half, half, edge, edge])
 
-    bottom_s, bottom_c = run(bottom_window, ids, [bottom_stiff, bottom_couple], [(3, ROWS, 128), (63, ROWS, 128)])
+    cut = lax.dynamic_slice_in_dim(bottom_stiff, start * 128, span * 256, 1)
+    cut_couple = lax.dynamic_slice_in_dim(bottom_couple, start * 128, span * 256, 3)
+    bottom_s, bottom_c = run(bottom_window, ids, [cut, cut_couple], [(3, ROWS, 128), (63, ROWS, 128)])
 
     halo = exchange(xs, ys)
     pre0, keep, send = run(
@@ -759,12 +771,12 @@
 
     tiles = (24, 8, 128)
     load1, edge1, pre1, load2 = run(
-        middle_down, ids, [got, packed1], [tiles, tiles, tiles, (8, 8, 128)], [tiles] * 5
+        middle_down, ids, [got, packed1, other1], [tiles, tiles, tiles, (8, 8, 128)], [tiles] * 5
     )
     low, high = shifted(load2, "gx", count, 1), shifted(load2, "gx", count, -1)
 
     load2, pre2, send, mine = run(
-        coarse_down, ids, [low, load2, high, packed2], [tiles, tiles, (6, 8, 128), (8, 128)], [tiles] * 3
+        coarse_down, ids, [low, load2, high, packed2, other2], [tiles, tiles, (6, 8, 128), (8, 128)], [tiles] * 3
     )
     got = group_gather(jnp.concatenate([skewed(mine, count, s) for s in SHIFTS]))
     low, high = shifted(send, "gx", count, 1), shifted(send, "gx", count, -1)
@@ -772,7 +784,7 @@
     guess1, lower, upper = run(
         bottom_and_up,
         ids,
-        [got, mine, bottom_s, bottom_c, load2, low, pre2, high, packed2, pre1, packed1],
+        [got, mine, bottom_s, bottom_c, load2, low, pre2, high, packed2, other2, pre1, packed1, other1],
         [tiles, (12, 8, 128), (12, 8, 128)],
         [(3, ROWS, 128), (3, ROWS, 128), tiles, tiles, tiles],
     )
@@ -781,7 +793,7 @@
     guess, xs, ys = run(
         middle_up,
         ids,
-        [low, guess1, high, load1, edge1, packed1, pre0, own, other],
+        [low, guess1, high, load1, edge1, packed1, other1, pre0, own, other],
         [half, edge, edge],
         [tiles] * 4 + [(8, 24, 128)],
     )

time: 224 us -> 274 us (1.22)
  waiting for transfers between devices: 22.6 us -> 80.9 us
  local copies, waits for them, and re-layouts: 23.9 us -> 9.55 us
  Pallas kernels: 19.6 us -> 33.8 us
  starting transfers between devices: 91.4 us -> 84.3 us
  blocking collectives: 49.7 us -> 45 us
  other arithmetic: 0.48 us -> 3.91 us
    all_gather x2, waiting for transfers between devices: 5.58 us -> 59.4 us  [the longest x1 30.8 us: local(): packed2 = lax.all_gather(two, 'gy')]
    all_gather x0 -> x6, blocking collectives: none -> 31.1 us  [the longest x2 13.5 us: group_gather(): return lax.all_gather(four.reshape((4,) + value.shape), 'ga')]
    all_gather x5, blocking collectives: 33.4 us -> 11.3 us  [exchange(): return lax.all_gather(both, 'ga')]
    unnamed x53 -> x29, local copies, waits for them, and re-layouts: 23.3 us -> 8.51 us
    pallas_call x13, Pallas kernels: 19.6 us -> 33.8 us  [run(): pl.pallas_call(kernel, out_shape=[jax.ShapeDtypeStruct(s, F32) for s in o...]
    all_to_all x1 -> x0, blocking collectives: 11.9 us -> none  [group_gather(): lax.all_to_all(jnp.broadcast_to(value[None], (8,) + value.shape), ('gy',...]
    all_to_all x1 -> x0, starting transfers between devices: 7.86 us -> none  [group_gather(): lax.all_to_all(jnp.broadcast_to(value[None], (8,) + value.shape), ('gy',...]
    ppermute x11, waiting for transfers between devices: 9.25 us -> 16.8 us  [split_shift(): return lax.ppermute(value, (axis, 'ga'), pairs)]
  transfers between devices with their start and end apart: 25 -> 26, of which waited for: 13 -> 10; matrix products, arithmetic and copies ran while one was open for 2% -> 2% of each run, Pallas kernels for 3% -> 4%
where the time goes in v2:
time: 274 us; the launch traced here: 272 us
  starting transfers between devices  84.3 us (31%)
  waiting for transfers between devices  80.9 us (30%)
  blocking collectives  45 us (16%)
  Pallas kernels  33.8 us (12%)
  between operations  14.5 us (5%)
  local copies, waits for them, and re-layouts  9.55 us (3%)
  other arithmetic  3.91 us (1%)
    pallas_call x13, Pallas kernels, run(): pl.pallas_call(kernel, out_shape=[jax.ShapeDtypeStruct(s, F32) for s in o...  33.8 us
    ppermute x11, starting transfers between devices, split_shift(): return lax.ppermute(value, (axis, 'ga'), pairs)  33.3 us
    ppermute x8, starting transfers between devices, shifted(): lax.ppermute(value, axis, [(i, i + shift) for i in range(count) if 0 <= i...  32.4 us
    all_gather x1, waiting for transfers between devices, local(): packed2 = lax.all_gather(two, 'gy')  30.8 us
    all_gather x1, waiting for transfers between devices, local(): packed1 = lax.all_gather(one, 'gy')  28.6 us
    ppermute x11, waiting for transfers between devices, split_shift(): return lax.ppermute(value, (axis, 'ga'), pairs)  16.8 us
    all_gather x2, blocking collectives, group_gather(): return lax.all_gather(four.reshape((4,) + value.shape), 'ga')  13.5 us
    all_gather x5, blocking collectives, exchange(): return lax.all_gather(both, 'ga')  11.3 us
  transfers between devices with their start and end apart: 26, of which 10 were waited for; matrix products, arithmetic and copies ran while one was open for 2% of the time, Pallas kernels for 4%

profile of v2, /device:TPU:25, one launch (start us, length us, event | category | flops | bytes accessed | tf_op | source)
XLA Modules:
  0.0 272.1 jit_solution(12049257101186166638)
XLA Ops:
  13.1 3.5 %collective-permute-start.6 = (f32[73,4,128]{2,1,0:T(4,128)S(1)}, f32[73,4,128]{2,1,0:T(4,128)S(1)}, u32[]{:S(2)}, u32[]{:S(2)}) collective-permute-start(f32[73,4,128]{2,1,0:T(4,128)S(1)} %get-tuple-element.53), channel_id=1, source_target_pairs={{0,8},{8,16},{16,24},{24,32},{32,40},{40,48},{48,56},{56,64},{64,7... | collective-permute-start | bytes 448520 | tf_op jit(solution)/shard_map/ppermute | solution.py:690
  16.7 9.7 %collective-permute-start.7 = (f32[73,4,128]{2,1,0:T(4,128)S(1)}, f32[73,4,128]{2,1,0:T(4,128)S(1)}, u32[]{:S(2)}, u32[]{:S(2)}) collective-permute-start(f32[73,4,128]{2,1,0:T(4,128)S(1)} %get-tuple-element.54), channel_id=1, source_target_pairs={{8,0},{16,8},{24,16},{32,24},{40,32},{48,40},{56,48},{64,56},{72,6... | collective-permute-start | bytes 448520 | tf_op jit(solution)/shard_map/ppermute | solution.py:690
  39.2 28.6 %all-gather.17.cloned.1.call-done = f32[440,8,128]{2,1,0:T(8,128)} async-done(((f32[110,8,128]{2,1,0:T(8,128)}), f32[440,8,128]{2,1,0:T(8,128)}) %all-gather.17.cloned.1.call-update) | async-done | bytes 1802256 | tf_op jit(solution)/shard_map/all_gather | solution.py:755
  70.4 30.8 %all-gather.19.cloned.1.call-done = f32[304,8,128]{2,1,0:T(8,128)} async-done(((f32[76,8,128]{2,1,0:T(8,128)}), f32[304,8,128]{2,1,0:T(8,128)}) %all-gather.19.cloned.1.call-update) | async-done | bytes 1245200 | tf_op jit(solution)/shard_map/all_gather | solution.py:756
  101.2 3.6 %collective-permute-start.11 = (f32[4,76,8,128]{3,2,1,0:T(8,128)}, f32[4,76,8,128]{3,2,1,0:T(8,128)}, u32[]{:S(2)}, u32[]{:S(2)}) collective-permute-start(f32[4,76,8,128]{3,2,1,0:T(8,128)} %bitcast.44), channel_id=1, source_target_pairs={{0,1},{1,0},{2,3},{3,2},{4,5},{5,4},{6,7},{7,6},{8,9},{9,8},{10,11... | collective-permute-start | bytes 3735560 | tf_op jit(solution)/shard_map/ppermute | solution.py:758
  106.2 5.9 %collective-permute-start = (f32[2,24,128]{2,1,0:T(8,128)S(1)}, f32[2,24,128]{2,1,0:T(8,128)S(1)}, u32[]{:S(2)}, u32[]{:S(2)}) collective-permute-start(f32[2,24,128]{2,1,0:T(8,128)S(1)} %get-tuple-element.45), channel_id=1, source_target_pairs={{0,8},{8,16},{16,24},{24,32},{32,40},{40,48},{48,56},{56,64},{64,7... | collective-permute-start | bytes 73736 | tf_op jit(solution)/shard_map/ppermute | solution.py:695
  113.1 3.9 %all-gather.1 = f32[4,2,24,128]{3,2,1,0:T(8,128)S(1)} all-gather(f32[2,2,24,128]{3,2,1,0:T(8,128)S(1)} %pad_maximum_fusion.2), channel_id=3, replica_groups=mesh['gx'=64,'gy'=4,'ga'=2] {'ga'}, dimensions={0}, use_global_device_ids=true | all-gather | bytes 147456 | tf_op jit(solution)/shard_map/all_gather | solution.py:733
  116.9 3.1 %shard_map.132 = (f32[2,24,8,128]{3,2,1,0:T(8,128)S(1)}, f32[2,24,8,128]{3,2,1,0:T(8,128)S(1)}, f32[2,24,128]{2,1,0:T(8,128)S(1)}, f32[2,24,128]{2,1,0:T(8,128)S(1)}) custom-call(s32[5]{0:T(128)S(1)} %stack.67.ids, f32[2,2,24,8,128]{4,3,2,1,0:T(8,128)S(1)} %bitcast.35, f32[2,24,8,128]{3,2,1,0:T(8,128)S(1)} %get-tuple-element.44.first, ...), custom_call_target="tpu_custom_call" | custom-call | tf_op jit(solution)/shard_map/pallas_call | solution.py:679
  120.0 3.8 %collective-permute-start.3 = (f32[2,24,128]{2,1,0:T(8,128)S(1)}, f32[2,24,128]{2,1,0:T(8,128)S(1)}, u32[]{:S(2)}, u32[]{:S(2)}) collective-permute-start(f32[2,24,128]{2,1,0:T(8,128)S(1)} %get-tuple-element.49), channel_id=1, source_target_pairs={{0,8},{8,16},{16,24},{24,32},{32,40},{40,48},{48,56},{56,64},{64,7... | collective-permute-start | bytes 73736 | tf_op jit(solution)/shard_map/ppermute | solution.py:695
  125.1 3.9 %collective-permute-done.4 = f32[2,24,128]{2,1,0:T(8,128)S(1)} collective-permute-done((f32[2,24,128]{2,1,0:T(8,128)S(1)}, f32[2,24,128]{2,1,0:T(8,128)S(1)}, u32[]{:S(2)}, u32[]{:S(2)}) %collective-permute-start.4) | collective-permute-done | bytes 24608 | tf_op jit(solution)/shard_map/ppermute | solution.py:695
  130.8 3.7 %shard_map.133 = (f32[2,24,8,128]{3,2,1,0:T(8,128)S(1)}, f32[24,128]{1,0:T(8,128)S(1)}, f32[24,128]{1,0:T(8,128)S(1)}) custom-call(s32[5]{0:T(128)S(1)} %stack.67.ids, f32[2,2,24,8,128]{4,3,2,1,0:T(8,128)S(1)} %bitcast.36, f32[2,24,8,128]{3,2,1,0:T(8,128)S(1)} %get-tuple-element.44.first, f32[2,24,8,128]{3,2,1,0:T(8,128)S(1)} %get-tuple-element.47.second, ...), custom_call_target="tpu_custom_call" | custom-call | tf_op jit(solution)/shard_map/pallas_call | solution.py:679
  134.5 3.8 %collective-permute-start.5 = (f32[24,128]{1,0:T(8,128)S(1)}, f32[24,128]{1,0:T(8,128)S(1)}, u32[]{:S(2)}, u32[]{:S(2)}) collective-permute-start(f32[24,128]{1,0:T(8,128)S(1)} %get-tuple-element.52), channel_id=1, source_target_pairs={{0,8},{8,16},{16,24},{24,32},{32,40},{40,48},{48,56},{56,64},{64,7... | collective-permute-start | bytes 36872 | tf_op jit(solution)/shard_map/ppermute | solution.py:695
  139.1 3.9 %all-gather.3 = f32[96,128]{1,0:T(8,128)S(1)} all-gather(f32[48,128]{1,0:T(8,128)S(1)} %pad_maximum_fusion.7), channel_id=5, replica_groups={{0,2},{4,6},{1,3},{5,7},{8,10},{12,14},{9,11},{13,15},{16,18},{20,22},{..., dimensions={0}, use_global_device_ids=true | all-gather | bytes 73728 | tf_op jit(solution)/shard_map/all_gather | solution.py:706
  143.0 5.1 %all-gather.4 = f32[4,48,128]{2,1,0:T(8,128)S(1)} all-gather(f32[2,48,128]{2,1,0:T(8,128)S(1)} %bitcast.55), channel_id=6, replica_groups={{0,4},{2,6},{1,5},{3,7},{8,12},{10,14},{9,13},{11,15},{16,20},{18,22},{..., dimensions={0}, use_global_device_ids=true | all-gather | bytes 147456 | tf_op jit(solution)/shard_map/all_gather | solution.py:707
  148.1 6.6 %all-gather.12 = f32[8,48,128]{2,1,0:T(8,128)S(1)} all-gather(f32[4,48,128]{2,1,0:T(8,128)S(1)} %all-gather.4), channel_id=14, replica_groups=mesh['gx'=64,'gy'=4,'ga'=2] {'ga'}, dimensions={0}, use_global_device_ids=true | all-gather | bytes 294912 | tf_op jit(solution)/shard_map/all_gather | solution.py:708
  161.1 3.1 %collective-permute-start.9 = (f32[8,8,128]{2,1,0:T(8,128)S(1)}, f32[8,8,128]{2,1,0:T(8,128)S(1)}, u32[]{:S(2)}, u32[]{:S(2)}) collective-permute-start(f32[8,8,128]{2,1,0:T(8,128)S(1)} %get-tuple-element.59.mid), channel_id=1, source_target_pairs={{0,8},{8,16},{16,24},{24,32},{32,40},{40,48},{48,56},{56,64},{64,7... | collective-permute-start | bytes 98312 | tf_op jit(solution)/shard_map/ppermute | solution.py:690
  164.3 3.5 %collective-permute-done.9.low = f32[8,8,128]{2,1,0:T(8,128)S(1)} collective-permute-done((f32[8,8,128]{2,1,0:T(8,128)S(1)}, f32[8,8,128]{2,1,0:T(8,128)S(1)}, u32[]{:S(2)}, u32[]{:S(2)}) %collective-permute-start.9) | collective-permute-done | bytes 32800 | tf_op jit(solution)/shard_map/ppermute | solution.py:690
  170.0 7.5 %collective-permute-start.13 = (f32[8,128]{1,0:T(8,128)S(1)}, f32[8,128]{1,0:T(8,128)S(1)}, u32[]{:S(2)}, u32[]{:S(2)}) collective-permute-start(f32[8,128]{1,0:T(8,128)S(1)} %get-tuple-element.61.mine), channel_id=1, source_target_pairs={{64,0},{72,8},{80,16},{88,24},{96,32},{104,40},{112,48},{120,56},{... | collective-permute-start | bytes 12296 | tf_op jit(solution)/shard_map/ppermute | solution.py:702
  182.3 4.0 %collective-permute-start.15 = (f32[6,8,128]{2,1,0:T(8,128)S(1)}, f32[6,8,128]{2,1,0:T(8,128)S(1)}, u32[]{:S(2)}, u32[]{:S(2)}) collective-permute-start(f32[6,8,128]{2,1,0:T(8,128)S(1)} %get-tuple-element.65), channel_id=1, source_target_pairs={{8,0},{16,8},{24,16},{32,24},{40,32},{48,40},{56,48},{64,56},{72,6... | collective-permute-start | bytes 73736 | tf_op jit(solution)/shard_map/ppermute | solution.py:690
  188.9 3.2 %all-gather.7 = f32[32,128]{1,0:T(8,128)S(1)} all-gather(f32[16,128]{1,0:T(8,128)S(1)} %pad_maximum_fusion.8), channel_id=9, replica_groups={{0,2},{4,6},{1,3},{5,7},{8,10},{12,14},{9,11},{13,15},{16,18},{20,22},{..., dimensions={0}, use_global_device_ids=true | all-gather | bytes 24576 | tf_op jit(solution)/shard_map/all_gather | solution.py:706
  192.1 5.3 %all-gather.8 = f32[4,16,128]{2,1,0:T(8,128)S(1)} all-gather(f32[2,16,128]{2,1,0:T(8,128)S(1)} %bitcast.59), channel_id=10, replica_groups={{0,4},{2,6},{1,5},{3,7},{8,12},{10,14},{9,13},{11,15},{16,20},{18,22},{..., dimensions={0}, use_global_device_ids=true | all-gather | bytes 49152 | tf_op jit(solution)/shard_map/all_gather | solution.py:707
  197.4 7.0 %all-gather.13 = f32[8,16,128]{2,1,0:T(8,128)S(1)} all-gather(f32[4,16,128]{2,1,0:T(8,128)S(1)} %all-gather.8), channel_id=15, replica_groups=mesh['gx'=64,'gy'=4,'ga'=2] {'ga'}, dimensions={0}, use_global_device_ids=true | all-gather | bytes 98304 | tf_op jit(solution)/shard_map/all_gather | solution.py:708
  204.4 4.3 %shard_map.139 = (f32[24,8,128]{2,1,0:T(8,128)S(1)}, f32[12,8,128]{2,1,0:T(8,128)S(1)}, f32[12,8,128]{2,1,0:T(8,128)S(1)}) custom-call(s32[5]{0:T(128)S(1)} %stack.67.ids, f32[2,4,16,128]{3,2,1,0:T(8,128)S(1)} %bitcast.53, f32[8,128]{1,0:T(8,128)S(1)} %get-tuple-element.61.mine, f32[3,40,128]{2,1,0:T(8,128)S(1)} %get-tuple-element.62.bottom_stiff, ...), custom_call_target="tpu_custom_call" | custom-call | tf_op jit(solution)/shard_map/pallas_call | solution.py:679
  210.6 5.5 %collective-permute-start.17 = (f32[12,8,128]{2,1,0:T(8,128)S(1)}, f32[12,8,128]{2,1,0:T(8,128)S(1)}, u32[]{:S(2)}, u32[]{:S(2)}) collective-permute-start(f32[12,8,128]{2,1,0:T(8,128)S(1)} %get-tuple-element.70), channel_id=1, source_target_pairs={{8,0},{16,8},{24,16},{32,24},{40,32},{48,40},{56,48},{64,56},{72,6... | collective-permute-start | bytes 147464 | tf_op jit(solution)/shard_map/ppermute | solution.py:690
  217.3 4.6 %shard_map.140 = (f32[2,24,8,128]{3,2,1,0:T(8,128)S(1)}, f32[2,24,128]{2,1,0:T(8,128)S(1)}, f32[2,24,128]{2,1,0:T(8,128)S(1)}) custom-call(s32[5]{0:T(128)S(1)} %stack.67.ids, f32[12,8,128]{2,1,0:T(8,128)S(1)} %collective-permute-done.16.low, f32[24,8,128]{2,1,0:T(8,128)S(1)} %get-tuple-element.69.mid, f32[12,8,128]{2,1,0:T(8,128)S(1)} %collective-permute-done.17.high, ...), custom_call_target="tpu_custom_call" | custom-call | tf_op jit(solution)/shard_map/pallas_call | solution.py:679
  221.9 5.8 %collective-permute-start.18 = (f32[2,24,128]{2,1,0:T(8,128)S(1)}, f32[2,24,128]{2,1,0:T(8,128)S(1)}, u32[]{:S(2)}, u32[]{:S(2)}) collective-permute-start(f32[2,24,128]{2,1,0:T(8,128)S(1)} %get-tuple-element.75), channel_id=1, source_target_pairs={{0,8},{8,16},{16,24},{24,32},{32,40},{40,48},{48,56},{56,64},{64,7... | collective-permute-start | bytes 73736 | tf_op jit(solution)/shard_map/ppermute | solution.py:695
  229.0 3.6 %collective-permute-done.19 = f32[2,24,128]{2,1,0:T(8,128)S(1)} collective-permute-done((f32[2,24,128]{2,1,0:T(8,128)S(1)}, f32[2,24,128]{2,1,0:T(8,128)S(1)}, u32[]{:S(2)}, u32[]{:S(2)}) %collective-permute-start.19) | collective-permute-done | bytes 24608 | tf_op jit(solution)/shard_map/ppermute | solution.py:695
  237.5 3.9 %collective-permute-start.20 = (f32[2,24,128]{2,1,0:T(8,128)S(1)}, f32[2,24,128]{2,1,0:T(8,128)S(1)}, u32[]{:S(2)}, u32[]{:S(2)}) collective-permute-start(f32[2,24,128]{2,1,0:T(8,128)S(1)} %get-tuple-element.79), channel_id=1, source_target_pairs={{0,8},{8,16},{16,24},{24,32},{32,40},{40,48},{48,56},{56,64},{64,7... | collective-permute-start | bytes 73736 | tf_op jit(solution)/shard_map/ppermute | solution.py:695
  242.7 3.8 %collective-permute-done.21 = f32[2,24,128]{2,1,0:T(8,128)S(1)} collective-permute-done((f32[2,24,128]{2,1,0:T(8,128)S(1)}, f32[2,24,128]{2,1,0:T(8,128)S(1)}, u32[]{:S(2)}, u32[]{:S(2)}) %collective-permute-start.21) | collective-permute-done | bytes 24608 | tf_op jit(solution)/shard_map/ppermute | solution.py:695
  248.4 3.7 %shard_map.142 = (f32[24,8,128]{2,1,0:T(8,128)}, f32[24,8,128]{2,1,0:T(8,128)S(1)}, f32[2,24,8,128]{3,2,1,0:T(8,128)S(1)}, f32[2,24,128]{2,1,0:T(8,128)S(1)}, f32[2,24,128]{2,1,0:T(8,128)S(1)}) custom-call(s32[5]{0:T(128)S(1)} %stack.67.ids, f32[2,2,24,8,128]{4,3,2,1,0:T(8,128)S(1)} %bitcast.38, f32[2,24,8,128]{3,2,1,0:T(8,128)S(1)} %get-tuple-element.74.guess, ...), custom_call_target="tpu_custom_call" | custom-call | tf_op jit(solution)/shard_map/pallas_call | solution.py:679
  252.1 3.6 %collective-permute-start.22 = (f32[2,24,128]{2,1,0:T(8,128)S(1)}, f32[2,24,128]{2,1,0:T(8,128)S(1)}, u32[]{:S(2)}, u32[]{:S(2)}) collective-permute-start(f32[2,24,128]{2,1,0:T(8,128)S(1)} %get-tuple-element.84), channel_id=1, source_target_pairs={{0,8},{8,16},{16,24},{24,32},{32,40},{40,48},{48,56},{56,64},{64,7... | collective-permute-start | bytes 73736 | tf_op jit(solution)/shard_map/ppermute | solution.py:695
  257.0 3.8 %collective-permute-done.23 = f32[2,24,128]{2,1,0:T(8,128)S(1)} collective-permute-done((f32[2,24,128]{2,1,0:T(8,128)S(1)}, f32[2,24,128]{2,1,0:T(8,128)S(1)}, u32[]{:S(2)}, u32[]{:S(2)}) %collective-permute-start.23) | collective-permute-done | bytes 24608 | tf_op jit(solution)/shard_map/ppermute | solution.py:695
  (89 shorter events, 61.5 us)
Async XLA Ops:
  7.2 157.1 %copy-start = (bf16[7,3,3,16384]{3,0,2,1:T(8,128)(2,1)S(1)}, bf16[7,3,3,16384]{3,0,2,1:T(8,128)(2,1)}, u32[]{:S(2)}) copy-start(bf16[7,3,3,16384]{3,0,2,1:T(8,128)(2,1)} %param.23) | copy-start | bytes 6193156
  7.2 60.6 %all-gather.17.cloned.1.call-start = ((), (), s32[]{:S(2)}) async-start(), calls=%async_computation | async-start | bytes 2252800 | tf_op jit(solution)/shard_map/all_gather | solution.py:755
  12.4 18.2 %copy-start.5 = (bf16[7,3,3,4,4,64]{5,4,3,2,1,0:T(4,128)(2,1)S(1)}, bf16[7,3,3,4,4,64]{5,4,3,2,1,0:T(4,128)(2,1)}, u32[]{:S(2)}) copy-start(bf16[7,3,3,4,4,64]{5,4,3,2,1,0:T(4,128)(2,1)} %mc.3) | copy-start | bytes 387076
  13.1 17.5 %collective-permute-start.6 = (f32[73,4,128]{2,1,0:T(4,128)S(1)}, f32[73,4,128]{2,1,0:T(4,128)S(1)}, u32[]{:S(2)}, u32[]{:S(2)}) collective-permute-start(f32[73,4,128]{2,1,0:T(4,128)S(1)} %get-tuple-element.53), channel_id=1, source_target_pairs={{0,8},{8,16},{16,24},{24,32},{32,40},{40,48},{48,56},{56,64},{64,7... | collective-permute-start | bytes 448520 | tf_op jit(solution)/shard_map/ppermute | solution.py:690
  16.7 13.9 %collective-permute-start.7 = (f32[73,4,128]{2,1,0:T(4,128)S(1)}, f32[73,4,128]{2,1,0:T(4,128)S(1)}, u32[]{:S(2)}, u32[]{:S(2)}) collective-permute-start(f32[73,4,128]{2,1,0:T(4,128)S(1)} %get-tuple-element.54), channel_id=1, source_target_pairs={{8,0},{16,8},{24,16},{32,24},{40,32},{48,40},{56,48},{64,56},{72,6... | collective-permute-start | bytes 448520 | tf_op jit(solution)/shard_map/ppermute | solution.py:690
  32.3 3.1 %copy-start.13 = (f32[3,3,8,8,128]{4,3,2,1,0:T(8,128)S(1)}, f32[3,3,8,8,128]{4,3,2,1,0:T(8,128)}, u32[]{:S(2)}) copy-start(f32[3,3,8,8,128]{4,3,2,1,0:T(8,128)} %param.15) | copy-start | bytes 884740
  34.0 67.3 %all-gather.19.cloned.1.call-start = ((), (), s32[]{:S(2)}) async-start(), calls=%async_computation.1 | async-start | bytes 1556480 | tf_op jit(solution)/shard_map/all_gather | solution.py:756
  36.9 80.0 %collective-permute-start.2 = (f32[576,8,128]{2,1,0:T(8,128)}, f32[576,8,128]{2,1,0:T(8,128)}, u32[]{:S(2)}, u32[]{:S(2)}) collective-permute-start(f32[576,8,128]{2,1,0:T(8,128)} %pad_maximum_fusion.own), channel_id=1, source_target_pairs={{0,1},{1,0},{2,3},{3,2},{4,5},{5,4},{6,7},{7,6},{8,9},{9,8},{10,11... | collective-permute-start | bytes 7077896 | tf_op jit(solution)/shard_map/ppermute | solution.py:750
  67.8 86.8 %collective-permute-start.8 = (f32[4,110,8,128]{3,2,1,0:T(8,128)}, f32[4,110,8,128]{3,2,1,0:T(8,128)}, u32[]{:S(2)}, u32[]{:S(2)}) collective-permute-start(f32[4,110,8,128]{3,2,1,0:T(8,128)} %bitcast.40), channel_id=1, source_target_pairs={{0,1},{1,0},{2,3},{3,2},{4,5},{5,4},{6,7},{7,6},{8,9},{9,8},{10,11... | collective-permute-start | bytes 5406728 | tf_op jit(solution)/shard_map/ppermute | solution.py:757
  101.2 63.1 %collective-permute-start.11 = (f32[4,76,8,128]{3,2,1,0:T(8,128)}, f32[4,76,8,128]{3,2,1,0:T(8,128)}, u32[]{:S(2)}, u32[]{:S(2)}) collective-permute-start(f32[4,76,8,128]{3,2,1,0:T(8,128)} %bitcast.44), channel_id=1, source_target_pairs={{0,1},{1,0},{2,3},{3,2},{4,5},{5,4},{6,7},{7,6},{8,9},{9,8},{10,11... | collective-permute-start | bytes 3735560 | tf_op jit(solution)/shard_map/ppermute | solution.py:758
  104.9 7.3 %collective-permute-start.1 = (f32[2,24,128]{2,1,0:T(8,128)S(1)}, f32[2,24,128]{2,1,0:T(8,128)S(1)}, u32[]{:S(2)}, u32[]{:S(2)}) collective-permute-start(f32[2,24,128]{2,1,0:T(8,128)S(1)} %get-tuple-element.46), channel_id=1, source_target_pairs={{0,2},{2,4},{4,6},{3,1},{5,3},{7,5},{8,10},{10,12},{12,14},{11,9},... | collective-permute-start | bytes 73736 | tf_op jit(solution)/shard_map/ppermute | solution.py:695
  106.2 6.9 %collective-permute-start = (f32[2,24,128]{2,1,0:T(8,128)S(1)}, f32[2,24,128]{2,1,0:T(8,128)S(1)}, u32[]{:S(2)}, u32[]{:S(2)}) collective-permute-start(f32[2,24,128]{2,1,0:T(8,128)S(1)} %get-tuple-element.45), channel_id=1, source_target_pairs={{0,8},{8,16},{16,24},{24,32},{32,40},{40,48},{48,56},{56,64},{64,7... | collective-permute-start | bytes 73736 | tf_op jit(solution)/shard_map/ppermute | solution.py:695
  120.0 5.1 %collective-permute-start.3 = (f32[2,24,128]{2,1,0:T(8,128)S(1)}, f32[2,24,128]{2,1,0:T(8,128)S(1)}, u32[]{:S(2)}, u32[]{:S(2)}) collective-permute-start(f32[2,24,128]{2,1,0:T(8,128)S(1)} %get-tuple-element.49), channel_id=1, source_target_pairs={{0,8},{8,16},{16,24},{24,32},{32,40},{40,48},{48,56},{56,64},{64,7... | collective-permute-start | bytes 73736 | tf_op jit(solution)/shard_map/ppermute | solution.py:695
  123.8 5.2 %collective-permute-start.4 = (f32[2,24,128]{2,1,0:T(8,128)S(1)}, f32[2,24,128]{2,1,0:T(8,128)S(1)}, u32[]{:S(2)}, u32[]{:S(2)}) collective-permute-start(f32[2,24,128]{2,1,0:T(8,128)S(1)} %get-tuple-element.50), channel_id=1, source_target_pairs={{0,2},{2,4},{4,6},{3,1},{5,3},{7,5},{8,10},{10,12},{12,14},{11,9},... | collective-permute-start | bytes 73736 | tf_op jit(solution)/shard_map/ppermute | solution.py:695
  134.5 4.6 %collective-permute-start.5 = (f32[24,128]{1,0:T(8,128)S(1)}, f32[24,128]{1,0:T(8,128)S(1)}, u32[]{:S(2)}, u32[]{:S(2)}) collective-permute-start(f32[24,128]{1,0:T(8,128)S(1)} %get-tuple-element.52), channel_id=1, source_target_pairs={{0,8},{8,16},{16,24},{24,32},{32,40},{40,48},{48,56},{56,64},{64,7... | collective-permute-start | bytes 36872 | tf_op jit(solution)/shard_map/ppermute | solution.py:695
  154.7 1.5 copy-start.1
  156.2 11.7 %copy-start.3 = (f32[304,8,128]{2,1,0:T(8,128)S(1)}, f32[304,8,128]{2,1,0:T(8,128)}, u32[]{:S(2)}) copy-start(f32[304,8,128]{2,1,0:T(8,128)} %all-gather.19.cloned.1.call-done) | copy-start | bytes 3735556
  158.9 5.4 %collective-permute-start.10 = (f32[8,8,128]{2,1,0:T(8,128)S(1)}, f32[8,8,128]{2,1,0:T(8,128)S(1)}, u32[]{:S(2)}, u32[]{:S(2)}) collective-permute-start(f32[8,8,128]{2,1,0:T(8,128)S(1)} %get-tuple-element.59.mid), channel_id=1, source_target_pairs={{8,0},{16,8},{24,16},{32,24},{40,32},{48,40},{56,48},{64,56},{72,6... | collective-permute-start | bytes 98312 | tf_op jit(solution)/shard_map/ppermute | solution.py:690
  161.1 6.8 %collective-permute-start.9 = (f32[8,8,128]{2,1,0:T(8,128)S(1)}, f32[8,8,128]{2,1,0:T(8,128)S(1)}, u32[]{:S(2)}, u32[]{:S(2)}) collective-permute-start(f32[8,8,128]{2,1,0:T(8,128)S(1)} %get-tuple-element.59.mid), channel_id=1, source_target_pairs={{0,8},{8,16},{16,24},{24,32},{32,40},{40,48},{48,56},{56,64},{64,7... | collective-permute-start | bytes 98312 | tf_op jit(solution)/shard_map/ppermute | solution.py:690
  164.3 40.1 %copy-start.2 = (f32[440,8,128]{2,1,0:T(8,128)S(1)}, f32[440,8,128]{2,1,0:T(8,128)}, u32[]{:S(2)}) copy-start(f32[440,8,128]{2,1,0:T(8,128)} %all-gather.17.cloned.1.call-done) | copy-start | bytes 5406724
  170.0 18.8 %collective-permute-start.13 = (f32[8,128]{1,0:T(8,128)S(1)}, f32[8,128]{1,0:T(8,128)S(1)}, u32[]{:S(2)}, u32[]{:S(2)}) collective-permute-start(f32[8,128]{1,0:T(8,128)S(1)} %get-tuple-element.61.mine), channel_id=1, source_target_pairs={{64,0},{72,8},{80,16},{88,24},{96,32},{104,40},{112,48},{120,56},{... | collective-permute-start | bytes 12296 | tf_op jit(solution)/shard_map/ppermute | solution.py:702
  177.6 11.3 %collective-permute-start.12 = (f32[8,128]{1,0:T(8,128)S(1)}, f32[8,128]{1,0:T(8,128)S(1)}, u32[]{:S(2)}, u32[]{:S(2)}) collective-permute-start(f32[8,128]{1,0:T(8,128)S(1)} %get-tuple-element.61.mine), channel_id=1, source_target_pairs={{32,0},{40,8},{48,16},{56,24},{64,32},{72,40},{80,48},{88,56},{96,... | collective-permute-start | bytes 12296 | tf_op jit(solution)/shard_map/ppermute | solution.py:702
  182.3 22.0 %collective-permute-start.15 = (f32[6,8,128]{2,1,0:T(8,128)S(1)}, f32[6,8,128]{2,1,0:T(8,128)S(1)}, u32[]{:S(2)}, u32[]{:S(2)}) collective-permute-start(f32[6,8,128]{2,1,0:T(8,128)S(1)} %get-tuple-element.65), channel_id=1, source_target_pairs={{8,0},{16,8},{24,16},{32,24},{40,32},{48,40},{56,48},{64,56},{72,6... | collective-permute-start | bytes 73736 | tf_op jit(solution)/shard_map/ppermute | solution.py:690
  186.3 18.1 %collective-permute-start.14 = (f32[6,8,128]{2,1,0:T(8,128)S(1)}, f32[6,8,128]{2,1,0:T(8,128)S(1)}, u32[]{:S(2)}, u32[]{:S(2)}) collective-permute-start(f32[6,8,128]{2,1,0:T(8,128)S(1)} %get-tuple-element.65), channel_id=1, source_target_pairs={{0,8},{8,16},{16,24},{24,32},{32,40},{40,48},{48,56},{56,64},{64,7... | collective-permute-start | bytes 73736 | tf_op jit(solution)/shard_map/ppermute | solution.py:690
  208.7 7.4 %collective-permute-start.16 = (f32[12,8,128]{2,1,0:T(8,128)S(1)}, f32[12,8,128]{2,1,0:T(8,128)S(1)}, u32[]{:S(2)}, u32[]{:S(2)}) collective-permute-start(f32[12,8,128]{2,1,0:T(8,128)S(1)} %get-tuple-element.68), channel_id=1, source_target_pairs={{0,8},{8,16},{16,24},{24,32},{32,40},{40,48},{48,56},{56,64},{64,7... | collective-permute-start | bytes 147464 | tf_op jit(solution)/shard_map/ppermute | solution.py:690
  210.6 6.6 %collective-permute-start.17 = (f32[12,8,128]{2,1,0:T(8,128)S(1)}, f32[12,8,128]{2,1,0:T(8,128)S(1)}, u32[]{:S(2)}, u32[]{:S(2)}) collective-permute-start(f32[12,8,128]{2,1,0:T(8,128)S(1)} %get-tuple-element.70), channel_id=1, source_target_pairs={{8,0},{16,8},{24,16},{32,24},{40,32},{48,40},{56,48},{64,56},{72,6... | collective-permute-start | bytes 147464 | tf_op jit(solution)/shard_map/ppermute | solution.py:690
  221.9 7.1 %collective-permute-start.18 = (f32[2,24,128]{2,1,0:T(8,128)S(1)}, f32[2,24,128]{2,1,0:T(8,128)S(1)}, u32[]{:S(2)}, u32[]{:S(2)}) collective-permute-start(f32[2,24,128]{2,1,0:T(8,128)S(1)} %get-tuple-element.75), channel_id=1, source_target_pairs={{0,8},{8,16},{16,24},{24,32},{32,40},{40,48},{48,56},{56,64},{64,7... | collective-permute-start | bytes 73736 | tf_op jit(solution)/shard_map/ppermute | solution.py:695
  227.7 4.9 %collective-permute-start.19 = (f32[2,24,128]{2,1,0:T(8,128)S(1)}, f32[2,24,128]{2,1,0:T(8,128)S(1)}, u32[]{:S(2)}, u32[]{:S(2)}) collective-permute-start(f32[2,24,128]{2,1,0:T(8,128)S(1)} %get-tuple-element.76), channel_id=1, source_target_pairs={{0,2},{2,4},{4,6},{3,1},{5,3},{7,5},{8,10},{10,12},{12,14},{11,9},... | collective-permute-start | bytes 73736 | tf_op jit(solution)/shard_map/ppermute | solution.py:695
  237.5 5.2 %collective-permute-start.20 = (f32[2,24,128]{2,1,0:T(8,128)S(1)}, f32[2,24,128]{2,1,0:T(8,128)S(1)}, u32[]{:S(2)}, u32[]{:S(2)}) collective-permute-start(f32[2,24,128]{2,1,0:T(8,128)S(1)} %get-tuple-element.79), channel_id=1, source_target_pairs={{0,8},{8,16},{16,24},{24,32},{32,40},{40,48},{48,56},{56,64},{64,7... | collective-permute-start | bytes 73736 | tf_op jit(solution)/shard_map/ppermute | solution.py:695
  241.4 5.1 %collective-permute-start.21 = (f32[2,24,128]{2,1,0:T(8,128)S(1)}, f32[2,24,128]{2,1,0:T(8,128)S(1)}, u32[]{:S(2)}, u32[]{:S(2)}) collective-permute-start(f32[2,24,128]{2,1,0:T(8,128)S(1)} %get-tuple-element.80), channel_id=1, source_target_pairs={{0,2},{2,4},{4,6},{3,1},{5,3},{7,5},{8,10},{10,12},{12,14},{11,9},... | collective-permute-start | bytes 73736 | tf_op jit(solution)/shard_map/ppermute | solution.py:695
  252.1 4.9 %collective-permute-start.22 = (f32[2,24,128]{2,1,0:T(8,128)S(1)}, f32[2,24,128]{2,1,0:T(8,128)S(1)}, u32[]{:S(2)}, u32[]{:S(2)}) collective-permute-start(f32[2,24,128]{2,1,0:T(8,128)S(1)} %get-tuple-element.84), channel_id=1, source_target_pairs={{0,8},{8,16},{16,24},{24,32},{32,40},{40,48},{48,56},{56,64},{64,7... | collective-permute-start | bytes 73736 | tf_op jit(solution)/shard_map/ppermute | solution.py:695
  255.7 5.1 %collective-permute-start.23 = (f32[2,24,128]{2,1,0:T(8,128)S(1)}, f32[2,24,128]{2,1,0:T(8,128)S(1)}, u32[]{:S(2)}, u32[]{:S(2)}) collective-permute-start(f32[2,24,128]{2,1,0:T(8,128)S(1)} %get-tuple-element.85), channel_id=1, source_target_pairs={{0,2},{2,4},{4,6},{3,1},{5,3},{7,5},{8,10},{10,12},{12,14},{11,9},... | collective-permute-start | bytes 73736 | tf_op jit(solution)/shard_map/ppermute | solution.py:695
  (8 other events, 6.7 us)
Sparse Core Ops, SparseCore 0:
  34.1 33.6 all-gather.16
  69.9 31.2 all-gather.18

commit v3 on v2

--- a/solution.py
+++ b/solution.py
@@ -105,13 +105,19 @@
     return lambda h, b, x: ref[fine.spot[h], which, 8 * b + x]
 
 
-def fine_first(ids, ls, first, xs, ys):
+def fine_first(ids, ls, couple, prolong, first, xs, ys, own):
     fine = Fine(ids)
     load, stiff = given(fine, ls, 0), given(fine, ls, 1)
     for h in range(2):
         for i in range(24):
             first[h, i] = load(h, i // 8, i % 8) / stiff(h, i // 8, i % 8)
     fine.send(at(first), xs, ys)
+    for i in range(63):
+        for x in range(8):
+            own[8 * i + x] = couple[i // 9, i // 3 % 3, i % 3, x].astype(F32)
+    for i in range(9):
+        for x in range(8):
+            own[504 + 8 * i + x] = prolong[i // 3, i % 3, x]
 
 
 def fine_second(ids, ls, first, halo, own, other, rest, second, xs, ys):
@@ -215,24 +221,30 @@
 
 
 class Group:
+    offset = 0
+
     def __init__(self, ids, own, other):
         self.packed = (own, other)
+        self.y = [lax.rem(ids[1] + r, 4) for r in range(4)]
+        self.below = [(y != 0).astype(F32) for y in self.y]
+        self.above = [(y != 3).astype(F32) for y in self.y]
         self.spot = (ids[0], 1 - ids[0])
         right = ids[0].astype(F32)
         self.right = (right, 1.0 - right)
 
     def field(self, g, i):
-        return self.packed[g % 2][g // 2, i]
+        return self.packed[g % 2][g // 2, self.offset + i]
 
     def sides(self, tiles, g, width):
         row, lane = rows8(), lanes8()
-        y, h = g // 2, g % 2
+        r, h = g // 2, g % 2
+        down, up = 2 * ((r + 3) % 4) + h, 2 * ((r + 1) % 4) + h
         views = [[], [], [], []]
         for b in range(3):
             v, o = tiles[g][b], tiles[g ^ 1][b]
-            edge = pltpu.roll(tiles[g - 2][b], 5, 0) if y > 0 else jnp.zeros_like(v)
+            edge = pltpu.roll(tiles[down][b], 5, 0) * self.below[r]
             views[0].append(jnp.where(row % 4 == 0, edge, pltpu.roll(v, 1, 0)))
-            edge = pltpu.roll(tiles[g + 2][b], 3, 0) if y < 3 else jnp.zeros_like(v)
+            edge = pltpu.roll(tiles[up][b], 3, 0) * self.above[r]
             views[1].append(jnp.where(row % 4 == 3, edge, pltpu.roll(v, 7, 0)))
             edge = pltpu.roll(o, 129 - width, 1) * self.right[h]
             views[2].append(jnp.where(lane % width == 0, edge, pltpu.roll(v, 1, 1)))
@@ -290,6 +302,8 @@
 
 
 class Coarse(Group):
+    offset = 110
+
     def stiff(self, g, a):
         return filled(self.field(g, 63 + a))
 
@@ -314,7 +328,7 @@
     level = Middle(ids, packed, other)
     row, lane = rows8(), lanes8()
     for g in range(8):
-        y, z = g // 2, level.spot[g % 2]
+        y, z = level.y[g // 2], level.spot[g % 2]
         for b in range(3):
             n = 3 * g + b
             load[n] = got[z, y, 8 * b : 8 * b + 8, :]
@@ -364,7 +378,7 @@
     return lanes8() // 8 == (4 * (y % 2) + rows8() % 4) * 2 + z
 
 
-def coarse_down(ids, low, mid, high, packed, other, load, pre, send, down, first, rest, second):
+def coarse_down(ids, low, mid, high, packed, other, load, pre, down, first, rest, second, ordered):
     level = Coarse(ids, packed, other)
     row, lane = rows8(), lanes8()
     place = lane // 32
@@ -400,25 +414,30 @@
         for b in range(3):
             n = 3 * g + b
             pre[n] = first[n] + second[n]
+            ordered[3 * (2 * level.y[g // 2] + level.spot[g % 2]) + b] = pre[n]
             terms.append(sum(level.prolong(g, 3 * a + b) * r[a] for a in range(3)))
 
     level.apply(second, use_last)
     for m in range(6):
-        t = [pre[4 * m + i] for i in range(4)]
+        t = [ordered[4 * m + i] for i in range(4)]
         right = jnp.where(row < 4, t[0], pltpu.roll(t[1], 4, 0))
         left = pltpu.roll(jnp.where(row < 4, t[2], pltpu.roll(t[3], 4, 0)), 64, 1)
-        send[m] = jnp.where(lane >= 64, right, left)
+        down[8 + 8 * m : 16 + 8 * m, :] = jnp.where(lane >= 64, right, left)
     source, to = iota((128, 128), 0), iota((128, 128), 1)
     pick = (source >= 64) & (to % 8 == (source % 32) // 4)
     out = dot(jnp.concatenate(terms, axis=0), pick.astype(F32))
-    down[...] = jnp.zeros((8, 128), F32)
+    down[0:8, :] = jnp.zeros((8, 128), F32)
     for b in range(3):
+        totals = [jnp.zeros((8, 128), F32)] * 2
+        for g in range(8):
+            n = 8 * (3 * g + b)
+            y = level.y[g // 2]
+            mine = jnp.where((row < 4) & own_lanes(y, level.spot[g % 2]), out[n : n + 8], 0.0)
+            upper = (y // 2).astype(F32)
+            totals[0] = totals[0] + mine * (1.0 - upper)
+            totals[1] = totals[1] + mine * upper
         for half in range(2):
-            total = jnp.zeros((8, 128), F32)
-            for g in range(4 * half, 4 * half + 4):
-                n = 8 * (3 * g + b)
-                total = total + jnp.where((row < 4) & own_lanes(g // 2, level.spot[g % 2]), out[n : n + 8], 0.0)
-            down[2 * b + half : 2 * b + half + 1, :] = jnp.sum(total, axis=0, keepdims=True)
+            down[2 * b + half : 2 * b + half + 1, :] = jnp.sum(totals[half], axis=0, keepdims=True)
 
 
 SHIFTS = ((-4, -3, -2, -1, 1, 2, 3, 4), (-8, -7, -6, -5, 5, 6, 7, 8))
@@ -445,8 +464,8 @@
 
 
 def bottom_and_up(
-    ids, got, mine, bottom_stiff, bottom_coefs, load2, low, mid, high, packed2, other2, pre1, packed1, other1,
-    guess1, lower, upper, load, now, guess, first, rest,
+    ids, got, mine, bottom_stiff, bottom_coefs, load2, mid, packed, other, pre1,
+    guess1, lower, upper, load, now, guess, first, rest, ordered,
 ):
     load[...] = jnp.zeros((3, ROWS, 128), F32)
     for b in range(3):
@@ -454,7 +473,7 @@
         for s in range(2):
             for g in range(8):
                 p = REACH - SHIFTS[s][g]
-                load[b, 2 * p : 2 * p + 2, :] = got[g % 2, g // 2, 8 * s + 2 * b : 8 * s + 2 * b + 2, :]
+                load[b, 2 * p : 2 * p + 2, :] = got[g % 2, g // 2, 56 * s + 2 * b : 56 * s + 2 * b + 2, :]
     lane = iota((ROWS, 128), 1)
     row = iota((ROWS, 128), 0)
     plane = ids[2] - REACH + row // 2
@@ -487,20 +506,32 @@
 
     lax.fori_loop(0, SWEEPS - 1, sweep, 0)
 
-    level = Coarse(ids, packed2, other2)
+    level = Coarse(ids, packed, other)
     row, lane = rows8(), lanes8()
 
-    def spread(b, q, half):
-        r = 2 * (REACH + q) + half
-        return jnp.broadcast_to(now[b, r : r + 1, :], (8, 128))
-
+    def spread(b, q, y):
+        r = 2 * (REACH + q)
+        return jnp.broadcast_to(jnp.where(y < 2, now[b, r : r + 1, :], now[b, r + 1 : r + 2, :]), (8, 128))
+
+    for n in range(24):
+        m, u = n // 4, n % 4
+        rows = slice(8 + 8 * m, 16 + 8 * m)
+        under = got[SHIFTS[0].index(1) % 2, SHIFTS[0].index(1) // 2, rows, :]
+        over = got[SHIFTS[0].index(-1) % 2, SHIFTS[0].index(-1) // 2, rows, :]
+        if u % 2 == 1:
+            under = pltpu.roll(under, 4, 0)
+        else:
+            over = pltpu.roll(over, 4, 0)
+        sides = jnp.where(row < 4, under, over)
+        ordered[n] = pltpu.roll(sides, 64, 1) if u < 2 else sides
     outer, inner = [], []
     for g in range(8):
-        here = own_lanes(g // 2, level.spot[g % 2])
+        y = level.y[g // 2]
+        here = own_lanes(y, level.spot[g % 2])
         for b in range(3):
-            e = jnp.where(row < 4, spread(b, -1, g // 4), spread(b, 1, g // 4))
+            e = jnp.where(row < 4, spread(b, -1, y), spread(b, 1, y))
             outer.append(jnp.where(here, e, 0.0))
-            inner.append(jnp.where(here, spread(b, 0, g // 4), 0.0))
+            inner.append(jnp.where(here, spread(b, 0, y), 0.0))
     source, to = iota((128, 128), 0), iota((128, 128), 1)
     pick = (source % 8 == (to % 32) // 4).astype(F32)
     ups = dot(jnp.concatenate(outer + inner, axis=0), pick)
@@ -511,15 +542,7 @@
             up.append(jnp.where((row < 4) & (lane >= 64), ups[192 + n : 200 + n], ups[n : n + 8]))
         for a in range(3):
             n = 3 * g + a
-            m, u = n // 4, n % 4
-            under, over = low[m], high[m]
-            if u % 2 == 1:
-                under = pltpu.roll(under, 4, 0)
-            else:
-                over = pltpu.roll(over, 4, 0)
-            sides = jnp.where(row < 4, under, over)
-            if u < 2:
-                sides = pltpu.roll(sides, 64, 1)
+            sides = ordered[3 * (2 * level.y[g // 2] + level.spot[g % 2]) + a]
             total = jnp.where(lane < 64, sides, jnp.where(row < 4, mid[n], 0.0))
             for b in range(3):
                 total = total + level.prolong(g, 3 * a + b) * up[b]
@@ -548,7 +571,7 @@
 
     pick = (source >= 64) & (source % 32 == (to % 64) // 2)
     ups = dot(jnp.concatenate(final, axis=0), pick.astype(F32))
-    middle = Middle(ids, packed1, other1)
+    middle = Middle(ids, packed, other)
     for g in range(8):
         for a in range(3):
             total = pre1[3 * g + a]
@@ -601,7 +624,7 @@
     rows = (iota((48, 24), 0) // 2 == iota((48, 24), 1)).astype(F32)
     source, to = iota((128, 128), 0), iota((128, 128), 1)
     for h in range(2):
-        tall = dot(rows, final[2 * ids[1] + h])
+        tall = dot(rows, final[h])
         ups = [dot(tall, (source == 64 * p + to // 2).astype(F32)) for p in range(2)]
         coefs0 = (own, other)[h]
         for a in range(3):
@@ -618,7 +641,7 @@
     return jnp.concatenate([left, right], axis=1)
 
 
-def pack_edges(ids, mc, ms, mp, cc, cs, cp, up, down, coarse):
+def pack_edges(ids, mc, ms, mp, cc, cs, cp, up, down, coarse, body):
     def mid(i, x):
         if i < 63:
             return mc[i // 9, i // 3 % 3, i % 3, x].astype(F32)
@@ -649,7 +672,6 @@
         coarse[t] = both
 
 
-def pack_levels(ids, mc, ms, mp, low, high, coarse, one, two):
     for i in range(75):
         if i < 63:
             v = [mc[i // 9, i // 3 % 3, i % 3, x].astype(F32) for x in range(4)]
@@ -657,18 +679,23 @@
             v = [ms[i - 63, x] for x in range(4)]
         else:
             v = [mp[(i - 66) // 3, (i - 66) % 3, x] for x in range(4)]
-        one[i, 0:4, :] = side_by_side(v[0], v[1])
-        one[i, 4:8, :] = side_by_side(v[2], v[3])
+        body[i, 0:4, :] = side_by_side(v[0], v[1])
+        body[i, 4:8, :] = side_by_side(v[2], v[3])
+
+
+def pack_levels(ids, body, low, high, coarse, one):
+    for i in range(75):
+        one[i] = body[i]
     for t in range(35):
         one[75 + t, 0:4, :] = low[t]
         one[75 + t, 4:8, :] = high[t]
     lane = iota((4, 128), 1)
     for t in range(38):
         under, here, over = low[35 + t], coarse[t], high[35 + t]
-        two[2 * t, 0:4, :] = jnp.where(lane < 64, under, pltpu.roll(here, 64, 1))
-        two[2 * t, 4:8, :] = jnp.where(lane < 64, over, 0.0)
-        two[2 * t + 1, 0:4, :] = jnp.where(lane < 64, pltpu.roll(under, 64, 1), here)
-        two[2 * t + 1, 4:8, :] = jnp.where(lane < 64, pltpu.roll(over, 64, 1), 0.0)
+        one[110 + 2 * t, 0:4, :] = jnp.where(lane < 64, under, pltpu.roll(here, 64, 1))
+        one[110 + 2 * t, 4:8, :] = jnp.where(lane < 64, over, 0.0)
+        one[111 + 2 * t, 0:4, :] = jnp.where(lane < 64, pltpu.roll(under, 64, 1), here)
+        one[111 + 2 * t, 4:8, :] = jnp.where(lane < 64, pltpu.roll(over, 64, 1), 0.0)
 
 
 VMEM = pl.BlockSpec(memory_space=pltpu.VMEM)
@@ -736,32 +763,33 @@
     edge = (2, 24, 128)
     block = (24, 8, 128)
 
-    raw = [middle_couple, middle_stiff, middle_prolong]
-    up, down, packed = run(
-        pack_edges,
-        ids,
-        raw + [coarse_couple, coarse_stiff, coarse_prolong],
-        [(73, 4, 128), (73, 4, 128), (38, 4, 128)],
-    )
-    below, above = shifted(up, "gx", count, 1), shifted(down, "gx", count, -1)
-
-    ls = lax.all_gather(jnp.stack([right_side.reshape(block), fine_stiff.reshape(block)]), "ga")
-    own = jnp.concatenate([fine_couple.astype(F32).reshape(504, 8, 128), fine_prolong.reshape(72, 8, 128)])
-    other = lax.ppermute(own, "ga", [(0, 1), (1, 0)])
-    first, xs, ys = run(fine_first, ids, [ls], [half, edge, edge])
-    below, above, _ = lax.optimization_barrier((below, above, xs))
-    one, two = run(pack_levels, ids, raw + [below, above, packed], [(110, 8, 128), (76, 8, 128)])
-    swap = [(0, 1), (1, 0)]
-    packed1 = lax.all_gather(one, "gy")
-    packed2 = lax.all_gather(two, "gy")
-    other1 = lax.ppermute(packed1, "ga", swap)
-    other2 = lax.ppermute(packed2, "ga", swap)
-    halo = exchange(xs, ys)
-    rest, second, xs, ys = run(fine_second, ids, [ls, first, halo, own, other], [half, half, edge, edge])
-
     cut = lax.dynamic_slice_in_dim(bottom_stiff, start * 128, span * 256, 1)
     cut_couple = lax.dynamic_slice_in_dim(bottom_couple, start * 128, span * 256, 3)
     bottom_s, bottom_c = run(bottom_window, ids, [cut, cut_couple], [(3, ROWS, 128), (63, ROWS, 128)])
+    right_side, middle_stiff, bottom_s = lax.optimization_barrier((right_side, middle_stiff, bottom_s))
+
+    up, down, coarse, body = run(
+        pack_edges,
+        ids,
+        [middle_couple, middle_stiff, middle_prolong, coarse_couple, coarse_stiff, coarse_prolong],
+        [(73, 4, 128), (73, 4, 128), (38, 4, 128), (75, 8, 128)],
+    )
+    below, above = shifted(up, "gx", count, 1), shifted(down, "gx", count, -1)
+
+    ls = lax.all_gather(jnp.stack([right_side.reshape(block), fine_stiff.reshape(block)]), "ga")
+    first, xs, ys, own = run(
+        fine_first, ids, [ls, fine_couple, fine_prolong], [half, edge, edge, (576, 8, 128)]
+    )
+    swap = [(0, 1), (1, 0)]
+    other = lax.ppermute(own, "ga", swap)
+    below, above, _ = lax.optimization_barrier((below, above, xs))
+    (bulk,) = run(pack_levels, ids, [body, below, above, coarse], [(186, 8, 128)])
+    others = [lax.ppermute(bulk, "gy", [((i + r) % 4, i) for i in range(4)]) for r in range(1, 4)]
+    halo = exchange(xs, ys)
+    rest, second, xs, ys = run(fine_second, ids, [ls, first, halo, own, other], [half, half, edge, edge])
+    others = lax.optimization_barrier((*others, xs))[:3]
+    packed = jnp.stack([bulk, *others])
+    packed_other = lax.ppermute(packed, "ga", swap)
 
     halo = exchange(xs, ys)
     pre0, keep, send = run(
@@ -771,29 +799,28 @@
 
     tiles = (24, 8, 128)
     load1, edge1, pre1, load2 = run(
-        middle_down, ids, [got, packed1, other1], [tiles, tiles, tiles, (8, 8, 128)], [tiles] * 5
+        middle_down, ids, [got, packed, packed_other], [tiles, tiles, tiles, (8, 8, 128)], [tiles] * 5
     )
     low, high = shifted(load2, "gx", count, 1), shifted(load2, "gx", count, -1)
 
-    load2, pre2, send, mine = run(
-        coarse_down, ids, [low, load2, high, packed2, other2], [tiles, tiles, (6, 8, 128), (8, 128)], [tiles] * 3
-    )
-    got = group_gather(jnp.concatenate([skewed(mine, count, s) for s in SHIFTS]))
-    low, high = shifted(send, "gx", count, 1), shifted(send, "gx", count, -1)
+    load2, pre2, mine = run(
+        coarse_down, ids, [low, load2, high, packed, packed_other], [tiles, tiles, (56, 128)], [tiles] * 4
+    )
+    got = group_gather(jnp.concatenate([skewed(mine, count, SHIFTS[0]), skewed(mine[:8], count, SHIFTS[1])]))
 
     guess1, lower, upper = run(
         bottom_and_up,
         ids,
-        [got, mine, bottom_s, bottom_c, load2, low, pre2, high, packed2, other2, pre1, packed1, other1],
+        [got, mine, bottom_s, bottom_c, load2, pre2, packed, packed_other, pre1],
         [tiles, (12, 8, 128), (12, 8, 128)],
-        [(3, ROWS, 128), (3, ROWS, 128), tiles, tiles, tiles],
+        [(3, ROWS, 128), (3, ROWS, 128), tiles, tiles, tiles, tiles],
     )
     low, high = shifted(upper, "gx", count, 1), shifted(lower, "gx", count, -1)
 
     guess, xs, ys = run(
         middle_up,
         ids,
-        [low, guess1, high, load1, edge1, packed1, other1, pre0, own, other],
+        [low, guess1, high, load1, edge1, packed, packed_other, pre0, own, other],
         [half, edge, edge],
         [tiles] * 4 + [(8, 24, 128)],
     )

time: 274 us -> 216 us (0.79)
  waiting for transfers between devices: 80.9 us -> 55.8 us
  Pallas kernels: 33.8 us -> 18.3 us
  between operations: 14.5 us -> 1.08 us
  blocking collectives: 45 us -> 53.2 us
  local copies, waits for them, and re-layouts: 9.55 us -> 4.08 us
  starting transfers between devices: 84.3 us -> 80.4 us
    all_gather x2 -> x0, waiting for transfers between devices: 59.4 us -> none  [the longest x1 30.8 us: local(): packed2 = lax.all_gather(two, 'gy')]
    ppermute x11, waiting for transfers between devices: 16.8 us -> 41.2 us  [split_shift(): return lax.ppermute(value, (axis, 'ga'), pairs)]
    pallas_call x13, Pallas kernels: 33.8 us -> 18.3 us  [run(): pl.pallas_call(kernel, out_shape=[jax.ShapeDtypeStruct(s, F32) for s in o...]
    ppermute x2, waiting for transfers between devices: 0.01 us -> 6.91 us  [skewed(): return lax.ppermute(value, ('gx', 'gy', 'ga'), pairs)]
    ppermute x8 -> x6, starting transfers between devices: 32.4 us -> 25.9 us  [shifted(): lax.ppermute(value, axis, [(i, i + shift) for i in range(count) if 0 <= i...]
    ppermute x3 -> x5, starting transfers between devices: 8.48 us -> 14.9 us  [the longest x3 10.5 us: local(): lax.ppermute(bulk, 'gy', [((i + r) % 4, i) for i in range(4)])]
    unnamed x29 -> x19, local copies, waits for them, and re-layouts: 8.51 us -> 2.89 us
    all_gather x5, blocking collectives: 11.3 us -> 16.1 us  [exchange(): return lax.all_gather(both, 'ga')]
  transfers between devices with their start and end apart: 26 -> 24, of which waited for: 10 -> 14; matrix products, arithmetic and copies ran while one was open for 2% -> 0% of each run, Pallas kernels for 4% -> 2%
where the time goes in v3:
time: 216 us; the launch traced here: 214 us
  starting transfers between devices  80.4 us (37%)
  waiting for transfers between devices  55.8 us (26%)
  blocking collectives  53.2 us (25%)
  Pallas kernels  18.3 us (8%)
  local copies, waits for them, and re-layouts  4.08 us (2%)
    ppermute x11, waiting for transfers between devices, split_shift(): return lax.ppermute(value, (axis, 'ga'), pairs)  41.2 us
    ppermute x11, starting transfers between devices, split_shift(): return lax.ppermute(value, (axis, 'ga'), pairs)  33.7 us
    ppermute x6, starting transfers between devices, shifted(): lax.ppermute(value, axis, [(i, i + shift) for i in range(count) if 0 <= i...  25.9 us
    pallas_call x13, Pallas kernels, run(): pl.pallas_call(kernel, out_shape=[jax.ShapeDtypeStruct(s, F32) for s in o...  18.3 us
    all_gather x2, blocking collectives, group_gather(): return lax.all_gather(four.reshape((4,) + value.shape), 'ga')  16.9 us
    all_gather x5, blocking collectives, exchange(): return lax.all_gather(both, 'ga')  16.1 us
    all_gather x2, blocking collectives, group_gather(): four = lax.all_gather(pair, 'gy', axis_index_groups=[[0, 2], [1, 3]])  10.7 us
    ppermute x3, starting transfers between devices, local(): lax.ppermute(bulk, 'gy', [((i + r) % 4, i) for i in range(4)])  10.5 us
  transfers between devices with their start and end apart: 24, of which 14 were waited for; matrix products, arithmetic and copies ran while one was open for 0% of the time, Pallas kernels for 2%

profile of v3, /device:TPU:25, one launch (start us, length us, event | category | flops | bytes accessed | tf_op | source)
XLA Modules:
  0.0 214.1 jit_solution(5633964014189244044)
XLA Ops:
  4.8 2.4 %all-gather = f32[4,24,8,128]{3,2,1,0:T(8,128)S(1)} all-gather(f32[2,24,8,128]{3,2,1,0:T(8,128)S(1)} %pad_maximum_fusion.1), channel_id=2, replica_groups=mesh['gx'=64,'gy'=4,'ga'=2] {'ga'}, dimensions={0}, use_global_device_ids=true | all-gather | bytes 589824 | tf_op jit(solution)/shard_map/all_gather | solution.py:779
  9.1 2.3 %collective-permute-start.2 = (f32[576,8,128]{2,1,0:T(8,128)S(1)}, f32[576,8,128]{2,1,0:T(8,128)S(1)}, u32[]{:S(2)}, u32[]{:S(2)}) collective-permute-start(f32[576,8,128]{2,1,0:T(8,128)S(1)} %get-tuple-element.54.own), channel_id=1, source_target_pairs={{0,1},{1,0},{2,3},{3,2},{4,5},{5,4},{6,7},{7,6},{8,9},{9,8},{10,11... | collective-permute-start | bytes 7077896 | tf_op jit(solution)/shard_map/ppermute | solution.py:784
  13.0 3.5 %collective-permute-start.6 = (f32[73,4,128]{2,1,0:T(4,128)S(1)}, f32[73,4,128]{2,1,0:T(4,128)S(1)}, u32[]{:S(2)}, u32[]{:S(2)}) collective-permute-start(f32[73,4,128]{2,1,0:T(4,128)S(1)} %get-tuple-element.63), channel_id=1, source_target_pairs={{0,8},{8,16},{16,24},{24,32},{32,40},{40,48},{48,56},{56,64},{64,7... | collective-permute-start | bytes 448520 | tf_op jit(solution)/shard_map/ppermute | solution.py:717
  16.6 9.7 %collective-permute-start.7 = (f32[73,4,128]{2,1,0:T(4,128)S(1)}, f32[73,4,128]{2,1,0:T(4,128)S(1)}, u32[]{:S(2)}, u32[]{:S(2)}) collective-permute-start(f32[73,4,128]{2,1,0:T(4,128)S(1)} %get-tuple-element.64), channel_id=1, source_target_pairs={{8,0},{16,8},{24,16},{32,24},{40,32},{48,40},{56,48},{64,56},{72,6... | collective-permute-start | bytes 448520 | tf_op jit(solution)/shard_map/ppermute | solution.py:717
  26.2 2.2 %collective-permute-done.6.low = f32[73,4,128]{2,1,0:T(4,128)S(1)} collective-permute-done((f32[73,4,128]{2,1,0:T(4,128)S(1)}, f32[73,4,128]{2,1,0:T(4,128)S(1)}, u32[]{:S(2)}, u32[]{:S(2)}) %collective-permute-start.6) | collective-permute-done | bytes 149536 | tf_op jit(solution)/shard_map/ppermute | solution.py:717
  30.1 3.1 %collective-permute-start.10 = (f32[186,8,128]{2,1,0:T(8,128)S(1)}, f32[186,8,128]{2,1,0:T(8,128)S(1)}, u32[]{:S(2)}, u32[]{:S(2)}) collective-permute-start(f32[186,8,128]{2,1,0:T(8,128)S(1)} %shard_map.136), channel_id=1, source_target_pairs={{6,0},{0,2},{2,4},{4,6},{7,1},{1,3},{3,5},{5,7},{14,8},{8,10},{10,... | collective-permute-start | bytes 2285576 | tf_op jit(solution)/shard_map/ppermute | solution.py:787
  33.2 4.4 %collective-permute-start.9 = (f32[186,8,128]{2,1,0:T(8,128)S(1)}, f32[186,8,128]{2,1,0:T(8,128)S(1)}, u32[]{:S(2)}, u32[]{:S(2)}) collective-permute-start(f32[186,8,128]{2,1,0:T(8,128)S(1)} %shard_map.136), channel_id=1, source_target_pairs={{4,0},{6,2},{0,4},{2,6},{5,1},{7,3},{1,5},{3,7},{12,8},{14,10},{8,... | collective-permute-start | bytes 2285576 | tf_op jit(solution)/shard_map/ppermute | solution.py:787
  37.6 3.1 %collective-permute-start.8 = (f32[186,8,128]{2,1,0:T(8,128)S(1)}, f32[186,8,128]{2,1,0:T(8,128)S(1)}, u32[]{:S(2)}, u32[]{:S(2)}) collective-permute-start(f32[186,8,128]{2,1,0:T(8,128)S(1)} %shard_map.136), channel_id=1, source_target_pairs={{2,0},{4,2},{6,4},{0,6},{3,1},{5,3},{7,5},{1,7},{10,8},{12,10},{14... | collective-permute-start | bytes 2285576 | tf_op jit(solution)/shard_map/ppermute | solution.py:787
  42.0 27.9 %collective-permute-done.1 = f32[2,24,128]{2,1,0:T(8,128)S(1)} collective-permute-done((f32[2,24,128]{2,1,0:T(8,128)S(1)}, f32[2,24,128]{2,1,0:T(8,128)S(1)}, u32[]{:S(2)}, u32[]{:S(2)}) %collective-permute-start.1) | collective-permute-done | bytes 24608 | tf_op jit(solution)/shard_map/ppermute | solution.py:722
  69.9 6.2 %collective-permute-start = (f32[2,24,128]{2,1,0:T(8,128)S(1)}, f32[2,24,128]{2,1,0:T(8,128)S(1)}, u32[]{:S(2)}, u32[]{:S(2)}) collective-permute-start(f32[2,24,128]{2,1,0:T(8,128)S(1)} %get-tuple-element.52), channel_id=1, source_target_pairs={{0,8},{8,16},{16,24},{24,32},{32,40},{40,48},{48,56},{56,64},{64,7... | collective-permute-start | bytes 73736 | tf_op jit(solution)/shard_map/ppermute | solution.py:722
  83.7 5.7 %collective-permute-start.3 = (f32[2,24,128]{2,1,0:T(8,128)S(1)}, f32[2,24,128]{2,1,0:T(8,128)S(1)}, u32[]{:S(2)}, u32[]{:S(2)}) collective-permute-start(f32[2,24,128]{2,1,0:T(8,128)S(1)} %get-tuple-element.57), channel_id=1, source_target_pairs={{0,8},{8,16},{16,24},{24,32},{32,40},{40,48},{48,56},{56,64},{64,7... | collective-permute-start | bytes 73736 | tf_op jit(solution)/shard_map/ppermute | solution.py:722
  90.4 7.3 %all-gather.2 = f32[4,2,24,128]{3,2,1,0:T(8,128)S(1)} all-gather(f32[2,2,24,128]{3,2,1,0:T(8,128)S(1)} %pad_maximum_fusion.3), channel_id=4, replica_groups=mesh['gx'=64,'gy'=4,'ga'=2] {'ga'}, dimensions={0}, use_global_device_ids=true | all-gather | bytes 147456 | tf_op jit(solution)/shard_map/all_gather | solution.py:760
  99.5 3.6 %collective-permute-start.5 = (f32[24,128]{1,0:T(8,128)S(1)}, f32[24,128]{1,0:T(8,128)S(1)}, u32[]{:S(2)}, u32[]{:S(2)}) collective-permute-start(f32[24,128]{1,0:T(8,128)S(1)} %get-tuple-element.60), channel_id=1, source_target_pairs={{0,8},{8,16},{16,24},{24,32},{32,40},{40,48},{48,56},{56,64},{64,7... | collective-permute-start | bytes 36872 | tf_op jit(solution)/shard_map/ppermute | solution.py:722
  104.0 3.3 %all-gather.3 = f32[96,128]{1,0:T(8,128)S(1)} all-gather(f32[48,128]{1,0:T(8,128)S(1)} %pad_maximum_fusion.8), channel_id=5, replica_groups={{0,2},{4,6},{1,3},{5,7},{8,10},{12,14},{9,11},{13,15},{16,18},{20,22},{..., dimensions={0}, use_global_device_ids=true | all-gather | bytes 73728 | tf_op jit(solution)/shard_map/all_gather | solution.py:733
  107.3 5.1 %all-gather.4 = f32[4,48,128]{2,1,0:T(8,128)S(1)} all-gather(f32[2,48,128]{2,1,0:T(8,128)S(1)} %bitcast.50), channel_id=6, replica_groups={{0,4},{2,6},{1,5},{3,7},{8,12},{10,14},{9,13},{11,15},{16,20},{18,22},{..., dimensions={0}, use_global_device_ids=true | all-gather | bytes 147456 | tf_op jit(solution)/shard_map/all_gather | solution.py:734
  112.4 7.7 %all-gather.10 = f32[8,48,128]{2,1,0:T(8,128)S(1)} all-gather(f32[4,48,128]{2,1,0:T(8,128)S(1)} %all-gather.4), channel_id=12, replica_groups=mesh['gx'=64,'gy'=4,'ga'=2] {'ga'}, dimensions={0}, use_global_device_ids=true | all-gather | bytes 294912 | tf_op jit(solution)/shard_map/all_gather | solution.py:735
  123.8 3.4 %collective-permute-start.12 = (f32[8,8,128]{2,1,0:T(8,128)S(1)}, f32[8,8,128]{2,1,0:T(8,128)S(1)}, u32[]{:S(2)}, u32[]{:S(2)}) collective-permute-start(f32[8,8,128]{2,1,0:T(8,128)S(1)} %get-tuple-element.71.mid), channel_id=1, source_target_pairs={{0,8},{8,16},{16,24},{24,32},{32,40},{40,48},{48,56},{56,64},{64,7... | collective-permute-start | bytes 98312 | tf_op jit(solution)/shard_map/ppermute | solution.py:717
  127.2 3.4 %collective-permute-done.12.low = f32[8,8,128]{2,1,0:T(8,128)S(1)} collective-permute-done((f32[8,8,128]{2,1,0:T(8,128)S(1)}, f32[8,8,128]{2,1,0:T(8,128)S(1)}, u32[]{:S(2)}, u32[]{:S(2)}) %collective-permute-start.12) | collective-permute-done | bytes 32800 | tf_op jit(solution)/shard_map/ppermute | solution.py:717
  133.9 4.0 %collective-permute-start.15 = (f32[8,128]{1,0:T(8,128)S(1)}, f32[8,128]{1,0:T(8,128)S(1)}, u32[]{:S(2)}, u32[]{:S(2)}) collective-permute-start(f32[8,128]{1,0:T(8,128)S(1)} %slice.3), channel_id=1, source_target_pairs={{64,0},{72,8},{80,16},{88,24},{96,32},{104,40},{112,48},{120,56},{... | collective-permute-start | bytes 12296 | tf_op jit(solution)/shard_map/ppermute | solution.py:729
  137.9 6.9 %collective-permute-done.15 = f32[8,128]{1,0:T(8,128)S(1)} collective-permute-done((f32[8,128]{1,0:T(8,128)S(1)}, f32[8,128]{1,0:T(8,128)S(1)}, u32[]{:S(2)}, u32[]{:S(2)}) %collective-permute-start.15) | collective-permute-done | bytes 4128 | tf_op jit(solution)/shard_map/ppermute | solution.py:729
  144.8 3.7 %all-gather.5 = f32[128,128]{1,0:T(8,128)S(1)} all-gather(f32[64,128]{1,0:T(8,128)S(1)} %pad_maximum_fusion.7), channel_id=7, replica_groups={{0,2},{4,6},{1,3},{5,7},{8,10},{12,14},{9,11},{13,15},{16,18},{20,22},{..., dimensions={0}, use_global_device_ids=true | all-gather | bytes 98304 | tf_op jit(solution)/shard_map/all_gather | solution.py:733
  148.6 5.6 %all-gather.6 = f32[4,64,128]{2,1,0:T(8,128)S(1)} all-gather(f32[2,64,128]{2,1,0:T(8,128)S(1)} %bitcast.49), channel_id=8, replica_groups={{0,4},{2,6},{1,5},{3,7},{8,12},{10,14},{9,13},{11,15},{16,20},{18,22},{..., dimensions={0}, use_global_device_ids=true | all-gather | bytes 196608 | tf_op jit(solution)/shard_map/all_gather | solution.py:734
  154.2 9.2 %all-gather.11 = f32[8,64,128]{2,1,0:T(8,128)S(1)} all-gather(f32[4,64,128]{2,1,0:T(8,128)S(1)} %all-gather.6), channel_id=13, replica_groups=mesh['gx'=64,'gy'=4,'ga'=2] {'ga'}, dimensions={0}, use_global_device_ids=true | all-gather | bytes 393216 | tf_op jit(solution)/shard_map/all_gather | solution.py:735
  163.4 3.0 %shard_map.139 = (f32[24,8,128]{2,1,0:T(8,128)S(1)}, f32[12,8,128]{2,1,0:T(8,128)S(1)}, f32[12,8,128]{2,1,0:T(8,128)S(1)}) custom-call(s32[5]{0:T(128)S(1)} %stack.82.ids, f32[2,4,64,128]{3,2,1,0:T(8,128)S(1)} %bitcast.39, f32[56,128]{1,0:T(8,128)S(1)} %get-tuple-element.72.mine, f32[3,40,128]{2,1,0:T(8,128)S(1)} %get-tuple-element.73.bottom_stiff, ...), custom_call_target="tpu_custom_call" | custom-call | tf_op jit(solution)/shard_map/pallas_call | solution.py:706
  168.3 5.5 %collective-permute-start.17 = (f32[12,8,128]{2,1,0:T(8,128)S(1)}, f32[12,8,128]{2,1,0:T(8,128)S(1)}, u32[]{:S(2)}, u32[]{:S(2)}) collective-permute-start(f32[12,8,128]{2,1,0:T(8,128)S(1)} %get-tuple-element.80), channel_id=1, source_target_pairs={{8,0},{16,8},{24,16},{32,24},{40,32},{48,40},{56,48},{64,56},{72,6... | collective-permute-start | bytes 147464 | tf_op jit(solution)/shard_map/ppermute | solution.py:717
  176.5 5.8 %collective-permute-start.18 = (f32[2,24,128]{2,1,0:T(8,128)S(1)}, f32[2,24,128]{2,1,0:T(8,128)S(1)}, u32[]{:S(2)}, u32[]{:S(2)}) collective-permute-start(f32[2,24,128]{2,1,0:T(8,128)S(1)} %get-tuple-element.85), channel_id=1, source_target_pairs={{0,8},{8,16},{16,24},{24,32},{32,40},{40,48},{48,56},{56,64},{64,7... | collective-permute-start | bytes 73736 | tf_op jit(solution)/shard_map/ppermute | solution.py:722
  183.6 3.3 %collective-permute-done.19 = f32[2,24,128]{2,1,0:T(8,128)S(1)} collective-permute-done((f32[2,24,128]{2,1,0:T(8,128)S(1)}, f32[2,24,128]{2,1,0:T(8,128)S(1)}, u32[]{:S(2)}, u32[]{:S(2)}) %collective-permute-start.19) | collective-permute-done | bytes 24608 | tf_op jit(solution)/shard_map/ppermute | solution.py:722
  189.8 2.6 %collective-permute-start.20 = (f32[2,24,128]{2,1,0:T(8,128)S(1)}, f32[2,24,128]{2,1,0:T(8,128)S(1)}, u32[]{:S(2)}, u32[]{:S(2)}) collective-permute-start(f32[2,24,128]{2,1,0:T(8,128)S(1)} %get-tuple-element.89), channel_id=1, source_target_pairs={{0,8},{8,16},{16,24},{24,32},{32,40},{40,48},{48,56},{56,64},{64,7... | collective-permute-start | bytes 73736 | tf_op jit(solution)/shard_map/ppermute | solution.py:722
  194.4 2.9 %collective-permute-done.21 = f32[2,24,128]{2,1,0:T(8,128)S(1)} collective-permute-done((f32[2,24,128]{2,1,0:T(8,128)S(1)}, f32[2,24,128]{2,1,0:T(8,128)S(1)}, u32[]{:S(2)}, u32[]{:S(2)}) %collective-permute-start.21) | collective-permute-done | bytes 24608 | tf_op jit(solution)/shard_map/ppermute | solution.py:722
  201.2 3.2 %collective-permute-start.22 = (f32[2,24,128]{2,1,0:T(8,128)S(1)}, f32[2,24,128]{2,1,0:T(8,128)S(1)}, u32[]{:S(2)}, u32[]{:S(2)}) collective-permute-start(f32[2,24,128]{2,1,0:T(8,128)S(1)} %get-tuple-element.94), channel_id=1, source_target_pairs={{0,8},{8,16},{16,24},{24,32},{32,40},{40,48},{48,56},{56,64},{64,7... | collective-permute-start | bytes 73736 | tf_op jit(solution)/shard_map/ppermute | solution.py:722
  205.9 3.7 %collective-permute-done.23 = f32[2,24,128]{2,1,0:T(8,128)S(1)} collective-permute-done((f32[2,24,128]{2,1,0:T(8,128)S(1)}, f32[2,24,128]{2,1,0:T(8,128)S(1)}, u32[]{:S(2)}, u32[]{:S(2)}) %collective-permute-start.23) | collective-permute-done | bytes 24608 | tf_op jit(solution)/shard_map/ppermute | solution.py:722
  209.6 3.0 %all-gather.9 = f32[4,2,24,128]{3,2,1,0:T(8,128)S(1)} all-gather(f32[2,2,24,128]{3,2,1,0:T(8,128)S(1)} %pad_maximum_fusion.6), channel_id=11, replica_groups=mesh['gx'=64,'gy'=4,'ga'=2] {'ga'}, dimensions={0}, use_global_device_ids=true | all-gather | bytes 147456 | tf_op jit(solution)/shard_map/all_gather | solution.py:760
  (73 shorter events, 46.2 us)
Async XLA Ops:
  0.6 1.7 copy-start
  0.6 6.5 %copy-start.2 = (f32[3,3,8,8,128]{4,3,2,1,0:T(8,128)S(1)}, f32[3,3,8,8,128]{4,3,2,1,0:T(8,128)}, u32[]{:S(2)}) copy-start(f32[3,3,8,8,128]{4,3,2,1,0:T(8,128)} %prolong.1) | copy-start | bytes 884740
  2.3 9.1 %copy-start.5 = (f32[3,3,4,4,64]{4,3,2,1,0:T(4,128)S(1)}, f32[3,3,4,4,64]{4,3,2,1,0:T(4,128)}, u32[]{:S(2)}) copy-start(f32[3,3,4,4,64]{4,3,2,1,0:T(4,128)} %mp.1) | copy-start | bytes 110596
  2.3 9.1 %copy-start.8 = (f32[3,2,4,32]{3,2,1,0:T(4,128)S(1)}, f32[3,2,4,32]{3,2,1,0:T(4,128)}, u32[]{:S(2)}) copy-start(f32[3,2,4,32]{3,2,1,0:T(4,128)} %cs.1) | copy-start | bytes 9220
  2.8 8.6 %copy-start.3 = (bf16[7,3,3,4,4,64]{5,4,3,2,1,0:T(4,128)(2,1)S(1)}, bf16[7,3,3,4,4,64]{5,4,3,2,1,0:T(4,128)(2,1)}, u32[]{:S(2)}) copy-start(bf16[7,3,3,4,4,64]{5,4,3,2,1,0:T(4,128)(2,1)} %mc.1) | copy-start | bytes 387076
  2.8 8.6 %copy-start.4 = (bf16[7,3,3,2,4,32]{5,4,3,2,1,0:T(4,128)(2,1)S(1)}, bf16[7,3,3,2,4,32]{5,4,3,2,1,0:T(4,128)(2,1)}, u32[]{:S(2)}) copy-start(bf16[7,3,3,2,4,32]{5,4,3,2,1,0:T(4,128)(2,1)} %cc.1) | copy-start | bytes 96772
  2.8 8.7 %copy-start.6 = (f32[3,3,2,4,32]{4,3,2,1,0:T(4,128)S(1)}, f32[3,3,2,4,32]{4,3,2,1,0:T(4,128)}, u32[]{:S(2)}) copy-start(f32[3,3,2,4,32]{4,3,2,1,0:T(4,128)} %cp.1) | copy-start | bytes 27652
  7.2 1.2 copy-start.1
  9.1 69.8 %collective-permute-start.2 = (f32[576,8,128]{2,1,0:T(8,128)S(1)}, f32[576,8,128]{2,1,0:T(8,128)S(1)}, u32[]{:S(2)}, u32[]{:S(2)}) collective-permute-start(f32[576,8,128]{2,1,0:T(8,128)S(1)} %get-tuple-element.54.own), channel_id=1, source_target_pairs={{0,1},{1,0},{2,3},{3,2},{4,5},{5,4},{6,7},{7,6},{8,9},{9,8},{10,11... | collective-permute-start | bytes 7077896 | tf_op jit(solution)/shard_map/ppermute | solution.py:784
  13.0 15.4 %collective-permute-start.6 = (f32[73,4,128]{2,1,0:T(4,128)S(1)}, f32[73,4,128]{2,1,0:T(4,128)S(1)}, u32[]{:S(2)}, u32[]{:S(2)}) collective-permute-start(f32[73,4,128]{2,1,0:T(4,128)S(1)} %get-tuple-element.63), channel_id=1, source_target_pairs={{0,8},{8,16},{16,24},{24,32},{32,40},{40,48},{48,56},{56,64},{64,7... | collective-permute-start | bytes 448520 | tf_op jit(solution)/shard_map/ppermute | solution.py:717
  16.6 12.8 %collective-permute-start.7 = (f32[73,4,128]{2,1,0:T(4,128)S(1)}, f32[73,4,128]{2,1,0:T(4,128)S(1)}, u32[]{:S(2)}, u32[]{:S(2)}) collective-permute-start(f32[73,4,128]{2,1,0:T(4,128)S(1)} %get-tuple-element.64), channel_id=1, source_target_pairs={{8,0},{16,8},{24,16},{32,24},{40,32},{48,40},{56,48},{64,56},{72,6... | collective-permute-start | bytes 448520 | tf_op jit(solution)/shard_map/ppermute | solution.py:717
  30.1 50.0 %collective-permute-start.10 = (f32[186,8,128]{2,1,0:T(8,128)S(1)}, f32[186,8,128]{2,1,0:T(8,128)S(1)}, u32[]{:S(2)}, u32[]{:S(2)}) collective-permute-start(f32[186,8,128]{2,1,0:T(8,128)S(1)} %shard_map.136), channel_id=1, source_target_pairs={{6,0},{0,2},{2,4},{4,6},{7,1},{1,3},{3,5},{5,7},{14,8},{8,10},{10,... | collective-permute-start | bytes 2285576 | tf_op jit(solution)/shard_map/ppermute | solution.py:787
  33.2 46.9 %collective-permute-start.9 = (f32[186,8,128]{2,1,0:T(8,128)S(1)}, f32[186,8,128]{2,1,0:T(8,128)S(1)}, u32[]{:S(2)}, u32[]{:S(2)}) collective-permute-start(f32[186,8,128]{2,1,0:T(8,128)S(1)} %shard_map.136), channel_id=1, source_target_pairs={{4,0},{6,2},{0,4},{2,6},{5,1},{7,3},{1,5},{3,7},{12,8},{14,10},{8,... | collective-permute-start | bytes 2285576 | tf_op jit(solution)/shard_map/ppermute | solution.py:787
  37.6 42.5 %collective-permute-start.8 = (f32[186,8,128]{2,1,0:T(8,128)S(1)}, f32[186,8,128]{2,1,0:T(8,128)S(1)}, u32[]{:S(2)}, u32[]{:S(2)}) collective-permute-start(f32[186,8,128]{2,1,0:T(8,128)S(1)} %shard_map.136), channel_id=1, source_target_pairs={{2,0},{4,2},{6,4},{0,6},{3,1},{5,3},{7,5},{1,7},{10,8},{12,10},{14... | collective-permute-start | bytes 2285576 | tf_op jit(solution)/shard_map/ppermute | solution.py:787
  40.7 29.2 %collective-permute-start.1 = (f32[2,24,128]{2,1,0:T(8,128)S(1)}, f32[2,24,128]{2,1,0:T(8,128)S(1)}, u32[]{:S(2)}, u32[]{:S(2)}) collective-permute-start(f32[2,24,128]{2,1,0:T(8,128)S(1)} %get-tuple-element.53), channel_id=1, source_target_pairs={{0,2},{2,4},{4,6},{3,1},{5,3},{7,5},{8,10},{10,12},{12,14},{11,9},... | collective-permute-start | bytes 73736 | tf_op jit(solution)/shard_map/ppermute | solution.py:722
  69.9 7.1 %collective-permute-start = (f32[2,24,128]{2,1,0:T(8,128)S(1)}, f32[2,24,128]{2,1,0:T(8,128)S(1)}, u32[]{:S(2)}, u32[]{:S(2)}) collective-permute-start(f32[2,24,128]{2,1,0:T(8,128)S(1)} %get-tuple-element.52), channel_id=1, source_target_pairs={{0,8},{8,16},{16,24},{24,32},{32,40},{40,48},{48,56},{56,64},{64,7... | collective-permute-start | bytes 73736 | tf_op jit(solution)/shard_map/ppermute | solution.py:722
  80.3 39.8 %collective-permute-start.11 = (f32[4,186,8,128]{3,2,1,0:T(8,128)S(1)}, f32[4,186,8,128]{3,2,1,0:T(8,128)S(1)}, u32[]{:S(2)}, u32[]{:S(2)}) collective-permute-start(f32[4,186,8,128]{3,2,1,0:T(8,128)S(1)} %pad_maximum_fusion.packed), channel_id=1, source_target_pairs={{0,1},{1,0},{2,3},{3,2},{4,5},{5,4},{6,7},{7,6},{8,9},{9,8},{10,11... | collective-permute-start | bytes 9142280 | tf_op jit(solution)/shard_map/ppermute | solution.py:792
  82.4 7.1 %collective-permute-start.4 = (f32[2,24,128]{2,1,0:T(8,128)S(1)}, f32[2,24,128]{2,1,0:T(8,128)S(1)}, u32[]{:S(2)}, u32[]{:S(2)}) collective-permute-start(f32[2,24,128]{2,1,0:T(8,128)S(1)} %get-tuple-element.58), channel_id=1, source_target_pairs={{0,2},{2,4},{4,6},{3,1},{5,3},{7,5},{8,10},{10,12},{12,14},{11,9},... | collective-permute-start | bytes 73736 | tf_op jit(solution)/shard_map/ppermute | solution.py:722
  83.7 6.7 %collective-permute-start.3 = (f32[2,24,128]{2,1,0:T(8,128)S(1)}, f32[2,24,128]{2,1,0:T(8,128)S(1)}, u32[]{:S(2)}, u32[]{:S(2)}) collective-permute-start(f32[2,24,128]{2,1,0:T(8,128)S(1)} %get-tuple-element.57), channel_id=1, source_target_pairs={{0,8},{8,16},{16,24},{24,32},{32,40},{40,48},{48,56},{56,64},{64,7... | collective-permute-start | bytes 73736 | tf_op jit(solution)/shard_map/ppermute | solution.py:722
  99.5 4.5 %collective-permute-start.5 = (f32[24,128]{1,0:T(8,128)S(1)}, f32[24,128]{1,0:T(8,128)S(1)}, u32[]{:S(2)}, u32[]{:S(2)}) collective-permute-start(f32[24,128]{1,0:T(8,128)S(1)} %get-tuple-element.60), channel_id=1, source_target_pairs={{0,8},{8,16},{16,24},{24,32},{32,40},{40,48},{48,56},{56,64},{64,7... | collective-permute-start | bytes 36872 | tf_op jit(solution)/shard_map/ppermute | solution.py:722
  121.8 5.3 %collective-permute-start.13 = (f32[8,8,128]{2,1,0:T(8,128)S(1)}, f32[8,8,128]{2,1,0:T(8,128)S(1)}, u32[]{:S(2)}, u32[]{:S(2)}) collective-permute-start(f32[8,8,128]{2,1,0:T(8,128)S(1)} %get-tuple-element.71.mid), channel_id=1, source_target_pairs={{8,0},{16,8},{24,16},{32,24},{40,32},{48,40},{56,48},{64,56},{72,6... | collective-permute-start | bytes 98312 | tf_op jit(solution)/shard_map/ppermute | solution.py:717
  123.8 6.8 %collective-permute-start.12 = (f32[8,8,128]{2,1,0:T(8,128)S(1)}, f32[8,8,128]{2,1,0:T(8,128)S(1)}, u32[]{:S(2)}, u32[]{:S(2)}) collective-permute-start(f32[8,8,128]{2,1,0:T(8,128)S(1)} %get-tuple-element.71.mid), channel_id=1, source_target_pairs={{0,8},{8,16},{16,24},{24,32},{32,40},{40,48},{48,56},{56,64},{64,7... | collective-permute-start | bytes 98312 | tf_op jit(solution)/shard_map/ppermute | solution.py:717
  131.9 12.9 %collective-permute-start.14 = (f32[56,128]{1,0:T(8,128)S(1)}, f32[56,128]{1,0:T(8,128)S(1)}, u32[]{:S(2)}, u32[]{:S(2)}) collective-permute-start(f32[56,128]{1,0:T(8,128)S(1)} %get-tuple-element.72.mine), channel_id=1, source_target_pairs={{32,0},{40,8},{48,16},{56,24},{64,32},{72,40},{80,48},{88,56},{96,... | collective-permute-start | bytes 86024 | tf_op jit(solution)/shard_map/ppermute | solution.py:729
  133.9 11.0 %collective-permute-start.15 = (f32[8,128]{1,0:T(8,128)S(1)}, f32[8,128]{1,0:T(8,128)S(1)}, u32[]{:S(2)}, u32[]{:S(2)}) collective-permute-start(f32[8,128]{1,0:T(8,128)S(1)} %slice.3), channel_id=1, source_target_pairs={{64,0},{72,8},{80,16},{88,24},{96,32},{104,40},{112,48},{120,56},{... | collective-permute-start | bytes 12296 | tf_op jit(solution)/shard_map/ppermute | solution.py:729
  166.4 7.4 %collective-permute-start.16 = (f32[12,8,128]{2,1,0:T(8,128)S(1)}, f32[12,8,128]{2,1,0:T(8,128)S(1)}, u32[]{:S(2)}, u32[]{:S(2)}) collective-permute-start(f32[12,8,128]{2,1,0:T(8,128)S(1)} %get-tuple-element.78), channel_id=1, source_target_pairs={{0,8},{8,16},{16,24},{24,32},{32,40},{40,48},{48,56},{56,64},{64,7... | collective-permute-start | bytes 147464 | tf_op jit(solution)/shard_map/ppermute | solution.py:717
  168.3 6.6 %collective-permute-start.17 = (f32[12,8,128]{2,1,0:T(8,128)S(1)}, f32[12,8,128]{2,1,0:T(8,128)S(1)}, u32[]{:S(2)}, u32[]{:S(2)}) collective-permute-start(f32[12,8,128]{2,1,0:T(8,128)S(1)} %get-tuple-element.80), channel_id=1, source_target_pairs={{8,0},{16,8},{24,16},{32,24},{40,32},{48,40},{56,48},{64,56},{72,6... | collective-permute-start | bytes 147464 | tf_op jit(solution)/shard_map/ppermute | solution.py:717
  176.5 7.1 %collective-permute-start.18 = (f32[2,24,128]{2,1,0:T(8,128)S(1)}, f32[2,24,128]{2,1,0:T(8,128)S(1)}, u32[]{:S(2)}, u32[]{:S(2)}) collective-permute-start(f32[2,24,128]{2,1,0:T(8,128)S(1)} %get-tuple-element.85), channel_id=1, source_target_pairs={{0,8},{8,16},{16,24},{24,32},{32,40},{40,48},{48,56},{56,64},{64,7... | collective-permute-start | bytes 73736 | tf_op jit(solution)/shard_map/ppermute | solution.py:722
  182.2 4.6 %collective-permute-start.19 = (f32[2,24,128]{2,1,0:T(8,128)S(1)}, f32[2,24,128]{2,1,0:T(8,128)S(1)}, u32[]{:S(2)}, u32[]{:S(2)}) collective-permute-start(f32[2,24,128]{2,1,0:T(8,128)S(1)} %get-tuple-element.86), channel_id=1, source_target_pairs={{0,2},{2,4},{4,6},{3,1},{5,3},{7,5},{8,10},{10,12},{12,14},{11,9},... | collective-permute-start | bytes 73736 | tf_op jit(solution)/shard_map/ppermute | solution.py:722
  189.8 4.6 %collective-permute-start.20 = (f32[2,24,128]{2,1,0:T(8,128)S(1)}, f32[2,24,128]{2,1,0:T(8,128)S(1)}, u32[]{:S(2)}, u32[]{:S(2)}) collective-permute-start(f32[2,24,128]{2,1,0:T(8,128)S(1)} %get-tuple-element.89), channel_id=1, source_target_pairs={{0,8},{8,16},{16,24},{24,32},{32,40},{40,48},{48,56},{56,64},{64,7... | collective-permute-start | bytes 73736 | tf_op jit(solution)/shard_map/ppermute | solution.py:722
  192.4 4.9 %collective-permute-start.21 = (f32[2,24,128]{2,1,0:T(8,128)S(1)}, f32[2,24,128]{2,1,0:T(8,128)S(1)}, u32[]{:S(2)}, u32[]{:S(2)}) collective-permute-start(f32[2,24,128]{2,1,0:T(8,128)S(1)} %get-tuple-element.90), channel_id=1, source_target_pairs={{0,2},{2,4},{4,6},{3,1},{5,3},{7,5},{8,10},{10,12},{12,14},{11,9},... | collective-permute-start | bytes 73736 | tf_op jit(solution)/shard_map/ppermute | solution.py:722
  201.2 4.7 %collective-permute-start.22 = (f32[2,24,128]{2,1,0:T(8,128)S(1)}, f32[2,24,128]{2,1,0:T(8,128)S(1)}, u32[]{:S(2)}, u32[]{:S(2)}) collective-permute-start(f32[2,24,128]{2,1,0:T(8,128)S(1)} %get-tuple-element.94), channel_id=1, source_target_pairs={{0,8},{8,16},{16,24},{24,32},{32,40},{40,48},{48,56},{56,64},{64,7... | collective-permute-start | bytes 73736 | tf_op jit(solution)/shard_map/ppermute | solution.py:722
  204.5 5.1 %collective-permute-start.23 = (f32[2,24,128]{2,1,0:T(8,128)S(1)}, f32[2,24,128]{2,1,0:T(8,128)S(1)}, u32[]{:S(2)}, u32[]{:S(2)}) collective-permute-start(f32[2,24,128]{2,1,0:T(8,128)S(1)} %get-tuple-element.95), channel_id=1, source_target_pairs={{0,2},{2,4},{4,6},{3,1},{5,3},{7,5},{8,10},{10,12},{12,14},{11,9},... | collective-permute-start | bytes 73736 | tf_op jit(solution)/shard_map/ppermute | solution.py:722
  (1 other events, 0.7 us)

commit v4 on v3

--- a/solution.py
+++ b/solution.py
@@ -221,19 +221,18 @@
 
 
 class Group:
-    offset = 0
-
-    def __init__(self, ids, own, other):
-        self.packed = (own, other)
+    def __init__(self, ids, packed):
+        self.packed = packed
         self.y = [lax.rem(ids[1] + r, 4) for r in range(4)]
         self.below = [(y != 0).astype(F32) for y in self.y]
         self.above = [(y != 3).astype(F32) for y in self.y]
         self.spot = (ids[0], 1 - ids[0])
         right = ids[0].astype(F32)
         self.right = (right, 1.0 - right)
+        self.place = [2 * self.y[g // 2] + self.spot[g % 2] for g in range(8)]
 
     def field(self, g, i):
-        return self.packed[g % 2][g // 2, self.offset + i]
+        return self.packed[self.place[g], i]
 
     def sides(self, tiles, g, width):
         row, lane = rows8(), lanes8()
@@ -302,8 +301,6 @@
 
 
 class Coarse(Group):
-    offset = 110
-
     def stiff(self, g, a):
         return filled(self.field(g, 63 + a))
 
@@ -324,8 +321,8 @@
             use(g, combine([self.stiff(g, a) for a in range(3)], lambda i: self.field(g, i), views))
 
 
-def middle_down(ids, got, packed, other, load, load_edge, pre, down, first, first_edge, rest, second, second_edge):
-    level = Middle(ids, packed, other)
+def middle_down(ids, got, packed, load, load_edge, pre, down, first, first_edge, rest, second, second_edge):
+    level = Middle(ids, packed)
     row, lane = rows8(), lanes8()
     for g in range(8):
         y, z = level.y[g // 2], level.spot[g % 2]
@@ -378,8 +375,8 @@
     return lanes8() // 8 == (4 * (y % 2) + rows8() % 4) * 2 + z
 
 
-def coarse_down(ids, low, mid, high, packed, other, load, pre, down, first, rest, second, ordered):
-    level = Coarse(ids, packed, other)
+def coarse_down(ids, low, mid, high, packed, load, pre, down, first, rest, second, ordered):
+    level = Coarse(ids, packed)
     row, lane = rows8(), lanes8()
     place = lane // 32
     for g in range(8):
@@ -414,7 +411,7 @@
         for b in range(3):
             n = 3 * g + b
             pre[n] = first[n] + second[n]
-            ordered[3 * (2 * level.y[g // 2] + level.spot[g % 2]) + b] = pre[n]
+            ordered[3 * level.place[g] + b] = pre[n]
             terms.append(sum(level.prolong(g, 3 * a + b) * r[a] for a in range(3)))
 
     level.apply(second, use_last)
@@ -464,7 +461,7 @@
 
 
 def bottom_and_up(
-    ids, got, mine, bottom_stiff, bottom_coefs, load2, mid, packed, other, pre1,
+    ids, got, mine, bottom_stiff, bottom_coefs, load2, mid, packed, pre1, packed1,
     guess1, lower, upper, load, now, guess, first, rest, ordered,
 ):
     load[...] = jnp.zeros((3, ROWS, 128), F32)
@@ -506,7 +503,7 @@
 
     lax.fori_loop(0, SWEEPS - 1, sweep, 0)
 
-    level = Coarse(ids, packed, other)
+    level = Coarse(ids, packed)
     row, lane = rows8(), lanes8()
 
     def spread(b, q, y):
@@ -542,7 +539,7 @@
             up.append(jnp.where((row < 4) & (lane >= 64), ups[192 + n : 200 + n], ups[n : n + 8]))
         for a in range(3):
             n = 3 * g + a
-            sides = ordered[3 * (2 * level.y[g // 2] + level.spot[g % 2]) + a]
+            sides = ordered[3 * level.place[g] + a]
             total = jnp.where(lane < 64, sides, jnp.where(row < 4, mid[n], 0.0))
             for b in range(3):
                 total = total + level.prolong(g, 3 * a + b) * up[b]
@@ -571,7 +568,7 @@
 
     pick = (source >= 64) & (source % 32 == (to % 64) // 2)
     ups = dot(jnp.concatenate(final, axis=0), pick.astype(F32))
-    middle = Middle(ids, packed, other)
+    middle = Middle(ids, packed1)
     for g in range(8):
         for a in range(3):
             total = pre1[3 * g + a]
@@ -586,10 +583,10 @@
 
 
 def middle_up(
-    ids, low, mid, high, load, load_edge, packed, packed_other, pre, own, other, result, xs, ys, guess_edge, first, first_edge, rest, final
+    ids, low, mid, high, load, load_edge, packed, pre, own, other, result, xs, ys, guess_edge, first, first_edge, rest, final
 ):
     fine = Fine(ids)
-    level = Middle(ids, packed, packed_other)
+    level = Middle(ids, packed)
     row = rows8()
     for n in range(24):
         under, over = low[n // 2], high[n // 2]
@@ -683,7 +680,7 @@
         body[i, 4:8, :] = side_by_side(v[2], v[3])
 
 
-def pack_levels(ids, body, low, high, coarse, one):
+def pack_levels(ids, body, low, high, coarse, one, two):
     for i in range(75):
         one[i] = body[i]
     for t in range(35):
@@ -692,10 +689,10 @@
     lane = iota((4, 128), 1)
     for t in range(38):
         under, here, over = low[35 + t], coarse[t], high[35 + t]
-        one[110 + 2 * t, 0:4, :] = jnp.where(lane < 64, under, pltpu.roll(here, 64, 1))
-        one[110 + 2 * t, 4:8, :] = jnp.where(lane < 64, over, 0.0)
-        one[111 + 2 * t, 0:4, :] = jnp.where(lane < 64, pltpu.roll(under, 64, 1), here)
-        one[111 + 2 * t, 4:8, :] = jnp.where(lane < 64, pltpu.roll(over, 64, 1), 0.0)
+        two[2 * t, 0:4, :] = jnp.where(lane < 64, under, pltpu.roll(here, 64, 1))
+        two[2 * t, 4:8, :] = jnp.where(lane < 64, over, 0.0)
+        two[2 * t + 1, 0:4, :] = jnp.where(lane < 64, pltpu.roll(under, 64, 1), here)
+        two[2 * t + 1, 4:8, :] = jnp.where(lane < 64, pltpu.roll(over, 64, 1), 0.0)
 
 
 VMEM = pl.BlockSpec(memory_space=pltpu.VMEM)
@@ -783,14 +780,11 @@
     swap = [(0, 1), (1, 0)]
     other = lax.ppermute(own, "ga", swap)
     below, above, _ = lax.optimization_barrier((below, above, xs))
-    (bulk,) = run(pack_levels, ids, [body, below, above, coarse], [(186, 8, 128)])
-    others = [lax.ppermute(bulk, "gy", [((i + r) % 4, i) for i in range(4)]) for r in range(1, 4)]
+    one, two = run(pack_levels, ids, [body, below, above, coarse], [(110, 8, 128), (76, 8, 128)])
+    packed1 = lax.all_gather(one, ("gy", "ga"))
+    packed2 = lax.all_gather(two, ("gy", "ga"))
     halo = exchange(xs, ys)
     rest, second, xs, ys = run(fine_second, ids, [ls, first, halo, own, other], [half, half, edge, edge])
-    others = lax.optimization_barrier((*others, xs))[:3]
-    packed = jnp.stack([bulk, *others])
-    packed_other = lax.ppermute(packed, "ga", swap)
-
     halo = exchange(xs, ys)
     pre0, keep, send = run(
         fine_down, ids, [ls, first, second, rest, halo, own, other], [half, (24, 128), (24, 128)]
@@ -799,19 +793,19 @@
 
     tiles = (24, 8, 128)
     load1, edge1, pre1, load2 = run(
-        middle_down, ids, [got, packed, packed_other], [tiles, tiles, tiles, (8, 8, 128)], [tiles] * 5
+        middle_down, ids, [got, packed1], [tiles, tiles, tiles, (8, 8, 128)], [tiles] * 5
     )
     low, high = shifted(load2, "gx", count, 1), shifted(load2, "gx", count, -1)
 
     load2, pre2, mine = run(
-        coarse_down, ids, [low, load2, high, packed, packed_other], [tiles, tiles, (56, 128)], [tiles] * 4
+        coarse_down, ids, [low, load2, high, packed2], [tiles, tiles, (56, 128)], [tiles] * 4
     )
     got = group_gather(jnp.concatenate([skewed(mine, count, SHIFTS[0]), skewed(mine[:8], count, SHIFTS[1])]))
 
     guess1, lower, upper = run(
         bottom_and_up,
         ids,
-        [got, mine, bottom_s, bottom_c, load2, pre2, packed, packed_other, pre1],
+        [got, mine, bottom_s, bottom_c, load2, pre2, packed2, pre1, packed1],
         [tiles, (12, 8, 128), (12, 8, 128)],
         [(3, ROWS, 128), (3, ROWS, 128), tiles, tiles, tiles, tiles],
     )
@@ -820,7 +814,7 @@
     guess, xs, ys = run(
         middle_up,
         ids,
-        [low, guess1, high, load1, edge1, packed, packed_other, pre0, own, other],
+        [low, guess1, high, load1, edge1, packed1, pre0, own, other],
         [half, edge, edge],
         [tiles] * 4 + [(8, 24, 128)],
     )

time: 216 us -> 208 us (0.963)
  waiting for transfers between devices: 55.8 us -> 32.8 us
  local copies, waits for them, and re-layouts: 4.08 us -> 17.6 us
  between operations: 1.08 us -> 14.4 us
  starting transfers between devices: 80.4 us -> 72.1 us
  blocking collectives: 53.2 us -> 49.2 us
    ppermute x11, waiting for transfers between devices: 41.2 us -> 16.6 us  [split_shift(): return lax.ppermute(value, (axis, 'ga'), pairs)]
    unnamed x19 -> x47, local copies, waits for them, and re-layouts: 2.89 us -> 16.4 us
    ppermute x4 -> x0, starting transfers between devices: 12.6 us -> none  [the longest x3 10.5 us: local(): lax.ppermute(bulk, 'gy', [((i + r) % 4, i) for i in range(4)])]
    all_gather x0 -> x2, waiting for transfers between devices: none -> 10.6 us  [the longest x1 10.6 us: local(): packed2 = lax.all_gather(two, ('gy', 'ga'))]
    ppermute x2, starting transfers between devices: 5.96 us -> 14.8 us  [skewed(): return lax.ppermute(value, ('gx', 'gy', 'ga'), pairs)]
    ppermute x6, waiting for transfers between devices: 7.67 us -> 1.16 us  [shifted(): lax.ppermute(value, axis, [(i, i + shift) for i in range(count) if 0 <= i...]
    ppermute x11, starting transfers between devices: 33.7 us -> 29 us  [split_shift(): return lax.ppermute(value, (axis, 'ga'), pairs)]
    all_gather x2, blocking collectives: 16.9 us -> 13.1 us  [group_gather(): return lax.all_gather(four.reshape((4,) + value.shape), 'ga')]
  transfers between devices with their start and end apart: 24 -> 22, of which waited for: 14 -> 11; matrix products, arithmetic and copies ran while one was open for 0% -> 0% of each run, Pallas kernels for 2% -> 3%
where the time goes in v4:
time: 208 us; the launch traced here: 206 us
  starting transfers between devices  72.1 us (35%)
  blocking collectives  49.2 us (24%)
  waiting for transfers between devices  32.8 us (16%)
  Pallas kernels  19 us (9%)
  local copies, waits for them, and re-layouts  17.6 us (8%)
  between operations  14.4 us (7%)
    ppermute x11, starting transfers between devices, split_shift(): return lax.ppermute(value, (axis, 'ga'), pairs)  29 us
    ppermute x6, starting transfers between devices, shifted(): lax.ppermute(value, axis, [(i, i + shift) for i in range(count) if 0 <= i...  25.9 us
    pallas_call x13, Pallas kernels, run(): pl.pallas_call(kernel, out_shape=[jax.ShapeDtypeStruct(s, F32) for s in o...  19 us
    ppermute x11, waiting for transfers between devices, split_shift(): return lax.ppermute(value, (axis, 'ga'), pairs)  16.6 us
    unnamed x47, local copies, waits for them, and re-layouts  16.4 us
    ppermute x2, starting transfers between devices, skewed(): return lax.ppermute(value, ('gx', 'gy', 'ga'), pairs)  14.8 us
    all_gather x5, blocking collectives, exchange(): return lax.all_gather(both, 'ga')  14.5 us
    all_gather x2, blocking collectives, group_gather(): return lax.all_gather(four.reshape((4,) + value.shape), 'ga')  13.1 us
  transfers between devices with their start and end apart: 22, of which 11 were waited for; matrix products, arithmetic and copies ran while one was open for 0% of the time, Pallas kernels for 3%

profile of v4, /device:TPU:25, one launch (start us, length us, event | category | flops | bytes accessed | tf_op | source)
XLA Modules:
  0.0 206.0 jit_solution(16799961190702085212)
XLA Ops:
  15.6 3.5 %collective-permute-start.6 = (f32[73,4,128]{2,1,0:T(4,128)S(1)}, f32[73,4,128]{2,1,0:T(4,128)S(1)}, u32[]{:S(2)}, u32[]{:S(2)}) collective-permute-start(f32[73,4,128]{2,1,0:T(4,128)S(1)} %get-tuple-element.62), channel_id=1, source_target_pairs={{0,8},{8,16},{16,24},{24,32},{32,40},{40,48},{48,56},{56,64},{64,7... | collective-permute-start | bytes 448520 | tf_op jit(solution)/shard_map/ppermute | solution.py:714
  19.2 9.7 %collective-permute-start.7 = (f32[73,4,128]{2,1,0:T(4,128)S(1)}, f32[73,4,128]{2,1,0:T(4,128)S(1)}, u32[]{:S(2)}, u32[]{:S(2)}) collective-permute-start(f32[73,4,128]{2,1,0:T(4,128)S(1)} %get-tuple-element.63), channel_id=1, source_target_pairs={{8,0},{16,8},{24,16},{32,24},{40,32},{48,40},{56,48},{64,56},{72,6... | collective-permute-start | bytes 448520 | tf_op jit(solution)/shard_map/ppermute | solution.py:714
  29.8 2.7 %all-gather = f32[4,24,8,128]{3,2,1,0:T(8,128)S(1)} all-gather(f32[2,24,8,128]{3,2,1,0:T(8,128)S(1)} %pad_maximum_fusion), channel_id=2, replica_groups=mesh['gx'=64,'gy'=4,'ga'=2] {'ga'}, dimensions={0}, use_global_device_ids=true | all-gather | bytes 589824 | tf_op jit(solution)/shard_map/all_gather | solution.py:776
  37.1 2.3 %collective-permute-start.2 = (f32[576,8,128]{2,1,0:T(8,128)}, f32[576,8,128]{2,1,0:T(8,128)S(1)}, u32[]{:S(2)}, u32[]{:S(2)}) collective-permute-start(f32[576,8,128]{2,1,0:T(8,128)} %copy-done.1), channel_id=1, source_target_pairs={{0,1},{1,0},{2,3},{3,2},{4,5},{5,4},{6,7},{7,6},{8,9},{9,8},{10,11... | collective-permute-start | bytes 7077896 | tf_op jit(solution)/shard_map/ppermute | solution.py:781
  40.7 4.1 %collective-permute-start = (f32[2,24,128]{2,1,0:T(8,128)S(1)}, f32[2,24,128]{2,1,0:T(8,128)S(1)}, u32[]{:S(2)}, u32[]{:S(2)}) collective-permute-start(f32[2,24,128]{2,1,0:T(8,128)S(1)} %get-tuple-element.51), channel_id=1, source_target_pairs={{0,8},{8,16},{16,24},{24,32},{32,40},{40,48},{48,56},{56,64},{64,7... | collective-permute-start | bytes 73736 | tf_op jit(solution)/shard_map/ppermute | solution.py:719
  45.8 6.6 %all-gather.1 = f32[4,2,24,128]{3,2,1,0:T(8,128)S(1)} all-gather(f32[2,2,24,128]{3,2,1,0:T(8,128)S(1)} %pad_maximum_fusion.1), channel_id=3, replica_groups=mesh['gx'=64,'gy'=4,'ga'=2] {'ga'}, dimensions={0}, use_global_device_ids=true | all-gather | bytes 147456 | tf_op jit(solution)/shard_map/all_gather | solution.py:757
  52.3 2.5 %copy-done.2 = f32[576,8,128]{2,1,0:T(8,128)S(1)} copy-done((f32[576,8,128]{2,1,0:T(8,128)S(1)}, f32[576,8,128]{2,1,0:T(8,128)}, u32[]{:S(2)}) %copy-start.2) | copy-done | bytes 2359320
  61.0 2.4 %collective-permute-done.4 = f32[2,24,128]{2,1,0:T(8,128)S(1)} collective-permute-done((f32[2,24,128]{2,1,0:T(8,128)S(1)}, f32[2,24,128]{2,1,0:T(8,128)S(1)}, u32[]{:S(2)}, u32[]{:S(2)}) %collective-permute-start.4) | collective-permute-done | bytes 24608 | tf_op jit(solution)/shard_map/ppermute | solution.py:719
  63.4 2.3 %all-gather.2 = f32[4,2,24,128]{3,2,1,0:T(8,128)S(1)} all-gather(f32[2,2,24,128]{3,2,1,0:T(8,128)S(1)} %pad_maximum_fusion.2), channel_id=4, replica_groups=mesh['gx'=64,'gy'=4,'ga'=2] {'ga'}, dimensions={0}, use_global_device_ids=true | all-gather | bytes 147456 | tf_op jit(solution)/shard_map/all_gather | solution.py:757
  67.6 4.8 %collective-permute-start.5 = (f32[24,128]{1,0:T(8,128)S(1)}, f32[24,128]{1,0:T(8,128)S(1)}, u32[]{:S(2)}, u32[]{:S(2)}) collective-permute-start(f32[24,128]{1,0:T(8,128)S(1)} %get-tuple-element.59), channel_id=1, source_target_pairs={{0,8},{8,16},{16,24},{24,32},{32,40},{40,48},{48,56},{56,64},{64,7... | collective-permute-start | bytes 36872 | tf_op jit(solution)/shard_map/ppermute | solution.py:719
  73.2 4.1 %all-gather.3 = f32[96,128]{1,0:T(8,128)S(1)} all-gather(f32[48,128]{1,0:T(8,128)S(1)} %pad_maximum_fusion.7), channel_id=5, replica_groups={{0,2},{4,6},{1,3},{5,7},{8,10},{12,14},{9,11},{13,15},{16,18},{20,22},{..., dimensions={0}, use_global_device_ids=true | all-gather | bytes 73728 | tf_op jit(solution)/shard_map/all_gather | solution.py:730
  77.3 5.1 %all-gather.4 = f32[4,48,128]{2,1,0:T(8,128)S(1)} all-gather(f32[2,48,128]{2,1,0:T(8,128)S(1)} %bitcast.49), channel_id=6, replica_groups={{0,4},{2,6},{1,5},{3,7},{8,12},{10,14},{9,13},{11,15},{16,20},{18,22},{..., dimensions={0}, use_global_device_ids=true | all-gather | bytes 147456 | tf_op jit(solution)/shard_map/all_gather | solution.py:731
  82.4 5.6 %all-gather.12 = f32[8,48,128]{2,1,0:T(8,128)S(1)} all-gather(f32[4,48,128]{2,1,0:T(8,128)S(1)} %all-gather.4), channel_id=14, replica_groups=mesh['gx'=64,'gy'=4,'ga'=2] {'ga'}, dimensions={0}, use_global_device_ids=true | all-gather | bytes 294912 | tf_op jit(solution)/shard_map/all_gather | solution.py:732
  91.8 3.3 %collective-permute-start.9 = (f32[8,8,128]{2,1,0:T(8,128)S(1)}, f32[8,8,128]{2,1,0:T(8,128)S(1)}, u32[]{:S(2)}, u32[]{:S(2)}) collective-permute-start(f32[8,8,128]{2,1,0:T(8,128)S(1)} %get-tuple-element.68.mid), channel_id=1, source_target_pairs={{8,0},{16,8},{24,16},{32,24},{40,32},{48,40},{56,48},{64,56},{72,6... | collective-permute-start | bytes 98312 | tf_op jit(solution)/shard_map/ppermute | solution.py:714
  95.0 2.0 collective-permute-start.8
  97.1 10.6 %all-gather.19.cloned.1.call-done = f32[608,8,128]{2,1,0:T(8,128)} async-done(((f32[76,8,128]{2,1,0:T(8,128)}), f32[608,8,128]{2,1,0:T(8,128)}) %all-gather.19.cloned.1.call-update) | async-done | bytes 2490384 | tf_op jit(solution)/shard_map/all_gather | solution.py:785
  110.7 7.6 %collective-permute-start.10 = (f32[56,128]{1,0:T(8,128)S(1)}, f32[56,128]{1,0:T(8,128)S(1)}, u32[]{:S(2)}, u32[]{:S(2)}) collective-permute-start(f32[56,128]{1,0:T(8,128)S(1)} %get-tuple-element.70.mine), channel_id=1, source_target_pairs={{32,0},{40,8},{48,16},{56,24},{64,32},{72,40},{80,48},{88,56},{96,... | collective-permute-start | bytes 86024 | tf_op jit(solution)/shard_map/ppermute | solution.py:726
  118.3 7.3 %collective-permute-start.11 = (f32[8,128]{1,0:T(8,128)S(1)}, f32[8,128]{1,0:T(8,128)S(1)}, u32[]{:S(2)}, u32[]{:S(2)}) collective-permute-start(f32[8,128]{1,0:T(8,128)S(1)} %slice.3), channel_id=1, source_target_pairs={{64,0},{72,8},{80,16},{88,24},{96,32},{104,40},{112,48},{120,56},{... | collective-permute-start | bytes 12296 | tf_op jit(solution)/shard_map/ppermute | solution.py:726
  125.5 3.7 %collective-permute-done.11 = f32[8,128]{1,0:T(8,128)S(1)} collective-permute-done((f32[8,128]{1,0:T(8,128)S(1)}, f32[8,128]{1,0:T(8,128)S(1)}, u32[]{:S(2)}, u32[]{:S(2)}) %collective-permute-start.11) | collective-permute-done | bytes 4128 | tf_op jit(solution)/shard_map/ppermute | solution.py:726
  129.2 3.7 %all-gather.7 = f32[128,128]{1,0:T(8,128)S(1)} all-gather(f32[64,128]{1,0:T(8,128)S(1)} %pad_maximum_fusion.6), channel_id=9, replica_groups={{0,2},{4,6},{1,3},{5,7},{8,10},{12,14},{9,11},{13,15},{16,18},{20,22},{..., dimensions={0}, use_global_device_ids=true | all-gather | bytes 98304 | tf_op jit(solution)/shard_map/all_gather | solution.py:730
  133.0 6.0 %all-gather.8 = f32[4,64,128]{2,1,0:T(8,128)S(1)} all-gather(f32[2,64,128]{2,1,0:T(8,128)S(1)} %bitcast.48), channel_id=10, replica_groups={{0,4},{2,6},{1,5},{3,7},{8,12},{10,14},{9,13},{11,15},{16,20},{18,22},{..., dimensions={0}, use_global_device_ids=true | all-gather | bytes 196608 | tf_op jit(solution)/shard_map/all_gather | solution.py:731
  138.9 7.6 %all-gather.13 = f32[8,64,128]{2,1,0:T(8,128)S(1)} all-gather(f32[4,64,128]{2,1,0:T(8,128)S(1)} %all-gather.8), channel_id=15, replica_groups=mesh['gx'=64,'gy'=4,'ga'=2] {'ga'}, dimensions={0}, use_global_device_ids=true | all-gather | bytes 393216 | tf_op jit(solution)/shard_map/all_gather | solution.py:732
  146.5 2.0 copy-done.8
  149.8 2.8 %shard_map.139 = (f32[24,8,128]{2,1,0:T(8,128)S(1)}, f32[12,8,128]{2,1,0:T(8,128)S(1)}, f32[12,8,128]{2,1,0:T(8,128)S(1)}) custom-call(s32[5]{0:T(128)S(1)} %stack.67.ids, f32[2,4,64,128]{3,2,1,0:T(8,128)S(1)} %bitcast.41, f32[56,128]{1,0:T(8,128)S(1)} %get-tuple-element.70.mine, f32[3,40,128]{2,1,0:T(8,128)S(1)} %copy-done.19, ...), custom_call_target="tpu_custom_call" | custom-call | tf_op jit(solution)/shard_map/pallas_call | solution.py:703
  152.6 2.3 %collective-permute-start.12 = (f32[12,8,128]{2,1,0:T(8,128)S(1)}, f32[12,8,128]{2,1,0:T(8,128)S(1)}, u32[]{:S(2)}, u32[]{:S(2)}) collective-permute-start(f32[12,8,128]{2,1,0:T(8,128)S(1)} %get-tuple-element.76), channel_id=1, source_target_pairs={{0,8},{8,16},{16,24},{24,32},{32,40},{40,48},{48,56},{56,64},{64,7... | collective-permute-start | bytes 147464 | tf_op jit(solution)/shard_map/ppermute | solution.py:714
  154.9 5.1 %collective-permute-start.13 = (f32[12,8,128]{2,1,0:T(8,128)S(1)}, f32[12,8,128]{2,1,0:T(8,128)S(1)}, u32[]{:S(2)}, u32[]{:S(2)}) collective-permute-start(f32[12,8,128]{2,1,0:T(8,128)S(1)} %get-tuple-element.78), channel_id=1, source_target_pairs={{8,0},{16,8},{24,16},{32,24},{40,32},{48,40},{56,48},{64,56},{72,6... | collective-permute-start | bytes 147464 | tf_op jit(solution)/shard_map/ppermute | solution.py:714
  162.7 5.8 %collective-permute-start.14 = (f32[2,24,128]{2,1,0:T(8,128)S(1)}, f32[2,24,128]{2,1,0:T(8,128)S(1)}, u32[]{:S(2)}, u32[]{:S(2)}) collective-permute-start(f32[2,24,128]{2,1,0:T(8,128)S(1)} %get-tuple-element.83), channel_id=1, source_target_pairs={{0,8},{8,16},{16,24},{24,32},{32,40},{40,48},{48,56},{56,64},{64,7... | collective-permute-start | bytes 73736 | tf_op jit(solution)/shard_map/ppermute | solution.py:719
  169.8 3.3 %collective-permute-done.15 = f32[2,24,128]{2,1,0:T(8,128)S(1)} collective-permute-done((f32[2,24,128]{2,1,0:T(8,128)S(1)}, f32[2,24,128]{2,1,0:T(8,128)S(1)}, u32[]{:S(2)}, u32[]{:S(2)}) %collective-permute-start.15) | collective-permute-done | bytes 24608 | tf_op jit(solution)/shard_map/ppermute | solution.py:719
  176.1 2.6 %collective-permute-start.16 = (f32[2,24,128]{2,1,0:T(8,128)S(1)}, f32[2,24,128]{2,1,0:T(8,128)S(1)}, u32[]{:S(2)}, u32[]{:S(2)}) collective-permute-start(f32[2,24,128]{2,1,0:T(8,128)S(1)} %get-tuple-element.87), channel_id=1, source_target_pairs={{0,8},{8,16},{16,24},{24,32},{32,40},{40,48},{48,56},{56,64},{64,7... | collective-permute-start | bytes 73736 | tf_op jit(solution)/shard_map/ppermute | solution.py:719
  180.6 3.0 %collective-permute-done.17 = f32[2,24,128]{2,1,0:T(8,128)S(1)} collective-permute-done((f32[2,24,128]{2,1,0:T(8,128)S(1)}, f32[2,24,128]{2,1,0:T(8,128)S(1)}, u32[]{:S(2)}, u32[]{:S(2)}) %collective-permute-start.17) | collective-permute-done | bytes 24608 | tf_op jit(solution)/shard_map/ppermute | solution.py:719
  187.4 3.3 %collective-permute-start.18 = (f32[2,24,128]{2,1,0:T(8,128)S(1)}, f32[2,24,128]{2,1,0:T(8,128)S(1)}, u32[]{:S(2)}, u32[]{:S(2)}) collective-permute-start(f32[2,24,128]{2,1,0:T(8,128)S(1)} %get-tuple-element.92), channel_id=1, source_target_pairs={{0,8},{8,16},{16,24},{24,32},{32,40},{40,48},{48,56},{56,64},{64,7... | collective-permute-start | bytes 73736 | tf_op jit(solution)/shard_map/ppermute | solution.py:719
  192.1 3.8 %collective-permute-done.19 = f32[2,24,128]{2,1,0:T(8,128)S(1)} collective-permute-done((f32[2,24,128]{2,1,0:T(8,128)S(1)}, f32[2,24,128]{2,1,0:T(8,128)S(1)}, u32[]{:S(2)}, u32[]{:S(2)}) %collective-permute-start.19) | collective-permute-done | bytes 24608 | tf_op jit(solution)/shard_map/ppermute | solution.py:719
  (98 shorter events, 50.3 us)
Async XLA Ops:
  7.2 4.3 %copy-start.22 = (f32[3,2,4,32]{3,2,1,0:T(4,128)S(1)}, f32[3,2,4,32]{3,2,1,0:T(4,128)}, u32[]{:S(2)}) copy-start(f32[3,2,4,32]{3,2,1,0:T(4,128)} %cs.1) | copy-start | bytes 9220
  7.2 80.8 %all-gather.17.cloned.1.call-start = ((), (), s32[]{:S(2)}) async-start(), calls=%async_computation | async-start | bytes 4055040 | tf_op jit(solution)/shard_map/all_gather | solution.py:784
  8.9 23.7 %copy-start.14 = (f32[3,3,8,8,128]{4,3,2,1,0:T(8,128)S(1)}, f32[3,3,8,8,128]{4,3,2,1,0:T(8,128)}, u32[]{:S(2)}) copy-start(f32[3,3,8,8,128]{4,3,2,1,0:T(8,128)} %prolong.1) | copy-start | bytes 884740
  9.3 23.2 %copy-start.13 = (bf16[7,3,3,8,8,128]{5,4,3,2,1,0:T(8,128)(2,1)S(1)}, bf16[7,3,3,8,8,128]{5,4,3,2,1,0:T(8,128)(2,1)}, u32[]{:S(2)}) copy-start(bf16[7,3,3,8,8,128]{5,4,3,2,1,0:T(8,128)(2,1)} %couple.1) | copy-start | bytes 3096580
  11.4 7.8 %copy-start.18 = (f32[3,40,128]{2,1,0:T(8,128)}, f32[3,40,128]{2,1,0:T(8,128)S(1)}, u32[]{:S(2)}) copy-start(f32[3,40,128]{2,1,0:T(8,128)S(1)} %get-tuple-element.71.bottom_stiff) | copy-start | bytes 184324
  15.6 19.1 %collective-permute-start.6 = (f32[73,4,128]{2,1,0:T(4,128)S(1)}, f32[73,4,128]{2,1,0:T(4,128)S(1)}, u32[]{:S(2)}, u32[]{:S(2)}) collective-permute-start(f32[73,4,128]{2,1,0:T(4,128)S(1)} %get-tuple-element.62), channel_id=1, source_target_pairs={{0,8},{8,16},{16,24},{24,32},{32,40},{40,48},{48,56},{56,64},{64,7... | collective-permute-start | bytes 448520 | tf_op jit(solution)/shard_map/ppermute | solution.py:714
  19.2 15.5 %collective-permute-start.7 = (f32[73,4,128]{2,1,0:T(4,128)S(1)}, f32[73,4,128]{2,1,0:T(4,128)S(1)}, u32[]{:S(2)}, u32[]{:S(2)}) collective-permute-start(f32[73,4,128]{2,1,0:T(4,128)S(1)} %get-tuple-element.63), channel_id=1, source_target_pairs={{8,0},{16,8},{24,16},{32,24},{40,32},{48,40},{56,48},{64,56},{72,6... | collective-permute-start | bytes 448520 | tf_op jit(solution)/shard_map/ppermute | solution.py:714
  36.4 71.3 %all-gather.19.cloned.1.call-start = ((), (), s32[]{:S(2)}) async-start(), calls=%async_computation.1 | async-start | bytes 2801664 | tf_op jit(solution)/shard_map/all_gather | solution.py:785
  37.1 15.2 %collective-permute-start.2 = (f32[576,8,128]{2,1,0:T(8,128)}, f32[576,8,128]{2,1,0:T(8,128)S(1)}, u32[]{:S(2)}, u32[]{:S(2)}) collective-permute-start(f32[576,8,128]{2,1,0:T(8,128)} %copy-done.1), channel_id=1, source_target_pairs={{0,1},{1,0},{2,3},{3,2},{4,5},{5,4},{6,7},{7,6},{8,9},{9,8},{10,11... | collective-permute-start | bytes 7077896 | tf_op jit(solution)/shard_map/ppermute | solution.py:781
  39.4 5.4 %collective-permute-start.1 = (f32[2,24,128]{2,1,0:T(8,128)S(1)}, f32[2,24,128]{2,1,0:T(8,128)S(1)}, u32[]{:S(2)}, u32[]{:S(2)}) collective-permute-start(f32[2,24,128]{2,1,0:T(8,128)S(1)} %get-tuple-element.52), channel_id=1, source_target_pairs={{0,2},{2,4},{4,6},{3,1},{5,3},{7,5},{8,10},{10,12},{12,14},{11,9},... | collective-permute-start | bytes 73736 | tf_op jit(solution)/shard_map/ppermute | solution.py:719
  40.7 5.0 %collective-permute-start = (f32[2,24,128]{2,1,0:T(8,128)S(1)}, f32[2,24,128]{2,1,0:T(8,128)S(1)}, u32[]{:S(2)}, u32[]{:S(2)}) collective-permute-start(f32[2,24,128]{2,1,0:T(8,128)S(1)} %get-tuple-element.51), channel_id=1, source_target_pairs={{0,8},{8,16},{16,24},{24,32},{32,40},{40,48},{48,56},{56,64},{64,7... | collective-permute-start | bytes 73736 | tf_op jit(solution)/shard_map/ppermute | solution.py:719
  52.3 13.4 %copy-start.5 = (f32[576,8,128]{2,1,0:T(8,128)}, f32[576,8,128]{2,1,0:T(8,128)S(1)}, u32[]{:S(2)}) copy-start(f32[576,8,128]{2,1,0:T(8,128)S(1)} %collective-permute-done.2.other) | copy-start | bytes 7077892
  54.9 10.9 %copy-start.3 = (f32[576,8,128]{2,1,0:T(8,128)S(1)}, f32[576,8,128]{2,1,0:T(8,128)}, u32[]{:S(2)}) copy-start(f32[576,8,128]{2,1,0:T(8,128)} %copy-done.1) | copy-start | bytes 7077892
  56.0 5.0 %collective-permute-start.3 = (f32[2,24,128]{2,1,0:T(8,128)S(1)}, f32[2,24,128]{2,1,0:T(8,128)S(1)}, u32[]{:S(2)}, u32[]{:S(2)}) collective-permute-start(f32[2,24,128]{2,1,0:T(8,128)S(1)} %get-tuple-element.56), channel_id=1, source_target_pairs={{0,8},{8,16},{16,24},{24,32},{32,40},{40,48},{48,56},{56,64},{64,7... | collective-permute-start | bytes 73736 | tf_op jit(solution)/shard_map/ppermute | solution.py:719
  58.0 5.5 %collective-permute-start.4 = (f32[2,24,128]{2,1,0:T(8,128)S(1)}, f32[2,24,128]{2,1,0:T(8,128)S(1)}, u32[]{:S(2)}, u32[]{:S(2)}) collective-permute-start(f32[2,24,128]{2,1,0:T(8,128)S(1)} %get-tuple-element.57), channel_id=1, source_target_pairs={{0,2},{2,4},{4,6},{3,1},{5,3},{7,5},{8,10},{10,12},{12,14},{11,9},... | collective-permute-start | bytes 73736 | tf_op jit(solution)/shard_map/ppermute | solution.py:719
  67.6 5.6 %collective-permute-start.5 = (f32[24,128]{1,0:T(8,128)S(1)}, f32[24,128]{1,0:T(8,128)S(1)}, u32[]{:S(2)}, u32[]{:S(2)}) collective-permute-start(f32[24,128]{1,0:T(8,128)S(1)} %get-tuple-element.59), channel_id=1, source_target_pairs={{0,8},{8,16},{16,24},{24,32},{32,40},{40,48},{48,56},{56,64},{64,7... | collective-permute-start | bytes 36872 | tf_op jit(solution)/shard_map/ppermute | solution.py:719
  90.0 56.5 %copy-start.19 = (f32[3,40,128]{2,1,0:T(8,128)S(1)}, f32[3,40,128]{2,1,0:T(8,128)}, u32[]{:S(2)}) copy-start(f32[3,40,128]{2,1,0:T(8,128)} %copy-done.18) | copy-start | bytes 184324
  91.8 15.9 %collective-permute-start.9 = (f32[8,8,128]{2,1,0:T(8,128)S(1)}, f32[8,8,128]{2,1,0:T(8,128)S(1)}, u32[]{:S(2)}, u32[]{:S(2)}) collective-permute-start(f32[8,8,128]{2,1,0:T(8,128)S(1)} %get-tuple-element.68.mid), channel_id=1, source_target_pairs={{8,0},{16,8},{24,16},{32,24},{40,32},{48,40},{56,48},{64,56},{72,6... | collective-permute-start | bytes 98312 | tf_op jit(solution)/shard_map/ppermute | solution.py:714
  95.0 12.6 %collective-permute-start.8 = (f32[8,8,128]{2,1,0:T(8,128)S(1)}, f32[8,8,128]{2,1,0:T(8,128)S(1)}, u32[]{:S(2)}, u32[]{:S(2)}) collective-permute-start(f32[8,8,128]{2,1,0:T(8,128)S(1)} %get-tuple-element.68.mid), channel_id=1, source_target_pairs={{0,8},{8,16},{16,24},{24,32},{32,40},{40,48},{48,56},{56,64},{64,7... | collective-permute-start | bytes 98312 | tf_op jit(solution)/shard_map/ppermute | solution.py:714
  109.4 37.1 %copy-start.10 = (f32[608,8,128]{2,1,0:T(8,128)S(1)}, f32[608,8,128]{2,1,0:T(8,128)}, u32[]{:S(2)}) copy-start(f32[608,8,128]{2,1,0:T(8,128)} %all-gather.19.cloned.1.call-done) | copy-start | bytes 7471108
  110.7 18.5 %collective-permute-start.10 = (f32[56,128]{1,0:T(8,128)S(1)}, f32[56,128]{1,0:T(8,128)S(1)}, u32[]{:S(2)}, u32[]{:S(2)}) collective-permute-start(f32[56,128]{1,0:T(8,128)S(1)} %get-tuple-element.70.mine), channel_id=1, source_target_pairs={{32,0},{40,8},{48,16},{56,24},{64,32},{72,40},{80,48},{88,56},{96,... | collective-permute-start | bytes 86024 | tf_op jit(solution)/shard_map/ppermute | solution.py:726
  118.3 11.0 %collective-permute-start.11 = (f32[8,128]{1,0:T(8,128)S(1)}, f32[8,128]{1,0:T(8,128)S(1)}, u32[]{:S(2)}, u32[]{:S(2)}) collective-permute-start(f32[8,128]{1,0:T(8,128)S(1)} %slice.3), channel_id=1, source_target_pairs={{64,0},{72,8},{80,16},{88,24},{96,32},{104,40},{112,48},{120,56},{... | collective-permute-start | bytes 12296 | tf_op jit(solution)/shard_map/ppermute | solution.py:726
  149.8 11.4 %copy-start.4 = (f32[576,8,128]{2,1,0:T(8,128)S(1)}, f32[576,8,128]{2,1,0:T(8,128)}, u32[]{:S(2)}) copy-start(f32[576,8,128]{2,1,0:T(8,128)} %copy-done.1) | copy-start | bytes 7077892
  149.8 11.4 %copy-start.6 = (f32[576,8,128]{2,1,0:T(8,128)S(1)}, f32[576,8,128]{2,1,0:T(8,128)}, u32[]{:S(2)}) copy-start(f32[576,8,128]{2,1,0:T(8,128)} %copy-done.5) | copy-start | bytes 7077892
  152.6 7.4 %collective-permute-start.12 = (f32[12,8,128]{2,1,0:T(8,128)S(1)}, f32[12,8,128]{2,1,0:T(8,128)S(1)}, u32[]{:S(2)}, u32[]{:S(2)}) collective-permute-start(f32[12,8,128]{2,1,0:T(8,128)S(1)} %get-tuple-element.76), channel_id=1, source_target_pairs={{0,8},{8,16},{16,24},{24,32},{32,40},{40,48},{48,56},{56,64},{64,7... | collective-permute-start | bytes 147464 | tf_op jit(solution)/shard_map/ppermute | solution.py:714
  154.9 6.3 %collective-permute-start.13 = (f32[12,8,128]{2,1,0:T(8,128)S(1)}, f32[12,8,128]{2,1,0:T(8,128)S(1)}, u32[]{:S(2)}, u32[]{:S(2)}) collective-permute-start(f32[12,8,128]{2,1,0:T(8,128)S(1)} %get-tuple-element.78), channel_id=1, source_target_pairs={{8,0},{16,8},{24,16},{32,24},{40,32},{48,40},{56,48},{64,56},{72,6... | collective-permute-start | bytes 147464 | tf_op jit(solution)/shard_map/ppermute | solution.py:714
  162.7 7.1 %collective-permute-start.14 = (f32[2,24,128]{2,1,0:T(8,128)S(1)}, f32[2,24,128]{2,1,0:T(8,128)S(1)}, u32[]{:S(2)}, u32[]{:S(2)}) collective-permute-start(f32[2,24,128]{2,1,0:T(8,128)S(1)} %get-tuple-element.83), channel_id=1, source_target_pairs={{0,8},{8,16},{16,24},{24,32},{32,40},{40,48},{48,56},{56,64},{64,7... | collective-permute-start | bytes 73736 | tf_op jit(solution)/shard_map/ppermute | solution.py:719
  168.5 4.6 %collective-permute-start.15 = (f32[2,24,128]{2,1,0:T(8,128)S(1)}, f32[2,24,128]{2,1,0:T(8,128)S(1)}, u32[]{:S(2)}, u32[]{:S(2)}) collective-permute-start(f32[2,24,128]{2,1,0:T(8,128)S(1)} %get-tuple-element.84), channel_id=1, source_target_pairs={{0,2},{2,4},{4,6},{3,1},{5,3},{7,5},{8,10},{10,12},{12,14},{11,9},... | collective-permute-start | bytes 73736 | tf_op jit(solution)/shard_map/ppermute | solution.py:719
  176.1 4.6 %collective-permute-start.16 = (f32[2,24,128]{2,1,0:T(8,128)S(1)}, f32[2,24,128]{2,1,0:T(8,128)S(1)}, u32[]{:S(2)}, u32[]{:S(2)}) collective-permute-start(f32[2,24,128]{2,1,0:T(8,128)S(1)} %get-tuple-element.87), channel_id=1, source_target_pairs={{0,8},{8,16},{16,24},{24,32},{32,40},{40,48},{48,56},{56,64},{64,7... | collective-permute-start | bytes 73736 | tf_op jit(solution)/shard_map/ppermute | solution.py:719
  178.7 5.0 %collective-permute-start.17 = (f32[2,24,128]{2,1,0:T(8,128)S(1)}, f32[2,24,128]{2,1,0:T(8,128)S(1)}, u32[]{:S(2)}, u32[]{:S(2)}) collective-permute-start(f32[2,24,128]{2,1,0:T(8,128)S(1)} %get-tuple-element.88), channel_id=1, source_target_pairs={{0,2},{2,4},{4,6},{3,1},{5,3},{7,5},{8,10},{10,12},{12,14},{11,9},... | collective-permute-start | bytes 73736 | tf_op jit(solution)/shard_map/ppermute | solution.py:719
  187.4 4.6 %collective-permute-start.18 = (f32[2,24,128]{2,1,0:T(8,128)S(1)}, f32[2,24,128]{2,1,0:T(8,128)S(1)}, u32[]{:S(2)}, u32[]{:S(2)}) collective-permute-start(f32[2,24,128]{2,1,0:T(8,128)S(1)} %get-tuple-element.92), channel_id=1, source_target_pairs={{0,8},{8,16},{16,24},{24,32},{32,40},{40,48},{48,56},{56,64},{64,7... | collective-permute-start | bytes 73736 | tf_op jit(solution)/shard_map/ppermute | solution.py:719
  190.8 5.1 %collective-permute-start.19 = (f32[2,24,128]{2,1,0:T(8,128)S(1)}, f32[2,24,128]{2,1,0:T(8,128)S(1)}, u32[]{:S(2)}, u32[]{:S(2)}) collective-permute-start(f32[2,24,128]{2,1,0:T(8,128)S(1)} %get-tuple-element.93), channel_id=1, source_target_pairs={{0,2},{2,4},{4,6},{3,1},{5,3},{7,5},{8,10},{10,12},{12,14},{11,9},... | collective-permute-start | bytes 73736 | tf_op jit(solution)/shard_map/ppermute | solution.py:719
  (13 other events, 21.5 us)
Sparse Core Ops, SparseCore 0:
  36.5 35.1 all-gather.16
  73.8 33.7 all-gather.18

commit v5 on v4

--- a/solution.py
+++ b/solution.py
@@ -664,9 +664,15 @@
 
     for t in range(38):
         both = jnp.concatenate(low(2 * t) + low(2 * t + 1), axis=1)
-        up[35 + t] = both
-        down[35 + t] = both
         coarse[t] = both
+    for t in range(16):
+        four = [low(i) if i < 63 else low(75) for i in range(4 * t, 4 * t + 4)]
+        up[35 + t] = jnp.concatenate([v[1] for v in four], axis=1)
+        down[35 + t] = jnp.concatenate([v[0] for v in four], axis=1)
+    for t in range(6):
+        both = jnp.concatenate(low(63 + 2 * t) + low(64 + 2 * t), axis=1)
+        up[51 + t] = both
+        down[51 + t] = both
 
 
     for i in range(75):
@@ -686,13 +692,42 @@
     for t in range(35):
         one[75 + t, 0:4, :] = low[t]
         one[75 + t, 4:8, :] = high[t]
-    lane = iota((4, 128), 1)
-    for t in range(38):
-        under, here, over = low[35 + t], coarse[t], high[35 + t]
-        two[2 * t, 0:4, :] = jnp.where(lane < 64, under, pltpu.roll(here, 64, 1))
-        two[2 * t, 4:8, :] = jnp.where(lane < 64, over, 0.0)
-        two[2 * t + 1, 0:4, :] = jnp.where(lane < 64, pltpu.roll(under, 64, 1), here)
-        two[2 * t + 1, 4:8, :] = jnp.where(lane < 64, pltpu.roll(over, 64, 1), 0.0)
+    for t in range(19):
+        two[t, 0:4, :] = coarse[2 * t]
+        two[t, 4:8, :] = coarse[2 * t + 1]
+    for t in range(22):
+        two[19 + t, 0:4, :] = low[35 + t]
+        two[19 + t, 4:8, :] = high[35 + t]
+
+
+def unpack_coarse(ids, packed, fields):
+    row, lane = rows8(), lanes8()
+    own = (row < 4) & (lane >= 64)
+    free = (row >= 4) & (lane >= 64)
+
+    def turned(v, shift):
+        return pltpu.roll(v, shift % 128, 1) if shift % 128 else v
+
+    def block(g, carry):
+        for f in range(75):
+            i = f % 4
+            mine = packed[g, f // 4]
+            if i // 2:
+                mine = pltpu.roll(mine, 4, 0)
+            if i % 2 == 0:
+                mine = turned(mine, 64)
+            if f < 63:
+                v = packed[g, 19 + f // 4]
+                edges = jnp.where(row < 4, turned(v, 32 - 32 * i), turned(v, -32 * i))
+            else:
+                edges = turned(packed[g, 35 + (f - 63) // 2], 64 * ((f - 63) % 2))
+            v = jnp.where(own, mine, edges)
+            if 63 <= f < 66:
+                v = jnp.where(free, 1.0, v)
+            fields[g, f] = v
+        return carry
+
+    lax.fori_loop(0, 8, block, 0)
 
 
 VMEM = pl.BlockSpec(memory_space=pltpu.VMEM)
@@ -762,14 +797,13 @@
 
     cut = lax.dynamic_slice_in_dim(bottom_stiff, start * 128, span * 256, 1)
     cut_couple = lax.dynamic_slice_in_dim(bottom_couple, start * 128, span * 256, 3)
-    bottom_s, bottom_c = run(bottom_window, ids, [cut, cut_couple], [(3, ROWS, 128), (63, ROWS, 128)])
-    right_side, middle_stiff, bottom_s = lax.optimization_barrier((right_side, middle_stiff, bottom_s))
+    right_side, middle_stiff, cut = lax.optimization_barrier((right_side, middle_stiff, cut))
 
     up, down, coarse, body = run(
         pack_edges,
         ids,
         [middle_couple, middle_stiff, middle_prolong, coarse_couple, coarse_stiff, coarse_prolong],
-        [(73, 4, 128), (73, 4, 128), (38, 4, 128), (75, 8, 128)],
+        [(57, 4, 128), (57, 4, 128), (38, 4, 128), (75, 8, 128)],
     )
     below, above = shifted(up, "gx", count, 1), shifted(down, "gx", count, -1)
 
@@ -780,10 +814,11 @@
     swap = [(0, 1), (1, 0)]
     other = lax.ppermute(own, "ga", swap)
     below, above, _ = lax.optimization_barrier((below, above, xs))
-    one, two = run(pack_levels, ids, [body, below, above, coarse], [(110, 8, 128), (76, 8, 128)])
+    one, two = run(pack_levels, ids, [body, below, above, coarse], [(110, 8, 128), (41, 8, 128)])
     packed1 = lax.all_gather(one, ("gy", "ga"))
+    halo = exchange(xs, ys)
+    two, _ = lax.optimization_barrier((two, halo))
     packed2 = lax.all_gather(two, ("gy", "ga"))
-    halo = exchange(xs, ys)
     rest, second, xs, ys = run(fine_second, ids, [ls, first, halo, own, other], [half, half, edge, edge])
     halo = exchange(xs, ys)
     pre0, keep, send = run(
@@ -797,15 +832,19 @@
     )
     low, high = shifted(load2, "gx", count, 1), shifted(load2, "gx", count, -1)
 
+    cut, cut_couple, packed2, _ = lax.optimization_barrier((cut, cut_couple, packed2, load2))
+    bottom_s, bottom_c = run(bottom_window, ids, [cut, cut_couple], [(3, ROWS, 128), (63, ROWS, 128)])
+    (fields2,) = run(unpack_coarse, ids, [packed2], [(8, 75, 8, 128)])
+
     load2, pre2, mine = run(
-        coarse_down, ids, [low, load2, high, packed2], [tiles, tiles, (56, 128)], [tiles] * 4
+        coarse_down, ids, [low, load2, high, fields2], [tiles, tiles, (56, 128)], [tiles] * 4
     )
     got = group_gather(jnp.concatenate([skewed(mine, count, SHIFTS[0]), skewed(mine[:8], count, SHIFTS[1])]))
 
     guess1, lower, upper = run(
         bottom_and_up,
         ids,
-        [got, mine, bottom_s, bottom_c, load2, pre2, packed2, pre1, packed1],
+        [got, mine, bottom_s, bottom_c, load2, pre2, fields2, pre1, packed1],
         [tiles, (12, 8, 128), (12, 8, 128)],
         [(3, ROWS, 128), (3, ROWS, 128), tiles, tiles, tiles, tiles],
     )

time: 208 us -> 210 us (level)
  Pallas kernels: 19 us -> 28.2 us
  waiting for transfers between devices: 32.8 us -> 24.5 us
    pallas_call x13 -> x14, Pallas kernels: 19 us -> 28.2 us  [run(): pl.pallas_call(kernel, out_shape=[jax.ShapeDtypeStruct(s, F32) for s in o...]
    all_gather x1, waiting for transfers between devices: 10.6 us -> 3.99 us  [local(): packed2 = lax.all_gather(two, ('gy', 'ga'))]
    unnamed x47 -> x54, local copies, waits for them, and re-layouts: 16.4 us -> 17.3 us
  transfers between devices with their start and end apart: 22 -> 22, of which waited for: 11 -> 11; matrix products, arithmetic and copies ran while one was open for 0% -> 1% of each run, Pallas kernels for 3% -> 6%
where the time goes in v5:
time: 210 us; the launch traced here: 208 us
  starting transfers between devices  71.6 us (34%)
  blocking collectives  49.7 us (24%)
  Pallas kernels  28.2 us (13%)
  waiting for transfers between devices  24.5 us (12%)
  local copies, waits for them, and re-layouts  18.8 us (9%)
  between operations  14.5 us (7%)
    ppermute x11, starting transfers between devices, split_shift(): return lax.ppermute(value, (axis, 'ga'), pairs)  28.5 us
    pallas_call x14, Pallas kernels, run(): pl.pallas_call(kernel, out_shape=[jax.ShapeDtypeStruct(s, F32) for s in o...  28.2 us
    ppermute x6, starting transfers between devices, shifted(): lax.ppermute(value, axis, [(i, i + shift) for i in range(count) if 0 <= i...  25.9 us
    unnamed x54, local copies, waits for them, and re-layouts  17.3 us
    ppermute x11, waiting for transfers between devices, split_shift(): return lax.ppermute(value, (axis, 'ga'), pairs)  16.6 us
    all_gather x5, blocking collectives, exchange(): return lax.all_gather(both, 'ga')  15 us
    ppermute x2, starting transfers between devices, skewed(): return lax.ppermute(value, ('gx', 'gy', 'ga'), pairs)  14.8 us
    all_gather x2, blocking collectives, group_gather(): return lax.all_gather(four.reshape((4,) + value.shape), 'ga')  13.8 us
  transfers between devices with their start and end apart: 22, of which 11 were waited for; matrix products, arithmetic and copies ran while one was open for 1% of the time, Pallas kernels for 6%

profile of v5, /device:TPU:25, one launch (start us, length us, event | category | flops | bytes accessed | tf_op | source)
XLA Modules:
  0.0 208.1 jit_solution(15072760116291671964)
XLA Ops:
  14.2 3.5 %collective-permute-start.6 = (f32[57,4,128]{2,1,0:T(4,128)S(1)}, f32[57,4,128]{2,1,0:T(4,128)S(1)}, u32[]{:S(2)}, u32[]{:S(2)}) collective-permute-start(f32[57,4,128]{2,1,0:T(4,128)S(1)} %get-tuple-element.65), channel_id=1, source_target_pairs={{0,8},{8,16},{16,24},{24,32},{32,40},{40,48},{48,56},{56,64},{64,7... | collective-permute-start | bytes 350216 | tf_op jit(solution)/shard_map/ppermute | solution.py:749
  17.8 9.7 %collective-permute-start.7 = (f32[57,4,128]{2,1,0:T(4,128)S(1)}, f32[57,4,128]{2,1,0:T(4,128)S(1)}, u32[]{:S(2)}, u32[]{:S(2)}) collective-permute-start(f32[57,4,128]{2,1,0:T(4,128)S(1)} %get-tuple-element.66), channel_id=1, source_target_pairs={{8,0},{16,8},{24,16},{32,24},{40,32},{48,40},{56,48},{64,56},{72,6... | collective-permute-start | bytes 350216 | tf_op jit(solution)/shard_map/ppermute | solution.py:749
  28.4 2.7 %all-gather = f32[4,24,8,128]{3,2,1,0:T(8,128)S(1)} all-gather(f32[2,24,8,128]{3,2,1,0:T(8,128)S(1)} %pad_maximum_fusion), channel_id=2, replica_groups=mesh['gx'=64,'gy'=4,'ga'=2] {'ga'}, dimensions={0}, use_global_device_ids=true | all-gather | bytes 589824 | tf_op jit(solution)/shard_map/all_gather | solution.py:810
  40.6 3.6 %collective-permute-start = (f32[2,24,128]{2,1,0:T(8,128)S(1)}, f32[2,24,128]{2,1,0:T(8,128)S(1)}, u32[]{:S(2)}, u32[]{:S(2)}) collective-permute-start(f32[2,24,128]{2,1,0:T(8,128)S(1)} %get-tuple-element.54), channel_id=1, source_target_pairs={{0,8},{8,16},{16,24},{24,32},{32,40},{40,48},{48,56},{56,64},{64,7... | collective-permute-start | bytes 73736 | tf_op jit(solution)/shard_map/ppermute | solution.py:754
  45.2 7.0 %all-gather.1 = f32[4,2,24,128]{3,2,1,0:T(8,128)S(1)} all-gather(f32[2,2,24,128]{3,2,1,0:T(8,128)S(1)} %pad_maximum_fusion.1), channel_id=3, replica_groups=mesh['gx'=64,'gy'=4,'ga'=2] {'ga'}, dimensions={0}, use_global_device_ids=true | all-gather | bytes 147456 | tf_op jit(solution)/shard_map/all_gather | solution.py:792
  54.2 2.4 %shard_map.132 = (f32[2,24,8,128]{3,2,1,0:T(8,128)S(1)}, f32[2,24,8,128]{3,2,1,0:T(8,128)S(1)}, f32[2,24,128]{2,1,0:T(8,128)S(1)}, f32[2,24,128]{2,1,0:T(8,128)S(1)}) custom-call(s32[5]{0:T(128)S(1)} %stack.67.ids, f32[2,2,24,8,128]{4,3,2,1,0:T(8,128)S(1)} %bitcast.34, f32[2,24,8,128]{3,2,1,0:T(8,128)S(1)} %get-tuple-element.53.first, ...), custom_call_target="tpu_custom_call" | custom-call | tf_op jit(solution)/shard_map/pallas_call | solution.py:738
  61.6 2.4 %collective-permute-done.4 = f32[2,24,128]{2,1,0:T(8,128)S(1)} collective-permute-done((f32[2,24,128]{2,1,0:T(8,128)S(1)}, f32[2,24,128]{2,1,0:T(8,128)S(1)}, u32[]{:S(2)}, u32[]{:S(2)}) %collective-permute-start.4) | collective-permute-done | bytes 24608 | tf_op jit(solution)/shard_map/ppermute | solution.py:754
  64.0 2.3 %all-gather.2 = f32[4,2,24,128]{3,2,1,0:T(8,128)S(1)} all-gather(f32[2,2,24,128]{3,2,1,0:T(8,128)S(1)} %pad_maximum_fusion.2), channel_id=4, replica_groups=mesh['gx'=64,'gy'=4,'ga'=2] {'ga'}, dimensions={0}, use_global_device_ids=true | all-gather | bytes 147456 | tf_op jit(solution)/shard_map/all_gather | solution.py:792
  66.3 2.9 %shard_map.133 = (f32[2,24,8,128]{3,2,1,0:T(8,128)S(1)}, f32[24,128]{1,0:T(8,128)S(1)}, f32[24,128]{1,0:T(8,128)S(1)}) custom-call(s32[5]{0:T(128)S(1)} %stack.67.ids, f32[2,2,24,8,128]{4,3,2,1,0:T(8,128)S(1)} %bitcast.35, f32[2,24,8,128]{3,2,1,0:T(8,128)S(1)} %get-tuple-element.53.first, f32[2,24,8,128]{3,2,1,0:T(8,128)S(1)} %get-tuple-element.57.second, ...), custom_call_target="tpu_custom_call" | custom-call | tf_op jit(solution)/shard_map/pallas_call | solution.py:738
  70.0 4.8 %collective-permute-start.5 = (f32[24,128]{1,0:T(8,128)S(1)}, f32[24,128]{1,0:T(8,128)S(1)}, u32[]{:S(2)}, u32[]{:S(2)}) collective-permute-start(f32[24,128]{1,0:T(8,128)S(1)} %get-tuple-element.62), channel_id=1, source_target_pairs={{0,8},{8,16},{16,24},{24,32},{32,40},{40,48},{48,56},{56,64},{64,7... | collective-permute-start | bytes 36872 | tf_op jit(solution)/shard_map/ppermute | solution.py:754
  75.6 4.1 %all-gather.3 = f32[96,128]{1,0:T(8,128)S(1)} all-gather(f32[48,128]{1,0:T(8,128)S(1)} %pad_maximum_fusion.7), channel_id=5, replica_groups={{0,2},{4,6},{1,3},{5,7},{8,10},{12,14},{9,11},{13,15},{16,18},{20,22},{..., dimensions={0}, use_global_device_ids=true | all-gather | bytes 73728 | tf_op jit(solution)/shard_map/all_gather | solution.py:765
  79.7 5.1 %all-gather.4 = f32[4,48,128]{2,1,0:T(8,128)S(1)} all-gather(f32[2,48,128]{2,1,0:T(8,128)S(1)} %bitcast.48), channel_id=6, replica_groups={{0,4},{2,6},{1,5},{3,7},{8,12},{10,14},{9,13},{11,15},{16,20},{18,22},{..., dimensions={0}, use_global_device_ids=true | all-gather | bytes 147456 | tf_op jit(solution)/shard_map/all_gather | solution.py:766
  84.8 5.6 %all-gather.12 = f32[8,48,128]{2,1,0:T(8,128)S(1)} all-gather(f32[4,48,128]{2,1,0:T(8,128)S(1)} %all-gather.4), channel_id=14, replica_groups=mesh['gx'=64,'gy'=4,'ga'=2] {'ga'}, dimensions={0}, use_global_device_ids=true | all-gather | bytes 294912 | tf_op jit(solution)/shard_map/all_gather | solution.py:767
  92.5 2.4 %shard_map.136 = (f32[24,8,128]{2,1,0:T(8,128)S(1)}, f32[24,8,128]{2,1,0:T(8,128)S(1)}, f32[24,8,128]{2,1,0:T(8,128)S(1)}, f32[8,8,128]{2,1,0:T(8,128)}) custom-call(s32[5]{0:T(128)S(1)} %stack.67.ids, f32[2,4,48,128]{3,2,1,0:T(8,128)S(1)} %bitcast.41, f32[8,110,8,128]{3,2,1,0:T(8,128)S(1)} %bitcast.30), custom_call_target="tpu_custom_call" | custom-call | tf_op jit(solution)/shard_map/pallas_call | solution.py:738
  96.8 3.0 %collective-permute-start.9 = (f32[8,8,128]{2,1,0:T(8,128)}, f32[8,8,128]{2,1,0:T(8,128)}, u32[]{:S(2)}, u32[]{:S(2)}) collective-permute-start(f32[8,8,128]{2,1,0:T(8,128)} %get-tuple-element.71.mid), channel_id=1, source_target_pairs={{8,0},{16,8},{24,16},{32,24},{40,32},{48,40},{56,48},{64,56},{72,6... | collective-permute-start | bytes 98312 | tf_op jit(solution)/shard_map/ppermute | solution.py:749
  102.5 4.0 %all-gather.19.cloned.1.call-done = f32[328,8,128]{2,1,0:T(8,128)} async-done(((f32[41,8,128]{2,1,0:T(8,128)}), f32[328,8,128]{2,1,0:T(8,128)}) %all-gather.19.cloned.1.call-update) | async-done | bytes 1343504 | tf_op jit(solution)/shard_map/all_gather | solution.py:821
  112.5 7.6 %collective-permute-start.10 = (f32[56,128]{1,0:T(8,128)S(1)}, f32[56,128]{1,0:T(8,128)S(1)}, u32[]{:S(2)}, u32[]{:S(2)}) collective-permute-start(f32[56,128]{1,0:T(8,128)S(1)} %get-tuple-element.76.mine), channel_id=1, source_target_pairs={{32,0},{40,8},{48,16},{56,24},{64,32},{72,40},{80,48},{88,56},{96,... | collective-permute-start | bytes 86024 | tf_op jit(solution)/shard_map/ppermute | solution.py:761
  120.1 7.3 %collective-permute-start.11 = (f32[8,128]{1,0:T(8,128)S(1)}, f32[8,128]{1,0:T(8,128)S(1)}, u32[]{:S(2)}, u32[]{:S(2)}) collective-permute-start(f32[8,128]{1,0:T(8,128)S(1)} %slice.3), channel_id=1, source_target_pairs={{64,0},{72,8},{80,16},{88,24},{96,32},{104,40},{112,48},{120,56},{... | collective-permute-start | bytes 12296 | tf_op jit(solution)/shard_map/ppermute | solution.py:761
  128.4 2.7 %collective-permute-done.11 = f32[8,128]{1,0:T(8,128)S(1)} collective-permute-done((f32[8,128]{1,0:T(8,128)S(1)}, f32[8,128]{1,0:T(8,128)S(1)}, u32[]{:S(2)}, u32[]{:S(2)}) %collective-permute-start.11) | collective-permute-done | bytes 4128 | tf_op jit(solution)/shard_map/ppermute | solution.py:761
  131.1 3.7 %all-gather.7 = f32[128,128]{1,0:T(8,128)S(1)} all-gather(f32[64,128]{1,0:T(8,128)S(1)} %pad_maximum_fusion.6), channel_id=9, replica_groups={{0,2},{4,6},{1,3},{5,7},{8,10},{12,14},{9,11},{13,15},{16,18},{20,22},{..., dimensions={0}, use_global_device_ids=true | all-gather | bytes 98304 | tf_op jit(solution)/shard_map/all_gather | solution.py:765
  134.8 5.3 %all-gather.8 = f32[4,64,128]{2,1,0:T(8,128)S(1)} all-gather(f32[2,64,128]{2,1,0:T(8,128)S(1)} %bitcast.47), channel_id=10, replica_groups={{0,4},{2,6},{1,5},{3,7},{8,12},{10,14},{9,13},{11,15},{16,20},{18,22},{..., dimensions={0}, use_global_device_ids=true | all-gather | bytes 196608 | tf_op jit(solution)/shard_map/all_gather | solution.py:766
  140.1 8.2 %all-gather.13 = f32[8,64,128]{2,1,0:T(8,128)S(1)} all-gather(f32[4,64,128]{2,1,0:T(8,128)S(1)} %all-gather.8), channel_id=15, replica_groups=mesh['gx'=64,'gy'=4,'ga'=2] {'ga'}, dimensions={0}, use_global_device_ids=true | all-gather | bytes 393216 | tf_op jit(solution)/shard_map/all_gather | solution.py:767
  148.3 3.0 %shard_map.140 = (f32[24,8,128]{2,1,0:T(8,128)S(1)}, f32[12,8,128]{2,1,0:T(8,128)S(1)}, f32[12,8,128]{2,1,0:T(8,128)S(1)}) custom-call(s32[5]{0:T(128)S(1)} %copy-done.16, f32[2,4,64,128]{3,2,1,0:T(8,128)S(1)} %bitcast.40, f32[56,128]{1,0:T(8,128)S(1)} %get-tuple-element.76.mine, f32[3,40,128]{2,1,0:T(8,128)S(1)} %get-tuple-element.79.bottom_stiff, ...), custom_call_target="tpu_custom_call" | custom-call | tf_op jit(solution)/shard_map/pallas_call | solution.py:738
  153.6 5.1 %collective-permute-start.13 = (f32[12,8,128]{2,1,0:T(8,128)S(1)}, f32[12,8,128]{2,1,0:T(8,128)S(1)}, u32[]{:S(2)}, u32[]{:S(2)}) collective-permute-start(f32[12,8,128]{2,1,0:T(8,128)S(1)} %get-tuple-element.86), channel_id=1, source_target_pairs={{8,0},{16,8},{24,16},{32,24},{40,32},{48,40},{56,48},{64,56},{72,6... | collective-permute-start | bytes 147464 | tf_op jit(solution)/shard_map/ppermute | solution.py:749
  159.9 2.6 %shard_map.141 = (f32[2,24,8,128]{3,2,1,0:T(8,128)S(1)}, f32[2,24,128]{2,1,0:T(8,128)S(1)}, f32[2,24,128]{2,1,0:T(8,128)S(1)}) custom-call(s32[5]{0:T(128)S(1)} %copy-done.16, f32[12,8,128]{2,1,0:T(8,128)S(1)} %collective-permute-done.12.low, f32[24,8,128]{2,1,0:T(8,128)S(1)} %get-tuple-element.85.mid, f32[12,8,128]{2,1,0:T(8,128)S(1)} %collective-permute-done.13.high, ...), custom_call_target="tpu_custom_call" | custom-call | tf_op jit(solution)/shard_map/pallas_call | solution.py:738
  162.5 5.8 %collective-permute-start.14 = (f32[2,24,128]{2,1,0:T(8,128)S(1)}, f32[2,24,128]{2,1,0:T(8,128)S(1)}, u32[]{:S(2)}, u32[]{:S(2)}) collective-permute-start(f32[2,24,128]{2,1,0:T(8,128)S(1)} %get-tuple-element.91), channel_id=1, source_target_pairs={{0,8},{8,16},{16,24},{24,32},{32,40},{40,48},{48,56},{56,64},{64,7... | collective-permute-start | bytes 73736 | tf_op jit(solution)/shard_map/ppermute | solution.py:754
  169.6 3.3 %collective-permute-done.15 = f32[2,24,128]{2,1,0:T(8,128)S(1)} collective-permute-done((f32[2,24,128]{2,1,0:T(8,128)S(1)}, f32[2,24,128]{2,1,0:T(8,128)S(1)}, u32[]{:S(2)}, u32[]{:S(2)}) %collective-permute-start.15) | collective-permute-done | bytes 24608 | tf_op jit(solution)/shard_map/ppermute | solution.py:754
  177.1 2.6 %collective-permute-start.16 = (f32[2,24,128]{2,1,0:T(8,128)S(1)}, f32[2,24,128]{2,1,0:T(8,128)S(1)}, u32[]{:S(2)}, u32[]{:S(2)}) collective-permute-start(f32[2,24,128]{2,1,0:T(8,128)S(1)} %get-tuple-element.95), channel_id=1, source_target_pairs={{0,8},{8,16},{16,24},{24,32},{32,40},{40,48},{48,56},{56,64},{64,7... | collective-permute-start | bytes 73736 | tf_op jit(solution)/shard_map/ppermute | solution.py:754
  181.6 3.0 %collective-permute-done.17 = f32[2,24,128]{2,1,0:T(8,128)S(1)} collective-permute-done((f32[2,24,128]{2,1,0:T(8,128)S(1)}, f32[2,24,128]{2,1,0:T(8,128)S(1)}, u32[]{:S(2)}, u32[]{:S(2)}) %collective-permute-start.17) | collective-permute-done | bytes 24608 | tf_op jit(solution)/shard_map/ppermute | solution.py:754
  186.6 3.0 %shard_map.143 = (f32[24,8,128]{2,1,0:T(8,128)}, f32[24,8,128]{2,1,0:T(8,128)S(1)}, f32[2,24,8,128]{3,2,1,0:T(8,128)S(1)}, f32[2,24,128]{2,1,0:T(8,128)S(1)}, f32[2,24,128]{2,1,0:T(8,128)S(1)}) custom-call(s32[5]{0:T(128)S(1)} %copy-done.16, f32[2,2,24,8,128]{4,3,2,1,0:T(8,128)S(1)} %bitcast.37, f32[2,24,8,128]{3,2,1,0:T(8,128)S(1)} %get-tuple-element.90.guess, ...), custom_call_target="tpu_custom_call" | custom-call | tf_op jit(solution)/shard_map/pallas_call | solution.py:738
  189.6 3.3 %collective-permute-start.18 = (f32[2,24,128]{2,1,0:T(8,128)S(1)}, f32[2,24,128]{2,1,0:T(8,128)S(1)}, u32[]{:S(2)}, u32[]{:S(2)}) collective-permute-start(f32[2,24,128]{2,1,0:T(8,128)S(1)} %get-tuple-element.100), channel_id=1, source_target_pairs={{0,8},{8,16},{16,24},{24,32},{32,40},{40,48},{48,56},{56,64},{64,7... | collective-permute-start | bytes 73736 | tf_op jit(solution)/shard_map/ppermute | solution.py:754
  194.2 3.8 %collective-permute-done.19 = f32[2,24,128]{2,1,0:T(8,128)S(1)} collective-permute-done((f32[2,24,128]{2,1,0:T(8,128)S(1)}, f32[2,24,128]{2,1,0:T(8,128)S(1)}, u32[]{:S(2)}, u32[]{:S(2)}) %collective-permute-start.19) | collective-permute-done | bytes 24608 | tf_op jit(solution)/shard_map/ppermute | solution.py:754
  (107 shorter events, 57.9 us)
Async XLA Ops:
  7.2 94.9 %copy-start = (bf16[7,3,3,16384]{3,0,2,1:T(8,128)(2,1)S(1)}, bf16[7,3,3,16384]{3,0,2,1:T(8,128)(2,1)}, u32[]{:S(2)}) copy-start(bf16[7,3,3,16384]{3,0,2,1:T(8,128)(2,1)} %param.23) | copy-start | bytes 6193156
  7.2 83.2 %all-gather.17.cloned.1.call-start = ((), (), s32[]{:S(2)}) async-start(), calls=%async_computation | async-start | bytes 4055040 | tf_op jit(solution)/shard_map/all_gather | solution.py:818
  13.3 77.1 %copy-start.14 = (s32[5]{0:T(128)}, s32[5]{0:T(128)S(1)}, u32[]{:S(2)}) copy-start(s32[5]{0:T(128)S(1)} %stack.67.ids) | copy-start | bytes 64
  14.2 21.2 %collective-permute-start.6 = (f32[57,4,128]{2,1,0:T(4,128)S(1)}, f32[57,4,128]{2,1,0:T(4,128)S(1)}, u32[]{:S(2)}, u32[]{:S(2)}) collective-permute-start(f32[57,4,128]{2,1,0:T(4,128)S(1)} %get-tuple-element.65), channel_id=1, source_target_pairs={{0,8},{8,16},{16,24},{24,32},{32,40},{40,48},{48,56},{56,64},{64,7... | collective-permute-start | bytes 350216 | tf_op jit(solution)/shard_map/ppermute | solution.py:749
  17.8 17.7 %collective-permute-start.7 = (f32[57,4,128]{2,1,0:T(4,128)S(1)}, f32[57,4,128]{2,1,0:T(4,128)S(1)}, u32[]{:S(2)}, u32[]{:S(2)}) collective-permute-start(f32[57,4,128]{2,1,0:T(4,128)S(1)} %get-tuple-element.66), channel_id=1, source_target_pairs={{8,0},{16,8},{24,16},{32,24},{40,32},{48,40},{56,48},{64,56},{72,6... | collective-permute-start | bytes 350216 | tf_op jit(solution)/shard_map/ppermute | solution.py:749
  36.9 69.5 %all-gather.19.cloned.1.call-start = ((), (), s32[]{:S(2)}) async-start(), calls=%async_computation.1 | async-start | bytes 1511424 | tf_op jit(solution)/shard_map/all_gather | solution.py:821
  37.0 15.2 %collective-permute-start.2 = (f32[576,8,128]{2,1,0:T(8,128)}, f32[576,8,128]{2,1,0:T(8,128)}, u32[]{:S(2)}, u32[]{:S(2)}) collective-permute-start(f32[576,8,128]{2,1,0:T(8,128)} %copy-done.1), channel_id=1, source_target_pairs={{0,1},{1,0},{2,3},{3,2},{4,5},{5,4},{6,7},{7,6},{8,9},{9,8},{10,11... | collective-permute-start | bytes 7077896 | tf_op jit(solution)/shard_map/ppermute | solution.py:815
  39.3 5.0 %collective-permute-start.1 = (f32[2,24,128]{2,1,0:T(8,128)S(1)}, f32[2,24,128]{2,1,0:T(8,128)S(1)}, u32[]{:S(2)}, u32[]{:S(2)}) collective-permute-start(f32[2,24,128]{2,1,0:T(8,128)S(1)} %get-tuple-element.55), channel_id=1, source_target_pairs={{0,2},{2,4},{4,6},{3,1},{5,3},{7,5},{8,10},{10,12},{12,14},{11,9},... | collective-permute-start | bytes 73736 | tf_op jit(solution)/shard_map/ppermute | solution.py:754
  40.6 4.6 %collective-permute-start = (f32[2,24,128]{2,1,0:T(8,128)S(1)}, f32[2,24,128]{2,1,0:T(8,128)S(1)}, u32[]{:S(2)}, u32[]{:S(2)}) collective-permute-start(f32[2,24,128]{2,1,0:T(8,128)S(1)} %get-tuple-element.54), channel_id=1, source_target_pairs={{0,8},{8,16},{16,24},{24,32},{32,40},{40,48},{48,56},{56,64},{64,7... | collective-permute-start | bytes 73736 | tf_op jit(solution)/shard_map/ppermute | solution.py:754
  54.2 12.1 %copy-start.3 = (f32[576,8,128]{2,1,0:T(8,128)S(1)}, f32[576,8,128]{2,1,0:T(8,128)}, u32[]{:S(2)}) copy-start(f32[576,8,128]{2,1,0:T(8,128)} %copy-done.1) | copy-start | bytes 7077892
  56.6 5.0 %collective-permute-start.3 = (f32[2,24,128]{2,1,0:T(8,128)S(1)}, f32[2,24,128]{2,1,0:T(8,128)S(1)}, u32[]{:S(2)}, u32[]{:S(2)}) collective-permute-start(f32[2,24,128]{2,1,0:T(8,128)S(1)} %get-tuple-element.59), channel_id=1, source_target_pairs={{0,8},{8,16},{16,24},{24,32},{32,40},{40,48},{48,56},{56,64},{64,7... | collective-permute-start | bytes 73736 | tf_op jit(solution)/shard_map/ppermute | solution.py:754
  58.5 5.5 %collective-permute-start.4 = (f32[2,24,128]{2,1,0:T(8,128)S(1)}, f32[2,24,128]{2,1,0:T(8,128)S(1)}, u32[]{:S(2)}, u32[]{:S(2)}) collective-permute-start(f32[2,24,128]{2,1,0:T(8,128)S(1)} %get-tuple-element.60), channel_id=1, source_target_pairs={{0,2},{2,4},{4,6},{3,1},{5,3},{7,5},{8,10},{10,12},{12,14},{11,9},... | collective-permute-start | bytes 73736 | tf_op jit(solution)/shard_map/ppermute | solution.py:754
  70.0 5.6 %collective-permute-start.5 = (f32[24,128]{1,0:T(8,128)S(1)}, f32[24,128]{1,0:T(8,128)S(1)}, u32[]{:S(2)}, u32[]{:S(2)}) collective-permute-start(f32[24,128]{1,0:T(8,128)S(1)} %get-tuple-element.62), channel_id=1, source_target_pairs={{0,8},{8,16},{16,24},{24,32},{32,40},{40,48},{48,56},{56,64},{64,7... | collective-permute-start | bytes 36872 | tf_op jit(solution)/shard_map/ppermute | solution.py:754
  96.8 13.9 %collective-permute-start.9 = (f32[8,8,128]{2,1,0:T(8,128)}, f32[8,8,128]{2,1,0:T(8,128)}, u32[]{:S(2)}, u32[]{:S(2)}) collective-permute-start(f32[8,8,128]{2,1,0:T(8,128)} %get-tuple-element.71.mid), channel_id=1, source_target_pairs={{8,0},{16,8},{24,16},{32,24},{40,32},{48,40},{56,48},{64,56},{72,6... | collective-permute-start | bytes 98312 | tf_op jit(solution)/shard_map/ppermute | solution.py:749
  99.9 10.8 %collective-permute-start.8 = (f32[8,8,128]{2,1,0:T(8,128)}, f32[8,8,128]{2,1,0:T(8,128)}, u32[]{:S(2)}, u32[]{:S(2)}) collective-permute-start(f32[8,8,128]{2,1,0:T(8,128)} %get-tuple-element.71.mid), channel_id=1, source_target_pairs={{0,8},{8,16},{16,24},{24,32},{32,40},{40,48},{48,56},{56,64},{64,7... | collective-permute-start | bytes 98312 | tf_op jit(solution)/shard_map/ppermute | solution.py:749
  108.4 18.9 %copy-start.16 = (s32[5]{0:T(128)S(1)}, s32[5]{0:T(128)}, u32[]{:S(2)}) copy-start(s32[5]{0:T(128)} %copy-done.14) | copy-start | bytes 64
  110.7 37.6 %copy-start.6 = (f32[880,8,128]{2,1,0:T(8,128)S(1)}, f32[880,8,128]{2,1,0:T(8,128)}, u32[]{:S(2)}) copy-start(f32[880,8,128]{2,1,0:T(8,128)} %all-gather.17.cloned.1.call-done) | copy-start | bytes 10813444
  110.7 37.6 %copy-start.22 = (f32[24,8,128]{2,1,0:T(8,128)S(1)}, f32[24,8,128]{2,1,0:T(8,128)}, u32[]{:S(2)}) copy-start(f32[24,8,128]{2,1,0:T(8,128)} %copy-done.21) | copy-start | bytes 294916
  112.5 18.5 %collective-permute-start.10 = (f32[56,128]{1,0:T(8,128)S(1)}, f32[56,128]{1,0:T(8,128)S(1)}, u32[]{:S(2)}, u32[]{:S(2)}) collective-permute-start(f32[56,128]{1,0:T(8,128)S(1)} %get-tuple-element.76.mine), channel_id=1, source_target_pairs={{32,0},{40,8},{48,16},{56,24},{64,32},{72,40},{80,48},{88,56},{96,... | collective-permute-start | bytes 86024 | tf_op jit(solution)/shard_map/ppermute | solution.py:761
  120.1 11.0 %collective-permute-start.11 = (f32[8,128]{1,0:T(8,128)S(1)}, f32[8,128]{1,0:T(8,128)S(1)}, u32[]{:S(2)}, u32[]{:S(2)}) collective-permute-start(f32[8,128]{1,0:T(8,128)S(1)} %slice.3), channel_id=1, source_target_pairs={{64,0},{72,8},{80,16},{88,24},{96,32},{104,40},{112,48},{120,56},{... | collective-permute-start | bytes 12296 | tf_op jit(solution)/shard_map/ppermute | solution.py:761
  148.3 11.6 %copy-start.4 = (f32[576,8,128]{2,1,0:T(8,128)S(1)}, f32[576,8,128]{2,1,0:T(8,128)}, u32[]{:S(2)}) copy-start(f32[576,8,128]{2,1,0:T(8,128)} %copy-done.1) | copy-start | bytes 7077892
  148.3 11.6 %copy-start.12 = (f32[2,24,8,128]{3,2,1,0:T(8,128)S(1)}, f32[2,24,8,128]{3,2,1,0:T(8,128)}, u32[]{:S(2)}) copy-start(f32[2,24,8,128]{3,2,1,0:T(8,128)} %copy-done.11) | copy-start | bytes 589828
  148.3 11.6 %copy-start.18 = (f32[24,8,128]{2,1,0:T(8,128)S(1)}, f32[24,8,128]{2,1,0:T(8,128)}, u32[]{:S(2)}) copy-start(f32[24,8,128]{2,1,0:T(8,128)} %copy-done.17) | copy-start | bytes 294916
  148.3 11.6 %copy-start.20 = (f32[24,8,128]{2,1,0:T(8,128)S(1)}, f32[24,8,128]{2,1,0:T(8,128)}, u32[]{:S(2)}) copy-start(f32[24,8,128]{2,1,0:T(8,128)} %copy-done.19) | copy-start | bytes 294916
  151.3 7.4 %collective-permute-start.12 = (f32[12,8,128]{2,1,0:T(8,128)S(1)}, f32[12,8,128]{2,1,0:T(8,128)S(1)}, u32[]{:S(2)}, u32[]{:S(2)}) collective-permute-start(f32[12,8,128]{2,1,0:T(8,128)S(1)} %get-tuple-element.84), channel_id=1, source_target_pairs={{0,8},{8,16},{16,24},{24,32},{32,40},{40,48},{48,56},{56,64},{64,7... | collective-permute-start | bytes 147464 | tf_op jit(solution)/shard_map/ppermute | solution.py:749
  153.6 6.3 %collective-permute-start.13 = (f32[12,8,128]{2,1,0:T(8,128)S(1)}, f32[12,8,128]{2,1,0:T(8,128)S(1)}, u32[]{:S(2)}, u32[]{:S(2)}) collective-permute-start(f32[12,8,128]{2,1,0:T(8,128)S(1)} %get-tuple-element.86), channel_id=1, source_target_pairs={{8,0},{16,8},{24,16},{32,24},{40,32},{48,40},{56,48},{64,56},{72,6... | collective-permute-start | bytes 147464 | tf_op jit(solution)/shard_map/ppermute | solution.py:749
  162.5 7.1 %collective-permute-start.14 = (f32[2,24,128]{2,1,0:T(8,128)S(1)}, f32[2,24,128]{2,1,0:T(8,128)S(1)}, u32[]{:S(2)}, u32[]{:S(2)}) collective-permute-start(f32[2,24,128]{2,1,0:T(8,128)S(1)} %get-tuple-element.91), channel_id=1, source_target_pairs={{0,8},{8,16},{16,24},{24,32},{32,40},{40,48},{48,56},{56,64},{64,7... | collective-permute-start | bytes 73736 | tf_op jit(solution)/shard_map/ppermute | solution.py:754
  168.3 4.6 %collective-permute-start.15 = (f32[2,24,128]{2,1,0:T(8,128)S(1)}, f32[2,24,128]{2,1,0:T(8,128)S(1)}, u32[]{:S(2)}, u32[]{:S(2)}) collective-permute-start(f32[2,24,128]{2,1,0:T(8,128)S(1)} %get-tuple-element.92), channel_id=1, source_target_pairs={{0,2},{2,4},{4,6},{3,1},{5,3},{7,5},{8,10},{10,12},{12,14},{11,9},... | collective-permute-start | bytes 73736 | tf_op jit(solution)/shard_map/ppermute | solution.py:754
  177.1 4.6 %collective-permute-start.16 = (f32[2,24,128]{2,1,0:T(8,128)S(1)}, f32[2,24,128]{2,1,0:T(8,128)S(1)}, u32[]{:S(2)}, u32[]{:S(2)}) collective-permute-start(f32[2,24,128]{2,1,0:T(8,128)S(1)} %get-tuple-element.95), channel_id=1, source_target_pairs={{0,8},{8,16},{16,24},{24,32},{32,40},{40,48},{48,56},{56,64},{64,7... | collective-permute-start | bytes 73736 | tf_op jit(solution)/shard_map/ppermute | solution.py:754
  179.7 5.0 %collective-permute-start.17 = (f32[2,24,128]{2,1,0:T(8,128)S(1)}, f32[2,24,128]{2,1,0:T(8,128)S(1)}, u32[]{:S(2)}, u32[]{:S(2)}) collective-permute-start(f32[2,24,128]{2,1,0:T(8,128)S(1)} %get-tuple-element.96), channel_id=1, source_target_pairs={{0,2},{2,4},{4,6},{3,1},{5,3},{7,5},{8,10},{10,12},{12,14},{11,9},... | collective-permute-start | bytes 73736 | tf_op jit(solution)/shard_map/ppermute | solution.py:754
  189.6 4.6 %collective-permute-start.18 = (f32[2,24,128]{2,1,0:T(8,128)S(1)}, f32[2,24,128]{2,1,0:T(8,128)S(1)}, u32[]{:S(2)}, u32[]{:S(2)}) collective-permute-start(f32[2,24,128]{2,1,0:T(8,128)S(1)} %get-tuple-element.100), channel_id=1, source_target_pairs={{0,8},{8,16},{16,24},{24,32},{32,40},{40,48},{48,56},{56,64},{64,7... | collective-permute-start | bytes 73736 | tf_op jit(solution)/shard_map/ppermute | solution.py:754
  192.9 5.1 %collective-permute-start.19 = (f32[2,24,128]{2,1,0:T(8,128)S(1)}, f32[2,24,128]{2,1,0:T(8,128)S(1)}, u32[]{:S(2)}, u32[]{:S(2)}) collective-permute-start(f32[2,24,128]{2,1,0:T(8,128)S(1)} %get-tuple-element.101), channel_id=1, source_target_pairs={{0,2},{2,4},{4,6},{3,1},{5,3},{7,5},{8,10},{10,12},{12,14},{11,9},... | collective-permute-start | bytes 73736 | tf_op jit(solution)/shard_map/ppermute | solution.py:754
  (17 other events, 17.2 us)
Sparse Core Ops, SparseCore 0:
  37.1 35.1 all-gather.16
  74.4 32.0 all-gather.18

commit v6 on v5

--- a/solution.py
+++ b/solution.py
@@ -120,7 +120,7 @@
             own[504 + 8 * i + x] = prolong[i // 3, i % 3, x]
 
 
-def fine_second(ids, ls, first, halo, own, other, rest, second, xs, ys):
+def fine_second(ids, ls, first, halo, own, other, rest, second, xs, ys, kept):
     fine = Fine(ids)
     load, stiff = given(fine, ls, 0), given(fine, ls, 1)
 
@@ -132,6 +132,8 @@
 
     fine.apply(at(first), halo, stiff, (own, other), use)
     fine.send(at(second), xs, ys)
+    for i in range(576):
+        kept[i] = other[i]
 
 
 def fine_down(ids, ls, first, second, rest, halo, own, other, pre, keep, send):
@@ -816,10 +818,11 @@
     below, above, _ = lax.optimization_barrier((below, above, xs))
     one, two = run(pack_levels, ids, [body, below, above, coarse], [(110, 8, 128), (41, 8, 128)])
     packed1 = lax.all_gather(one, ("gy", "ga"))
+    packed2 = lax.all_gather(two, ("gy", "ga"))
     halo = exchange(xs, ys)
-    two, _ = lax.optimization_barrier((two, halo))
-    packed2 = lax.all_gather(two, ("gy", "ga"))
-    rest, second, xs, ys = run(fine_second, ids, [ls, first, halo, own, other], [half, half, edge, edge])
+    rest, second, xs, ys, other = run(
+        fine_second, ids, [ls, first, halo, own, other], [half, half, edge, edge, (576, 8, 128)]
+    )
     halo = exchange(xs, ys)
     pre0, keep, send = run(
         fine_down, ids, [ls, first, second, rest, halo, own, other], [half, (24, 128), (24, 128)]

time: 210 us -> 206 us (0.981)
  Pallas kernels: 28.2 us -> 23.8 us
    pallas_call x14, Pallas kernels: 28.2 us -> 23.8 us  [run(): pl.pallas_call(kernel, out_shape=[jax.ShapeDtypeStruct(s, F32) for s in o...]
    unnamed x54 -> x58, local copies, waits for them, and re-layouts: 17.3 us -> 17.2 us
  transfers between devices with their start and end apart: 22 -> 22, of which waited for: 11 -> 11; matrix products, arithmetic and copies ran while one was open for 1% -> 1% of each run, Pallas kernels for 6% -> 5%
where the time goes in v6:
time: 206 us; the launch traced here: 205 us
  starting transfers between devices  71.5 us (35%)
  blocking collectives  49.7 us (24%)
  waiting for transfers between devices  25.6 us (12%)
  Pallas kernels  23.8 us (12%)
  local copies, waits for them, and re-layouts  18.6 us (9%)
  between operations  14.5 us (7%)
    ppermute x11, starting transfers between devices, split_shift(): return lax.ppermute(value, (axis, 'ga'), pairs)  28.4 us
    ppermute x6, starting transfers between devices, shifted(): lax.ppermute(value, axis, [(i, i + shift) for i in range(count) if 0 <= i...  25.9 us
    pallas_call x14, Pallas kernels, run(): pl.pallas_call(kernel, out_shape=[jax.ShapeDtypeStruct(s, F32) for s in o...  23.8 us
    unnamed x58, local copies, waits for them, and re-layouts  17.2 us
    ppermute x11, waiting for transfers between devices, split_shift(): return lax.ppermute(value, (axis, 'ga'), pairs)  16.6 us
    all_gather x5, blocking collectives, exchange(): return lax.all_gather(both, 'ga')  15 us
    ppermute x2, starting transfers between devices, skewed(): return lax.ppermute(value, ('gx', 'gy', 'ga'), pairs)  14.8 us
    all_gather x2, blocking collectives, group_gather(): return lax.all_gather(four.reshape((4,) + value.shape), 'ga')  13.9 us
  transfers between devices with their start and end apart: 22, of which 11 were waited for; matrix products, arithmetic and copies ran while one was open for 1% of the time, Pallas kernels for 5%

profile of v6, /device:TPU:25, one launch (start us, length us, event | category | flops | bytes accessed | tf_op | source)
XLA Modules:
  0.0 204.7 jit_solution(1811559192522258528)
XLA Ops:
  14.2 3.5 %collective-permute-start.6 = (f32[57,4,128]{2,1,0:T(4,128)S(1)}, f32[57,4,128]{2,1,0:T(4,128)S(1)}, u32[]{:S(2)}, u32[]{:S(2)}) collective-permute-start(f32[57,4,128]{2,1,0:T(4,128)S(1)} %get-tuple-element.66), channel_id=1, source_target_pairs={{0,8},{8,16},{16,24},{24,32},{32,40},{40,48},{48,56},{56,64},{64,7... | collective-permute-start | bytes 350216 | tf_op jit(solution)/shard_map/ppermute | solution.py:751
  17.8 9.7 %collective-permute-start.7 = (f32[57,4,128]{2,1,0:T(4,128)S(1)}, f32[57,4,128]{2,1,0:T(4,128)S(1)}, u32[]{:S(2)}, u32[]{:S(2)}) collective-permute-start(f32[57,4,128]{2,1,0:T(4,128)S(1)} %get-tuple-element.67), channel_id=1, source_target_pairs={{8,0},{16,8},{24,16},{32,24},{40,32},{48,40},{56,48},{64,56},{72,6... | collective-permute-start | bytes 350216 | tf_op jit(solution)/shard_map/ppermute | solution.py:751
  28.4 2.7 %all-gather = f32[4,24,8,128]{3,2,1,0:T(8,128)S(1)} all-gather(f32[2,24,8,128]{3,2,1,0:T(8,128)S(1)} %pad_maximum_fusion), channel_id=2, replica_groups=mesh['gx'=64,'gy'=4,'ga'=2] {'ga'}, dimensions={0}, use_global_device_ids=true | all-gather | bytes 589824 | tf_op jit(solution)/shard_map/all_gather | solution.py:812
  37.0 2.3 %collective-permute-start.2 = (f32[576,8,128]{2,1,0:T(8,128)}, f32[576,8,128]{2,1,0:T(8,128)}, u32[]{:S(2)}, u32[]{:S(2)}) collective-permute-start(f32[576,8,128]{2,1,0:T(8,128)} %copy-done.1), channel_id=1, source_target_pairs={{0,1},{1,0},{2,3},{3,2},{4,5},{5,4},{6,7},{7,6},{8,9},{9,8},{10,11... | collective-permute-start | bytes 7077896 | tf_op jit(solution)/shard_map/ppermute | solution.py:817
  40.6 3.6 %collective-permute-start = (f32[2,24,128]{2,1,0:T(8,128)S(1)}, f32[2,24,128]{2,1,0:T(8,128)S(1)}, u32[]{:S(2)}, u32[]{:S(2)}) collective-permute-start(f32[2,24,128]{2,1,0:T(8,128)S(1)} %get-tuple-element.54), channel_id=1, source_target_pairs={{0,8},{8,16},{16,24},{24,32},{32,40},{40,48},{48,56},{56,64},{64,7... | collective-permute-start | bytes 73736 | tf_op jit(solution)/shard_map/ppermute | solution.py:756
  45.2 7.0 %all-gather.1 = f32[4,2,24,128]{3,2,1,0:T(8,128)S(1)} all-gather(f32[2,2,24,128]{3,2,1,0:T(8,128)S(1)} %pad_maximum_fusion.1), channel_id=3, replica_groups=mesh['gx'=64,'gy'=4,'ga'=2] {'ga'}, dimensions={0}, use_global_device_ids=true | all-gather | bytes 147456 | tf_op jit(solution)/shard_map/all_gather | solution.py:794
  54.1 2.5 %shard_map.132 = (f32[2,24,8,128]{3,2,1,0:T(8,128)S(1)}, f32[2,24,8,128]{3,2,1,0:T(8,128)S(1)}, f32[2,24,128]{2,1,0:T(8,128)S(1)}, f32[2,24,128]{2,1,0:T(8,128)S(1)}, f32[576,8,128]{2,1,0:T(8,128)S(1)}) custom-call(s32[5]{0:T(128)S(1)} %stack.67.ids, f32[2,2,24,8,128]{4,3,2,1,0:T(8,128)S(1)} %bitcast.34, f32[2,24,8,128]{3,2,1,0:T(8,128)S(1)} %get-tuple-element.53.first, ...), custom_call_target="tpu_custom_call" | custom-call | tf_op jit(solution)/shard_map/pallas_call | solution.py:740
  61.7 2.4 %collective-permute-done.4 = f32[2,24,128]{2,1,0:T(8,128)S(1)} collective-permute-done((f32[2,24,128]{2,1,0:T(8,128)S(1)}, f32[2,24,128]{2,1,0:T(8,128)S(1)}, u32[]{:S(2)}, u32[]{:S(2)}) %collective-permute-start.4) | collective-permute-done | bytes 24608 | tf_op jit(solution)/shard_map/ppermute | solution.py:756
  64.1 2.3 %all-gather.2 = f32[4,2,24,128]{3,2,1,0:T(8,128)S(1)} all-gather(f32[2,2,24,128]{3,2,1,0:T(8,128)S(1)} %pad_maximum_fusion.2), channel_id=4, replica_groups=mesh['gx'=64,'gy'=4,'ga'=2] {'ga'}, dimensions={0}, use_global_device_ids=true | all-gather | bytes 147456 | tf_op jit(solution)/shard_map/all_gather | solution.py:794
  68.9 4.7 %collective-permute-start.5 = (f32[24,128]{1,0:T(8,128)S(1)}, f32[24,128]{1,0:T(8,128)S(1)}, u32[]{:S(2)}, u32[]{:S(2)}) collective-permute-start(f32[24,128]{1,0:T(8,128)S(1)} %get-tuple-element.63), channel_id=1, source_target_pairs={{0,8},{8,16},{16,24},{24,32},{32,40},{40,48},{48,56},{56,64},{64,7... | collective-permute-start | bytes 36872 | tf_op jit(solution)/shard_map/ppermute | solution.py:756
  74.5 4.0 %all-gather.3 = f32[96,128]{1,0:T(8,128)S(1)} all-gather(f32[48,128]{1,0:T(8,128)S(1)} %pad_maximum_fusion.7), channel_id=5, replica_groups={{0,2},{4,6},{1,3},{5,7},{8,10},{12,14},{9,11},{13,15},{16,18},{20,22},{..., dimensions={0}, use_global_device_ids=true | all-gather | bytes 73728 | tf_op jit(solution)/shard_map/all_gather | solution.py:767
  78.5 5.1 %all-gather.4 = f32[4,48,128]{2,1,0:T(8,128)S(1)} all-gather(f32[2,48,128]{2,1,0:T(8,128)S(1)} %bitcast.48), channel_id=6, replica_groups={{0,4},{2,6},{1,5},{3,7},{8,12},{10,14},{9,13},{11,15},{16,20},{18,22},{..., dimensions={0}, use_global_device_ids=true | all-gather | bytes 147456 | tf_op jit(solution)/shard_map/all_gather | solution.py:768
  83.6 5.7 %all-gather.12 = f32[8,48,128]{2,1,0:T(8,128)S(1)} all-gather(f32[4,48,128]{2,1,0:T(8,128)S(1)} %all-gather.4), channel_id=14, replica_groups=mesh['gx'=64,'gy'=4,'ga'=2] {'ga'}, dimensions={0}, use_global_device_ids=true | all-gather | bytes 294912 | tf_op jit(solution)/shard_map/all_gather | solution.py:769
  91.4 2.4 %shard_map.136 = (f32[24,8,128]{2,1,0:T(8,128)S(1)}, f32[24,8,128]{2,1,0:T(8,128)S(1)}, f32[24,8,128]{2,1,0:T(8,128)S(1)}, f32[8,8,128]{2,1,0:T(8,128)}) custom-call(s32[5]{0:T(128)S(1)} %stack.67.ids, f32[2,4,48,128]{3,2,1,0:T(8,128)S(1)} %bitcast.41, f32[8,110,8,128]{3,2,1,0:T(8,128)S(1)} %bitcast.30), custom_call_target="tpu_custom_call" | custom-call | tf_op jit(solution)/shard_map/pallas_call | solution.py:740
  95.6 3.1 %collective-permute-start.9 = (f32[8,8,128]{2,1,0:T(8,128)}, f32[8,8,128]{2,1,0:T(8,128)}, u32[]{:S(2)}, u32[]{:S(2)}) collective-permute-start(f32[8,8,128]{2,1,0:T(8,128)} %get-tuple-element.72.mid), channel_id=1, source_target_pairs={{8,0},{16,8},{24,16},{32,24},{40,32},{48,40},{56,48},{64,56},{72,6... | collective-permute-start | bytes 98312 | tf_op jit(solution)/shard_map/ppermute | solution.py:751
  101.3 5.1 %all-gather.19.cloned.1.call-done = f32[328,8,128]{2,1,0:T(8,128)} async-done(((f32[41,8,128]{2,1,0:T(8,128)}), f32[328,8,128]{2,1,0:T(8,128)}) %all-gather.19.cloned.1.call-update) | async-done | bytes 1343504 | tf_op jit(solution)/shard_map/all_gather | solution.py:821
  108.4 2.2 %shard_map.137.packed = f32[8,75,8,128]{3,2,1,0:T(8,128)S(1)} custom-call(s32[5]{0:T(128)S(1)} %copy-done.17, f32[8,41,8,128]{3,2,1,0:T(8,128)S(1)} %bitcast.39), custom_call_target="tpu_custom_call" | custom-call | tf_op jit(solution)/shard_map/pallas_call | solution.py:740
  112.4 7.6 %collective-permute-start.10 = (f32[56,128]{1,0:T(8,128)S(1)}, f32[56,128]{1,0:T(8,128)S(1)}, u32[]{:S(2)}, u32[]{:S(2)}) collective-permute-start(f32[56,128]{1,0:T(8,128)S(1)} %get-tuple-element.76.mine), channel_id=1, source_target_pairs={{32,0},{40,8},{48,16},{56,24},{64,32},{72,40},{80,48},{88,56},{96,... | collective-permute-start | bytes 86024 | tf_op jit(solution)/shard_map/ppermute | solution.py:763
  120.0 7.3 %collective-permute-start.11 = (f32[8,128]{1,0:T(8,128)S(1)}, f32[8,128]{1,0:T(8,128)S(1)}, u32[]{:S(2)}, u32[]{:S(2)}) collective-permute-start(f32[8,128]{1,0:T(8,128)S(1)} %slice.3), channel_id=1, source_target_pairs={{64,0},{72,8},{80,16},{88,24},{96,32},{104,40},{112,48},{120,56},{... | collective-permute-start | bytes 12296 | tf_op jit(solution)/shard_map/ppermute | solution.py:763
  128.3 2.7 %collective-permute-done.11 = f32[8,128]{1,0:T(8,128)S(1)} collective-permute-done((f32[8,128]{1,0:T(8,128)S(1)}, f32[8,128]{1,0:T(8,128)S(1)}, u32[]{:S(2)}, u32[]{:S(2)}) %collective-permute-start.11) | collective-permute-done | bytes 4128 | tf_op jit(solution)/shard_map/ppermute | solution.py:763
  131.0 3.7 %all-gather.7 = f32[128,128]{1,0:T(8,128)S(1)} all-gather(f32[64,128]{1,0:T(8,128)S(1)} %pad_maximum_fusion.6), channel_id=9, replica_groups={{0,2},{4,6},{1,3},{5,7},{8,10},{12,14},{9,11},{13,15},{16,18},{20,22},{..., dimensions={0}, use_global_device_ids=true | all-gather | bytes 98304 | tf_op jit(solution)/shard_map/all_gather | solution.py:767
  134.7 5.3 %all-gather.8 = f32[4,64,128]{2,1,0:T(8,128)S(1)} all-gather(f32[2,64,128]{2,1,0:T(8,128)S(1)} %bitcast.47), channel_id=10, replica_groups={{0,4},{2,6},{1,5},{3,7},{8,12},{10,14},{9,13},{11,15},{16,20},{18,22},{..., dimensions={0}, use_global_device_ids=true | all-gather | bytes 196608 | tf_op jit(solution)/shard_map/all_gather | solution.py:768
  140.0 8.2 %all-gather.13 = f32[8,64,128]{2,1,0:T(8,128)S(1)} all-gather(f32[4,64,128]{2,1,0:T(8,128)S(1)} %all-gather.8), channel_id=15, replica_groups=mesh['gx'=64,'gy'=4,'ga'=2] {'ga'}, dimensions={0}, use_global_device_ids=true | all-gather | bytes 393216 | tf_op jit(solution)/shard_map/all_gather | solution.py:769
  148.3 3.0 %shard_map.140 = (f32[24,8,128]{2,1,0:T(8,128)S(1)}, f32[12,8,128]{2,1,0:T(8,128)S(1)}, f32[12,8,128]{2,1,0:T(8,128)S(1)}) custom-call(s32[5]{0:T(128)S(1)} %copy-done.18, f32[2,4,64,128]{3,2,1,0:T(8,128)S(1)} %bitcast.40, f32[56,128]{1,0:T(8,128)S(1)} %get-tuple-element.76.mine, f32[3,40,128]{2,1,0:T(8,128)S(1)} %get-tuple-element.79.bottom_stiff, ...), custom_call_target="tpu_custom_call" | custom-call | tf_op jit(solution)/shard_map/pallas_call | solution.py:740
  151.3 2.3 %collective-permute-start.12 = (f32[12,8,128]{2,1,0:T(8,128)S(1)}, f32[12,8,128]{2,1,0:T(8,128)S(1)}, u32[]{:S(2)}, u32[]{:S(2)}) collective-permute-start(f32[12,8,128]{2,1,0:T(8,128)S(1)} %get-tuple-element.84), channel_id=1, source_target_pairs={{0,8},{8,16},{16,24},{24,32},{32,40},{40,48},{48,56},{56,64},{64,7... | collective-permute-start | bytes 147464 | tf_op jit(solution)/shard_map/ppermute | solution.py:751
  153.6 5.1 %collective-permute-start.13 = (f32[12,8,128]{2,1,0:T(8,128)S(1)}, f32[12,8,128]{2,1,0:T(8,128)S(1)}, u32[]{:S(2)}, u32[]{:S(2)}) collective-permute-start(f32[12,8,128]{2,1,0:T(8,128)S(1)} %get-tuple-element.86), channel_id=1, source_target_pairs={{8,0},{16,8},{24,16},{32,24},{40,32},{48,40},{56,48},{64,56},{72,6... | collective-permute-start | bytes 147464 | tf_op jit(solution)/shard_map/ppermute | solution.py:751
  161.4 5.8 %collective-permute-start.14 = (f32[2,24,128]{2,1,0:T(8,128)S(1)}, f32[2,24,128]{2,1,0:T(8,128)S(1)}, u32[]{:S(2)}, u32[]{:S(2)}) collective-permute-start(f32[2,24,128]{2,1,0:T(8,128)S(1)} %get-tuple-element.91), channel_id=1, source_target_pairs={{0,8},{8,16},{16,24},{24,32},{32,40},{40,48},{48,56},{56,64},{64,7... | collective-permute-start | bytes 73736 | tf_op jit(solution)/shard_map/ppermute | solution.py:756
  168.5 3.3 %collective-permute-done.15 = f32[2,24,128]{2,1,0:T(8,128)S(1)} collective-permute-done((f32[2,24,128]{2,1,0:T(8,128)S(1)}, f32[2,24,128]{2,1,0:T(8,128)S(1)}, u32[]{:S(2)}, u32[]{:S(2)}) %collective-permute-start.15) | collective-permute-done | bytes 24608 | tf_op jit(solution)/shard_map/ppermute | solution.py:756
  174.8 2.6 %collective-permute-start.16 = (f32[2,24,128]{2,1,0:T(8,128)S(1)}, f32[2,24,128]{2,1,0:T(8,128)S(1)}, u32[]{:S(2)}, u32[]{:S(2)}) collective-permute-start(f32[2,24,128]{2,1,0:T(8,128)S(1)} %get-tuple-element.95), channel_id=1, source_target_pairs={{0,8},{8,16},{16,24},{24,32},{32,40},{40,48},{48,56},{56,64},{64,7... | collective-permute-start | bytes 73736 | tf_op jit(solution)/shard_map/ppermute | solution.py:756
  179.4 3.0 %collective-permute-done.17 = f32[2,24,128]{2,1,0:T(8,128)S(1)} collective-permute-done((f32[2,24,128]{2,1,0:T(8,128)S(1)}, f32[2,24,128]{2,1,0:T(8,128)S(1)}, u32[]{:S(2)}, u32[]{:S(2)}) %collective-permute-start.17) | collective-permute-done | bytes 24608 | tf_op jit(solution)/shard_map/ppermute | solution.py:756
  186.2 3.3 %collective-permute-start.18 = (f32[2,24,128]{2,1,0:T(8,128)S(1)}, f32[2,24,128]{2,1,0:T(8,128)S(1)}, u32[]{:S(2)}, u32[]{:S(2)}) collective-permute-start(f32[2,24,128]{2,1,0:T(8,128)S(1)} %get-tuple-element.100), channel_id=1, source_target_pairs={{0,8},{8,16},{16,24},{24,32},{32,40},{40,48},{48,56},{56,64},{64,7... | collective-permute-start | bytes 73736 | tf_op jit(solution)/shard_map/ppermute | solution.py:756
  190.8 3.8 %collective-permute-done.19 = f32[2,24,128]{2,1,0:T(8,128)S(1)} collective-permute-done((f32[2,24,128]{2,1,0:T(8,128)S(1)}, f32[2,24,128]{2,1,0:T(8,128)S(1)}, u32[]{:S(2)}, u32[]{:S(2)}) %collective-permute-start.19) | collective-permute-done | bytes 24608 | tf_op jit(solution)/shard_map/ppermute | solution.py:756
  (111 shorter events, 54.9 us)
Async XLA Ops:
  7.2 93.8 %copy-start = (bf16[7,3,3,16384]{3,0,2,1:T(8,128)(2,1)S(1)}, bf16[7,3,3,16384]{3,0,2,1:T(8,128)(2,1)}, u32[]{:S(2)}) copy-start(bf16[7,3,3,16384]{3,0,2,1:T(8,128)(2,1)} %param.23) | copy-start | bytes 6193156
  7.2 82.1 %all-gather.17.cloned.1.call-start = ((), (), s32[]{:S(2)}) async-start(), calls=%async_computation | async-start | bytes 4055040 | tf_op jit(solution)/shard_map/all_gather | solution.py:820
  13.3 76.0 %copy-start.16 = (s32[5]{0:T(128)}, s32[5]{0:T(128)S(1)}, u32[]{:S(2)}) copy-start(s32[5]{0:T(128)S(1)} %stack.67.ids) | copy-start | bytes 64
  14.2 21.2 %collective-permute-start.6 = (f32[57,4,128]{2,1,0:T(4,128)S(1)}, f32[57,4,128]{2,1,0:T(4,128)S(1)}, u32[]{:S(2)}, u32[]{:S(2)}) collective-permute-start(f32[57,4,128]{2,1,0:T(4,128)S(1)} %get-tuple-element.66), channel_id=1, source_target_pairs={{0,8},{8,16},{16,24},{24,32},{32,40},{40,48},{48,56},{56,64},{64,7... | collective-permute-start | bytes 350216 | tf_op jit(solution)/shard_map/ppermute | solution.py:751
  17.8 17.7 %collective-permute-start.7 = (f32[57,4,128]{2,1,0:T(4,128)S(1)}, f32[57,4,128]{2,1,0:T(4,128)S(1)}, u32[]{:S(2)}, u32[]{:S(2)}) collective-permute-start(f32[57,4,128]{2,1,0:T(4,128)S(1)} %get-tuple-element.67), channel_id=1, source_target_pairs={{8,0},{16,8},{24,16},{32,24},{40,32},{48,40},{56,48},{64,56},{72,6... | collective-permute-start | bytes 350216 | tf_op jit(solution)/shard_map/ppermute | solution.py:751
  36.9 69.5 %all-gather.19.cloned.1.call-start = ((), (), s32[]{:S(2)}) async-start(), calls=%async_computation.1 | async-start | bytes 1511424 | tf_op jit(solution)/shard_map/all_gather | solution.py:821
  37.0 15.2 %collective-permute-start.2 = (f32[576,8,128]{2,1,0:T(8,128)}, f32[576,8,128]{2,1,0:T(8,128)}, u32[]{:S(2)}, u32[]{:S(2)}) collective-permute-start(f32[576,8,128]{2,1,0:T(8,128)} %copy-done.1), channel_id=1, source_target_pairs={{0,1},{1,0},{2,3},{3,2},{4,5},{5,4},{6,7},{7,6},{8,9},{9,8},{10,11... | collective-permute-start | bytes 7077896 | tf_op jit(solution)/shard_map/ppermute | solution.py:817
  39.3 5.0 %collective-permute-start.1 = (f32[2,24,128]{2,1,0:T(8,128)S(1)}, f32[2,24,128]{2,1,0:T(8,128)S(1)}, u32[]{:S(2)}, u32[]{:S(2)}) collective-permute-start(f32[2,24,128]{2,1,0:T(8,128)S(1)} %get-tuple-element.55), channel_id=1, source_target_pairs={{0,2},{2,4},{4,6},{3,1},{5,3},{7,5},{8,10},{10,12},{12,14},{11,9},... | collective-permute-start | bytes 73736 | tf_op jit(solution)/shard_map/ppermute | solution.py:756
  40.6 4.6 %collective-permute-start = (f32[2,24,128]{2,1,0:T(8,128)S(1)}, f32[2,24,128]{2,1,0:T(8,128)S(1)}, u32[]{:S(2)}, u32[]{:S(2)}) collective-permute-start(f32[2,24,128]{2,1,0:T(8,128)S(1)} %get-tuple-element.54), channel_id=1, source_target_pairs={{0,8},{8,16},{16,24},{24,32},{32,40},{40,48},{48,56},{56,64},{64,7... | collective-permute-start | bytes 73736 | tf_op jit(solution)/shard_map/ppermute | solution.py:756
  54.1 12.3 %copy-start.3 = (f32[576,8,128]{2,1,0:T(8,128)S(1)}, f32[576,8,128]{2,1,0:T(8,128)}, u32[]{:S(2)}) copy-start(f32[576,8,128]{2,1,0:T(8,128)} %copy-done.1) | copy-start | bytes 7077892
  56.7 5.0 %collective-permute-start.3 = (f32[2,24,128]{2,1,0:T(8,128)S(1)}, f32[2,24,128]{2,1,0:T(8,128)S(1)}, u32[]{:S(2)}, u32[]{:S(2)}) collective-permute-start(f32[2,24,128]{2,1,0:T(8,128)S(1)} %get-tuple-element.59), channel_id=1, source_target_pairs={{0,8},{8,16},{16,24},{24,32},{32,40},{40,48},{48,56},{56,64},{64,7... | collective-permute-start | bytes 73736 | tf_op jit(solution)/shard_map/ppermute | solution.py:756
  58.6 5.5 %collective-permute-start.4 = (f32[2,24,128]{2,1,0:T(8,128)S(1)}, f32[2,24,128]{2,1,0:T(8,128)S(1)}, u32[]{:S(2)}, u32[]{:S(2)}) collective-permute-start(f32[2,24,128]{2,1,0:T(8,128)S(1)} %get-tuple-element.60), channel_id=1, source_target_pairs={{0,2},{2,4},{4,6},{3,1},{5,3},{7,5},{8,10},{10,12},{12,14},{11,9},... | collective-permute-start | bytes 73736 | tf_op jit(solution)/shard_map/ppermute | solution.py:756
  68.9 5.5 %collective-permute-start.5 = (f32[24,128]{1,0:T(8,128)S(1)}, f32[24,128]{1,0:T(8,128)S(1)}, u32[]{:S(2)}, u32[]{:S(2)}) collective-permute-start(f32[24,128]{1,0:T(8,128)S(1)} %get-tuple-element.63), channel_id=1, source_target_pairs={{0,8},{8,16},{16,24},{24,32},{32,40},{40,48},{48,56},{56,64},{64,7... | collective-permute-start | bytes 36872 | tf_op jit(solution)/shard_map/ppermute | solution.py:756
  95.6 15.0 %collective-permute-start.9 = (f32[8,8,128]{2,1,0:T(8,128)}, f32[8,8,128]{2,1,0:T(8,128)}, u32[]{:S(2)}, u32[]{:S(2)}) collective-permute-start(f32[8,8,128]{2,1,0:T(8,128)} %get-tuple-element.72.mid), channel_id=1, source_target_pairs={{8,0},{16,8},{24,16},{32,24},{40,32},{48,40},{56,48},{64,56},{72,6... | collective-permute-start | bytes 98312 | tf_op jit(solution)/shard_map/ppermute | solution.py:751
  98.7 11.9 %collective-permute-start.8 = (f32[8,8,128]{2,1,0:T(8,128)}, f32[8,8,128]{2,1,0:T(8,128)}, u32[]{:S(2)}, u32[]{:S(2)}) collective-permute-start(f32[8,8,128]{2,1,0:T(8,128)} %get-tuple-element.72.mid), channel_id=1, source_target_pairs={{0,8},{8,16},{16,24},{24,32},{32,40},{40,48},{48,56},{56,64},{64,7... | collective-permute-start | bytes 98312 | tf_op jit(solution)/shard_map/ppermute | solution.py:751
  108.3 19.0 %copy-start.18 = (s32[5]{0:T(128)S(1)}, s32[5]{0:T(128)}, u32[]{:S(2)}) copy-start(s32[5]{0:T(128)} %copy-done.16) | copy-start | bytes 64
  110.6 37.6 %copy-start.8 = (f32[880,8,128]{2,1,0:T(8,128)S(1)}, f32[880,8,128]{2,1,0:T(8,128)}, u32[]{:S(2)}) copy-start(f32[880,8,128]{2,1,0:T(8,128)} %all-gather.17.cloned.1.call-done) | copy-start | bytes 10813444
  110.6 37.6 %copy-start.24 = (f32[24,8,128]{2,1,0:T(8,128)S(1)}, f32[24,8,128]{2,1,0:T(8,128)}, u32[]{:S(2)}) copy-start(f32[24,8,128]{2,1,0:T(8,128)} %copy-done.23) | copy-start | bytes 294916
  112.4 18.6 %collective-permute-start.10 = (f32[56,128]{1,0:T(8,128)S(1)}, f32[56,128]{1,0:T(8,128)S(1)}, u32[]{:S(2)}, u32[]{:S(2)}) collective-permute-start(f32[56,128]{1,0:T(8,128)S(1)} %get-tuple-element.76.mine), channel_id=1, source_target_pairs={{32,0},{40,8},{48,16},{56,24},{64,32},{72,40},{80,48},{88,56},{96,... | collective-permute-start | bytes 86024 | tf_op jit(solution)/shard_map/ppermute | solution.py:763
  120.0 11.0 %collective-permute-start.11 = (f32[8,128]{1,0:T(8,128)S(1)}, f32[8,128]{1,0:T(8,128)S(1)}, u32[]{:S(2)}, u32[]{:S(2)}) collective-permute-start(f32[8,128]{1,0:T(8,128)S(1)} %slice.3), channel_id=1, source_target_pairs={{64,0},{72,8},{80,16},{88,24},{96,32},{104,40},{112,48},{120,56},{... | collective-permute-start | bytes 12296 | tf_op jit(solution)/shard_map/ppermute | solution.py:763
  148.2 11.6 %copy-start.4 = (f32[576,8,128]{2,1,0:T(8,128)S(1)}, f32[576,8,128]{2,1,0:T(8,128)}, u32[]{:S(2)}) copy-start(f32[576,8,128]{2,1,0:T(8,128)} %copy-done.1) | copy-start | bytes 7077892
  148.2 11.6 %copy-start.6 = (f32[576,8,128]{2,1,0:T(8,128)S(1)}, f32[576,8,128]{2,1,0:T(8,128)}, u32[]{:S(2)}) copy-start(f32[576,8,128]{2,1,0:T(8,128)} %copy-done.5) | copy-start | bytes 7077892
  148.3 11.6 %copy-start.14 = (f32[2,24,8,128]{3,2,1,0:T(8,128)S(1)}, f32[2,24,8,128]{3,2,1,0:T(8,128)}, u32[]{:S(2)}) copy-start(f32[2,24,8,128]{3,2,1,0:T(8,128)} %copy-done.13) | copy-start | bytes 589828
  148.3 11.6 %copy-start.20 = (f32[24,8,128]{2,1,0:T(8,128)S(1)}, f32[24,8,128]{2,1,0:T(8,128)}, u32[]{:S(2)}) copy-start(f32[24,8,128]{2,1,0:T(8,128)} %copy-done.19) | copy-start | bytes 294916
  151.3 7.4 %collective-permute-start.12 = (f32[12,8,128]{2,1,0:T(8,128)S(1)}, f32[12,8,128]{2,1,0:T(8,128)S(1)}, u32[]{:S(2)}, u32[]{:S(2)}) collective-permute-start(f32[12,8,128]{2,1,0:T(8,128)S(1)} %get-tuple-element.84), channel_id=1, source_target_pairs={{0,8},{8,16},{16,24},{24,32},{32,40},{40,48},{48,56},{56,64},{64,7... | collective-permute-start | bytes 147464 | tf_op jit(solution)/shard_map/ppermute | solution.py:751
  153.6 6.3 %collective-permute-start.13 = (f32[12,8,128]{2,1,0:T(8,128)S(1)}, f32[12,8,128]{2,1,0:T(8,128)S(1)}, u32[]{:S(2)}, u32[]{:S(2)}) collective-permute-start(f32[12,8,128]{2,1,0:T(8,128)S(1)} %get-tuple-element.86), channel_id=1, source_target_pairs={{8,0},{16,8},{24,16},{32,24},{40,32},{48,40},{56,48},{64,56},{72,6... | collective-permute-start | bytes 147464 | tf_op jit(solution)/shard_map/ppermute | solution.py:751
  161.4 7.1 %collective-permute-start.14 = (f32[2,24,128]{2,1,0:T(8,128)S(1)}, f32[2,24,128]{2,1,0:T(8,128)S(1)}, u32[]{:S(2)}, u32[]{:S(2)}) collective-permute-start(f32[2,24,128]{2,1,0:T(8,128)S(1)} %get-tuple-element.91), channel_id=1, source_target_pairs={{0,8},{8,16},{16,24},{24,32},{32,40},{40,48},{48,56},{56,64},{64,7... | collective-permute-start | bytes 73736 | tf_op jit(solution)/shard_map/ppermute | solution.py:756
  167.2 4.6 %collective-permute-start.15 = (f32[2,24,128]{2,1,0:T(8,128)S(1)}, f32[2,24,128]{2,1,0:T(8,128)S(1)}, u32[]{:S(2)}, u32[]{:S(2)}) collective-permute-start(f32[2,24,128]{2,1,0:T(8,128)S(1)} %get-tuple-element.92), channel_id=1, source_target_pairs={{0,2},{2,4},{4,6},{3,1},{5,3},{7,5},{8,10},{10,12},{12,14},{11,9},... | collective-permute-start | bytes 73736 | tf_op jit(solution)/shard_map/ppermute | solution.py:756
  174.8 4.6 %collective-permute-start.16 = (f32[2,24,128]{2,1,0:T(8,128)S(1)}, f32[2,24,128]{2,1,0:T(8,128)S(1)}, u32[]{:S(2)}, u32[]{:S(2)}) collective-permute-start(f32[2,24,128]{2,1,0:T(8,128)S(1)} %get-tuple-element.95), channel_id=1, source_target_pairs={{0,8},{8,16},{16,24},{24,32},{32,40},{40,48},{48,56},{56,64},{64,7... | collective-permute-start | bytes 73736 | tf_op jit(solution)/shard_map/ppermute | solution.py:756
  177.4 5.0 %collective-permute-start.17 = (f32[2,24,128]{2,1,0:T(8,128)S(1)}, f32[2,24,128]{2,1,0:T(8,128)S(1)}, u32[]{:S(2)}, u32[]{:S(2)}) collective-permute-start(f32[2,24,128]{2,1,0:T(8,128)S(1)} %get-tuple-element.96), channel_id=1, source_target_pairs={{0,2},{2,4},{4,6},{3,1},{5,3},{7,5},{8,10},{10,12},{12,14},{11,9},... | collective-permute-start | bytes 73736 | tf_op jit(solution)/shard_map/ppermute | solution.py:756
  186.2 4.6 %collective-permute-start.18 = (f32[2,24,128]{2,1,0:T(8,128)S(1)}, f32[2,24,128]{2,1,0:T(8,128)S(1)}, u32[]{:S(2)}, u32[]{:S(2)}) collective-permute-start(f32[2,24,128]{2,1,0:T(8,128)S(1)} %get-tuple-element.100), channel_id=1, source_target_pairs={{0,8},{8,16},{16,24},{24,32},{32,40},{40,48},{48,56},{56,64},{64,7... | collective-permute-start | bytes 73736 | tf_op jit(solution)/shard_map/ppermute | solution.py:756
  189.5 5.1 %collective-permute-start.19 = (f32[2,24,128]{2,1,0:T(8,128)S(1)}, f32[2,24,128]{2,1,0:T(8,128)S(1)}, u32[]{:S(2)}, u32[]{:S(2)}) collective-permute-start(f32[2,24,128]{2,1,0:T(8,128)S(1)} %get-tuple-element.101), channel_id=1, source_target_pairs={{0,2},{2,4},{4,6},{3,1},{5,3},{7,5},{8,10},{10,12},{12,14},{11,9},... | collective-permute-start | bytes 73736 | tf_op jit(solution)/shard_map/ppermute | solution.py:756
  (19 other events, 40.3 us)
Sparse Core Ops, SparseCore 0:
  37.0 35.1 all-gather.16
  74.4 31.9 all-gather.18
